TPU v7x, 512 devices: a whole 4x4x16 slice. The times are simulated.
512 devices in a mesh: dp: 16 (over x_hi, y, core), space: 32 (over z, x_lo).
Axes of the slice: x: 4 (x_hi: 2, x_lo: 2; x = x_hi * 2 + x_lo), y: 4, z: 16, core: 2. Of those that a mesh axis runs over, the one named last changes fastest.
Arguments:
- fields: bfloat16 [16, 32, 48, 48, 128], P('dp', 'space'), may hold values from -6 to 6
- cotangent: bfloat16 [16, 32, 48, 48, 128], P('dp', 'space'), may hold values from -6 to 6
- land_mask: int32 [32, 48, 48], P('space'), may hold values from 0 to 1, as said below
- neighbours: int32 [32, 8], P('space'), may hold values from -1 to 31, as said below
- conv_kernel: float32 [7, 7, 128], replicated, may hold values from -0.875 to 0.875
- norm_gain: float32 [128], replicated, may hold values from 0.25 to 1.75
- up_weight: bfloat16 [128, 512], replicated, may hold values from -0.5 to 0.5
- up_bias: float32 [512], replicated, may hold values from -3 to 3
- down_weight: bfloat16 [512, 128], replicated, may hold values from -0.25 to 0.25
- layer_scale: float32 [128], replicated, may hold values from 0.3 to 1.5
Outputs:
- block_out: bfloat16 [16, 32, 48, 48, 128], P('dp', 'space')
- fields_grad: bfloat16 [16, 32, 48, 48, 128], P('dp', 'space')
- kernel_grad: float32 [7, 7, 128], replicated
- gain_grad: float32 [128], replicated
- up_weight_grad: float32 [128, 512], replicated
- up_bias_grad: float32 [512], replicated
- down_weight_grad: float32 [512, 128], replicated
- scale_grad: float32 [128], replicated
Inputs may be any that keep to these rules, and one draw needn't show every extreme that they name: `neighbours`: row t gives the ids of the tiles beside tile t in the order north, south, west, east, north-west, north-east, south-west, south-east, or -1. The curve runs over 32 + 8 tile positions in rows of two, alternately west to east and east to west, from the northern row southwards; 8 positions are land and skipped, and the 32 wet tiles are numbered along it, one in every slot. The relation is symmetric; a west or east neighbour differs from t by exactly 1, a northern one is lower and a southern one higher, and the difference reaches 3 and never more. `land_mask`: 1 for a sea cell, 0 for land; every tile has sea cells.
All inputs are finite; a program needn't handle non-finite values.
Results may differ from a plain program's by a relative error of at most 0.007.
Values may be sent and summed in bfloat16 or wider, within the bound.
No kernel may reach another device: no remote copies, remote signals or barrier semaphores. Data moves between devices by JAX's collectives and lax.ppermute only.
A program may use at most 64 MiB of HBM per device.

v0:
```python
import math

import jax
import jax.numpy as jnp
from jax import lax
from jax.sharding import PartitionSpec as P

KERNEL = 7
DILATION = 2
REACH = 3
HALO = 6


norm_eps = 1e-06
inv_sqrt_two = 0.7071067811865476
inv_sqrt_two_pi = 0.3989422804014327


def shifted(value, axis, steps):
    count = lax.axis_size(axis)
    leading, last = (max(0, -steps), min(count, count - steps))
    return lax.ppermute(value, axis, [(source, source + steps) for source in range(leading, last)])


def gather_rims(centre):
    top_rows = centre[:, :HALO]
    bottom_rows = centre[:, -HALO:]
    left_columns = centre[:, :, :HALO]
    right_columns = centre[:, :, -HALO:]
    zero_rows = jnp.zeros_like(top_rows)
    zero_columns = jnp.zeros_like(left_columns)
    north_pool = []
    south_pool = []
    west_pool = []
    east_pool = []
    for offset in range(-REACH, REACH + 1):
        if offset == 0:
            north_pool.append(zero_rows)
            south_pool.append(zero_rows)
            west_pool.append(zero_columns)
            east_pool.append(zero_columns)
        else:
            received = shifted(
                (top_rows, bottom_rows, left_columns, right_columns), "space", -offset
            )
            south_pool.append(received[0])
            north_pool.append(received[1])
            east_pool.append(received[2])
            west_pool.append(received[3])
    return (
        jnp.stack(north_pool),
        jnp.stack(south_pool),
        jnp.stack(west_pool),
        jnp.stack(east_pool),
    )


def choose_strip(stacked, beside_ids, position, direction):
    source = beside_ids[direction]
    slot_index = jnp.clip(source - position + REACH, 0, 2 * REACH)
    strip = lax.dynamic_index_in_dim(stacked, slot_index, 0, keepdims=False)
    return jnp.where(source >= 0, strip, jnp.zeros_like(strip))


def extend_tiles(centre, beside_ids, position):
    north_pool, south_pool, west_pool, east_pool = gather_rims(centre)
    north = choose_strip(north_pool, beside_ids, position, 0)
    south = choose_strip(south_pool, beside_ids, position, 1)
    west = choose_strip(west_pool, beside_ids, position, 2)
    east = choose_strip(east_pool, beside_ids, position, 3)
    north_west = choose_strip(north_pool, beside_ids, position, 4)[:, :, -HALO:]
    north_east = choose_strip(north_pool, beside_ids, position, 5)[:, :, :HALO]
    south_west = choose_strip(south_pool, beside_ids, position, 6)[:, :, -HALO:]
    south_east = choose_strip(south_pool, beside_ids, position, 7)[:, :, :HALO]
    upper = jnp.concatenate([north_west, north, north_east], axis=2)
    middle = jnp.concatenate([west, centre, east], axis=2)
    lower = jnp.concatenate([south_west, south, south_east], axis=2)
    return jnp.concatenate([upper, middle, lower], axis=1)


def depthwise(extended, conv_kernel):
    tile_rows = extended.shape[-3] - 2 * HALO
    tile_cols = extended.shape[-2] - 2 * HALO
    running = jnp.zeros(
        extended.shape[:-3] + (tile_rows, tile_cols, extended.shape[-1]), jnp.float32
    )
    for tap_row in range(KERNEL):
        for tap_col in range(KERNEL):
            window = extended[
                ...,
                DILATION * tap_row : DILATION * tap_row + tile_rows,
                DILATION * tap_col : DILATION * tap_col + tile_cols,
                :,
            ]
            running = running + conv_kernel[tap_row, tap_col] * window.astype(jnp.float32)
    return running


def depthwise_transpose(grad_extended, conv_kernel):
    tile_rows = grad_extended.shape[-3] - 2 * HALO
    tile_cols = grad_extended.shape[-2] - 2 * HALO
    running = jnp.zeros(
        grad_extended.shape[:-3] + (tile_rows, tile_cols, grad_extended.shape[-1]), jnp.float32
    )
    for tap_row in range(KERNEL):
        for tap_col in range(KERNEL):
            row_start = 2 * HALO - DILATION * tap_row
            col_start = 2 * HALO - DILATION * tap_col
            window = grad_extended[
                ..., row_start : row_start + tile_rows, col_start : col_start + tile_cols, :
            ]
            running = running + conv_kernel[tap_row, tap_col] * window.astype(jnp.float32)
    return running


def kernel_sums(conv_grad, extended):
    tile_rows = conv_grad.shape[-3]
    tile_cols = conv_grad.shape[-2]
    upstream = conv_grad.astype(jnp.float32)
    lead_axes = tuple(range(conv_grad.ndim - 1))
    rows_out = []
    for tap_row in range(KERNEL):
        row_terms = []
        for tap_col in range(KERNEL):
            window = extended[
                ...,
                DILATION * tap_row : DILATION * tap_row + tile_rows,
                DILATION * tap_col : DILATION * tap_col + tile_cols,
                :,
            ]
            row_terms.append(jnp.sum(upstream * window.astype(jnp.float32), axis=lead_axes))
        rows_out.append(jnp.stack(row_terms))
    return jnp.stack(rows_out)


def block_pass(
    fields,
    cotangent,
    maskf,
    extended,
    extend_fn,
    conv_kernel,
    norm_gain,
    up_weight,
    up_bias,
    down_weight,
    layer_scale,
):
    channels = fields.shape[-1]
    lead_axes = tuple(range(fields.ndim - 1))
    conv = depthwise(extended, conv_kernel)
    chan_mean = jnp.mean(conv, axis=-1, keepdims=True)
    centered = conv - chan_mean
    inv_std = lax.rsqrt(jnp.mean(centered * centered, axis=-1, keepdims=True) + norm_eps)
    standard = centered * inv_std
    normed = (standard * norm_gain).astype(jnp.bfloat16).reshape(-1, channels)
    hidden = jnp.dot(normed, up_weight, preferred_element_type=jnp.float32) + up_bias
    active = jax.nn.gelu(hidden, approximate=False).astype(jnp.bfloat16)
    branch = jnp.dot(active, down_weight, preferred_element_type=jnp.float32).reshape(fields.shape)
    block_out = (fields.astype(jnp.float32) + maskf * layer_scale * branch).astype(jnp.bfloat16)
    upstream = cotangent.astype(jnp.float32)
    scale_term = jnp.sum(maskf * branch * upstream, axis=lead_axes)
    branch_grad = (maskf * layer_scale * upstream).astype(jnp.bfloat16).reshape(-1, channels)
    down_term = lax.dot_general(
        active, branch_grad, (((0,), (0,)), ((), ())), preferred_element_type=jnp.float32
    )
    active_grad = lax.dot_general(
        branch_grad, down_weight, (((1,), (1,)), ((), ())), preferred_element_type=jnp.float32
    )
    gelu_slope = (
        0.5 * (1.0 + lax.erf(hidden * inv_sqrt_two))
        + hidden * jnp.exp(-0.5 * hidden * hidden) * inv_sqrt_two_pi
    )
    hidden_grad = (active_grad * gelu_slope).astype(jnp.bfloat16)
    up_term = lax.dot_general(
        normed, hidden_grad, (((0,), (0,)), ((), ())), preferred_element_type=jnp.float32
    )
    bias_term = jnp.sum(hidden_grad.astype(jnp.float32), axis=0)
    normed_grad = lax.dot_general(
        hidden_grad, up_weight, (((1,), (1,)), ((), ())), preferred_element_type=jnp.float32
    ).reshape(conv.shape)
    gain_term = jnp.sum(normed_grad * standard, axis=lead_axes)
    scaled_grad = normed_grad * norm_gain
    conv_grad = (
        inv_std
        * (
            scaled_grad
            - jnp.mean(scaled_grad, axis=-1, keepdims=True)
            - standard * jnp.mean(scaled_grad * standard, axis=-1, keepdims=True)
        )
    ).astype(jnp.bfloat16)
    kernel_term = kernel_sums(conv_grad, extended)
    grad_extended = extend_fn(conv_grad)
    input_grad = depthwise_transpose(grad_extended, conv_kernel)
    fields_grad = (upstream + maskf * input_grad).astype(jnp.bfloat16)
    return (
        block_out,
        fields_grad,
        (kernel_term, gain_term, up_term, bias_term, down_term, scale_term),
    )


def local(
    fields,
    cotangent,
    land_mask,
    neighbours,
    conv_kernel,
    norm_gain,
    up_weight,
    up_bias,
    down_weight,
    layer_scale,
):
    position = lax.axis_index("space")
    beside_ids = neighbours[0]
    maskf = land_mask.astype(jnp.float32)[..., None]
    centre = fields[:, 0]
    masked = centre * land_mask.astype(jnp.bfloat16)[..., None]

    def extend_here(tile_data):
        return extend_tiles(tile_data, beside_ids, position)

    block_out, fields_grad, partials = block_pass(
        centre,
        cotangent[:, 0],
        maskf,
        extend_here(masked),
        extend_here,
        conv_kernel,
        norm_gain,
        up_weight,
        up_bias,
        down_weight,
        layer_scale,
    )
    totals = lax.psum(
        (partials[0], partials[1], partials[2], partials[3], partials[4], partials[5]),
        ("dp", "space"),
    )
    cell_count = (
        fields.shape[0]
        * lax.axis_size("dp")
        * lax.axis_size("space")
        * fields.shape[2]
        * fields.shape[3]
    )
    factor = 1.0 / math.sqrt(cell_count)
    return (
        block_out[:, None],
        fields_grad[:, None],
        totals[0] * factor,
        totals[1] * factor,
        totals[2] * factor,
        totals[3] * factor,
        totals[4] * factor,
        totals[5] * factor,
    )


def solution(mesh):
    return jax.shard_map(
        local,
        mesh=mesh,
        in_specs=(
            P("dp", "space", None, None, None),
            P("dp", "space", None, None, None),
            P("space", None, None),
            P("space", None),
            P(),
            P(),
            P(),
            P(),
            P(),
            P(),
        ),
        out_specs=(
            P("dp", "space", None, None, None),
            P("dp", "space", None, None, None),
            P(),
            P(),
            P(),
            P(),
            P(),
            P(),
        ),
        check_vma=False,
    )
```

profile of v0, /device:TPU:1, one launch (start us, length us, event | category | flops | bytes accessed | tf_op | source)
XLA Modules:
  0.0 784.2 jit_solution(1415207172804839855)
XLA Ops:
  8.1 1.4 bitcast_multiply_fusion.2
  9.5 5.3 collective-permute-start
  14.8 3.5 collective-permute-start.1
  18.4 3.5 collective-permute-start.2
  23.3 6.6 collective-permute-start.6
  41.8 5.4 collective-permute-start.12
  47.2 1.6 collective-permute-done.12
  48.8 4.7 collective-permute-start.7
  53.5 1.6 collective-permute-done.7
  55.1 2.1 collective-permute-start.8
  57.2 1.6 collective-permute-done.8
  60.2 5.4 collective-permute-done.9
  66.9 6.4 collective-permute-start.18
  73.3 1.4 collective-permute-done.18
  76.0 5.0 collective-permute-start.19
  82.4 7.8 collective-permute-done.10
  90.2 3.6 collective-permute-start.20
  99.1 6.4 collective-permute-start.13
  105.6 2.9 collective-permute-done.11
  108.5 5.1 collective-permute-start.14
  119.0 3.1 collective-permute-done.16
  122.2 3.1 collective-permute-done.17
  126.1 11.8 %fusion.150 = (f32[48,48]{1,0:T(8,128)S(1)}, f32[1,48,48,128]{3,2,1,0:T(8,128)S(1)}) fusion(bf16[1,54,60,128]{3,2,1,0:T(8,128)(2,1)S(1)} %get-tuple-element.81, f32[128]{0:T(128)S(1)} %copy-done.40, f32[128]{0:T(128)S(1)} %copy-done.42, f32[128]{0:T(128)S(1)} %get-tuple-element.105, f32[128]{0:T(128)S(1)} %get-tuple-element.106, ...), kind=kLoop, calls=%fused_computation.438 | loop fusion | flops 48658176 | bytes 26723840 | tf_op jit(solution)/shard_map/reduce_sum | solution.py:152
  139.5 10.9 %fusion.2 = (bf16[2304,512]{1,0:T(8,128)(2,1)S(1)}, f32[2304,512]{1,0:T(8,128)S(1)}) fusion(f32[512]{0:T(512)S(1)} %copy-done.64, bf16[2304,128]{1,0:T(8,128)(2,1)S(1)} %bitcast.338, bf16[128,512]{1,0:T(8,128)(2,1)S(1)} %copy-done), kind=kOutput, calls=%fused_computation.56 | convolution fusion | flops 379846656 | bytes 7800832 | tf_op jit(solution)/shard_map/dot_general | solution.py:157
  150.4 2.3 fusion.140
  152.7 1.5 fusion.159
  154.2 3.9 convert_reduce_fusion
  158.1 2.9 fusion.158
  161.0 2.5 multiply_reduce_fusion.2
  164.6 1.6 multiply_reduce_fusion
  166.3 5.9 fusion.136
  172.2 2.1 fusion.135
  174.3 3.0 fusion.108
  178.1 5.8 collective-permute-start.42
  183.9 5.0 collective-permute-start.43
  188.9 2.6 collective-permute-start.44
  193.2 122.4 %all-reduce = (f32[7,7,128]{2,1,0:T(8,128)S(1)}, f32[128]{0:T(128)S(1)}, f32[512]{0:T(512)S(1)}, f32[128]{0:T(128)S(1)}) all-reduce(f32[7,7,128]{2,1,0:T(8,128)S(1)} %constant_dynamic-update-slice_fusion.56, f32[128]{0:T(128)S(1)} %copy-done.45, f32[512]{0:T(512)S(1)} %copy-done.61, ...), channel_id=1, replica_groups=mesh['dp'=16,'space'=32] {'dp','space'}, use_global_device_ids=true, to_apply=%region_53.54 | all-reduce | flops 7040 | bytes 56320 | tf_op jit(solution)/shard_map/psum | solution.py:237
  316.9 2.9 collective-permute-start.24
  321.5 7.7 collective-permute-start.30
  329.3 1.6 collective-permute-done.30
  332.2 1.6 collective-permute-done.25
  333.8 6.8 collective-permute-start.26
  340.6 1.6 collective-permute-done.26
  343.5 4.8 collective-permute-done.27
  349.6 4.9 collective-permute-done.28
  355.9 7.5 collective-permute-done.29
  363.4 5.2 collective-permute-start.31
  368.6 1.6 collective-permute-done.31
  370.2 3.8 collective-permute-start.32
  374.0 1.6 collective-permute-done.32
  377.0 5.2 collective-permute-done.33
  383.5 5.4 collective-permute-done.34
  390.2 8.6 %collective-permute-start.36 = (bf16[1,6,48,128]{3,2,1,0:T(8,128)(2,1)S(1)}, bf16[1,6,48,128]{3,2,1,0:T(8,128)(2,1)S(1)}, u32[]{:S(2)}, u32[]{:S(2)}) collective-permute-start(bf16[1,6,48,128]{3,2,1,0:T(8,128)(2,1)S(1)} %get-tuple-element.84), channel_id=1, source_target_pairs={{0,3},{1,4},{2,5},{3,6},{4,7},{5,8},{6,9},{7,10},{8,11},{9,12},{10... | collective-permute-start | bytes 221192 | tf_op jit(solution)/shard_map/ppermute | solution.py:22
  398.9 1.4 collective-permute-done.36
  402.9 5.4 collective-permute-start.37
  409.5 5.9 collective-permute-start.38
  418.2 1.4 collective-permute-start.41
  419.8 2.0 collective-permute-done.39
  421.9 4.0 collective-permute-done.40
  426.0 2.6 collective-permute-done.41
  429.8 10.5 %fusion.149 = bf16[1,1,48,48,128]{4,3,2,1,0:T(8,128)(2,1)} fusion(bf16[1,54,60,128]{3,2,1,0:T(8,128)(2,1)S(1)} %get-tuple-element.79, f32[128]{0:T(128)S(1)} %copy-done.41, f32[128]{0:T(128)S(1)} %copy-done.43, f32[128]{0:T(128)S(1)} %get-tuple-element.105, f32[128]{0:T(128)S(1)} %get-tuple-element.106, f32[128]{0:T(128)S(1)} %get-tuple-element.107, ...), kind=kLoop, calls=%fused_computation.297 | loop fusion | flops 49545216 | bytes 26723840 | tf_op jit(solution)/shard_map/broadcast_in_dim | solution.py:251
  440.3 333.7 %all-reduce.4.cloned.1.call-done = (f32[128,512]{1,0:T(8,128)}, f32[512,128]{1,0:T(8,128)}) async-done(((f32[128,512]{1,0:T(8,128)}, f32[512,128]{1,0:T(8,128)}), (f32[128,512]{1,0:T(8,128)}, f32[512,128]{1,0:T(8,128)})) %all-reduce.4.cloned.1.call-update) | async-done | bytes 524304 | tf_op jit(solution)/shard_map/psum | solution.py:237
  774.0 1.7 broadcast_multiply_fusion
  775.7 1.7 broadcast_multiply_fusion.1
  (291 shorter events, 44.7 us)
Async XLA Ops:
  7.2 132.3 %copy-start = (bf16[128,512]{1,0:T(8,128)(2,1)S(1)}, bf16[128,512]{1,0:T(8,128)(2,1)}, u32[]{:S(2)}) copy-start(bf16[128,512]{1,0:T(8,128)(2,1)} %param.16) | copy-start | bytes 393220
  7.2 766.8 %all-reduce.4.cloned.1.call-start = ((), (), s32[]{:S(2)}) async-start(), calls=%async_computation | async-start | bytes 1048576 | tf_op jit(solution)/shard_map/psum | solution.py:237
  9.5 115.8 %copy-start.3 = (bf16[1,48,48,128]{3,2,1,0:T(8,128)(2,1)}, bf16[1,48,48,128]{3,2,1,0:T(8,128)(2,1)S(1)}, u32[]{:S(2)}) copy-start(bf16[1,48,48,128]{3,2,1,0:T(8,128)(2,1)S(1)} %bitcast_multiply_fusion.2) | copy-start | bytes 1769476
  9.5 57.3 %collective-permute-start = (bf16[1,6,48,128]{3,2,1,0:T(8,128)(2,1)S(1)}, bf16[1,6,48,128]{3,2,1,0:T(8,128)(2,1)S(1)}, u32[]{:S(2)}, u32[]{:S(2)}) collective-permute-start(bf16[1,6,48,128]{3,2,1,0:T(8,128)(2,1)S(1)} %get-tuple-element.88), channel_id=1, source_target_pairs={{0,3},{1,4},{2,5},{3,6},{4,7},{5,8},{6,9},{7,10},{8,11},{9,12},{10... | collective-permute-start | bytes 221192 | tf_op jit(solution)/shard_map/ppermute | solution.py:22
  14.8 61.2 %collective-permute-start.1 = (bf16[1,6,48,128]{3,2,1,0:T(8,128)(2,1)S(1)}, bf16[1,6,48,128]{3,2,1,0:T(8,128)(2,1)S(1)}, u32[]{:S(2)}, u32[]{:S(2)}) collective-permute-start(bf16[1,6,48,128]{3,2,1,0:T(8,128)(2,1)S(1)} %get-tuple-element.88), channel_id=1, source_target_pairs={{0,2},{1,3},{2,4},{3,5},{4,6},{5,7},{6,8},{7,9},{8,10},{9,11},{10,... | collective-permute-start | bytes 221192 | tf_op jit(solution)/shard_map/ppermute | solution.py:22
  18.4 62.7 %collective-permute-start.2 = (bf16[1,6,48,128]{3,2,1,0:T(8,128)(2,1)S(1)}, bf16[1,6,48,128]{3,2,1,0:T(8,128)(2,1)S(1)}, u32[]{:S(2)}, u32[]{:S(2)}) collective-permute-start(bf16[1,6,48,128]{3,2,1,0:T(8,128)(2,1)S(1)} %get-tuple-element.88), channel_id=1, source_target_pairs={{0,1},{1,2},{2,3},{3,4},{4,5},{5,6},{6,7},{7,8},{8,9},{9,10},{10,1... | collective-permute-start | bytes 221192 | tf_op jit(solution)/shard_map/ppermute | solution.py:22
  21.9 71.9 %collective-permute-start.3 = (bf16[1,6,48,128]{3,2,1,0:T(8,128)(2,1)S(1)}, bf16[1,6,48,128]{3,2,1,0:T(8,128)(2,1)S(1)}, u32[]{:S(2)}, u32[]{:S(2)}) collective-permute-start(bf16[1,6,48,128]{3,2,1,0:T(8,128)(2,1)S(1)} %get-tuple-element.88), channel_id=1, source_target_pairs={{1,0},{2,1},{3,2},{4,3},{5,4},{6,5},{7,6},{8,7},{9,8},{10,9},{11,1... | collective-permute-start | bytes 221192 | tf_op jit(solution)/shard_map/ppermute | solution.py:22
  23.3 18.5 %collective-permute-start.6 = (bf16[1,48,6,128]{3,2,1,0:T(8,128)(2,1)S(1)}, bf16[1,48,6,128]{3,2,1,0:T(8,128)(2,1)S(1)}, u32[]{:S(2)}, u32[]{:S(2)}) collective-permute-start(bf16[1,48,6,128]{3,2,1,0:T(8,128)(2,1)S(1)} %get-tuple-element.90), channel_id=1, source_target_pairs={{0,3},{1,4},{2,5},{3,6},{4,7},{5,8},{6,9},{7,10},{8,11},{9,12},{10... | collective-permute-start | bytes 221192 | tf_op jit(solution)/shard_map/ppermute | solution.py:22
  29.9 96.0 %copy-start.14 = (f32[128]{0:T(128)}, f32[128]{0:T(128)S(1)}, u32[]{:S(2)}) copy-start(f32[128]{0:T(128)S(1)} %get-tuple-element.138) | copy-start | bytes 1540
  29.9 96.0 %copy-start.16 = (f32[128]{0:T(128)}, f32[128]{0:T(128)S(1)}, u32[]{:S(2)}) copy-start(f32[128]{0:T(128)S(1)} %get-tuple-element.139) | copy-start | bytes 1540
  29.9 96.0 %copy-start.18 = (f32[128]{0:T(128)}, f32[128]{0:T(128)S(1)}, u32[]{:S(2)}) copy-start(f32[128]{0:T(128)S(1)} %get-tuple-element.140) | copy-start | bytes 1540
  29.9 96.0 %copy-start.20 = (f32[128]{0:T(128)}, f32[128]{0:T(128)S(1)}, u32[]{:S(2)}) copy-start(f32[128]{0:T(128)S(1)} %get-tuple-element.141) | copy-start | bytes 1540
  30.5 95.5 %copy-start.28 = (f32[128]{0:T(128)}, f32[128]{0:T(128)S(1)}, u32[]{:S(2)}) copy-start(f32[128]{0:T(128)S(1)} %get-tuple-element.145) | copy-start | bytes 1540
  30.5 95.5 %copy-start.30 = (f32[128]{0:T(128)}, f32[128]{0:T(128)S(1)}, u32[]{:S(2)}) copy-start(f32[128]{0:T(128)S(1)} %get-tuple-element.146) | copy-start | bytes 1540
  30.5 95.5 %copy-start.32 = (f32[128]{0:T(128)}, f32[128]{0:T(128)S(1)}, u32[]{:S(2)}) copy-start(f32[128]{0:T(128)S(1)} %get-tuple-element.147) | copy-start | bytes 1540
  30.5 95.5 %copy-start.34 = (f32[128]{0:T(128)}, f32[128]{0:T(128)S(1)}, u32[]{:S(2)}) copy-start(f32[128]{0:T(128)S(1)} %get-tuple-element.148) | copy-start | bytes 1540
  30.5 95.5 %copy-start.36 = (f32[128]{0:T(128)}, f32[128]{0:T(128)S(1)}, u32[]{:S(2)}) copy-start(f32[128]{0:T(128)S(1)} %get-tuple-element.149) | copy-start | bytes 1540
  30.5 95.5 %copy-start.38 = (f32[128]{0:T(128)}, f32[128]{0:T(128)S(1)}, u32[]{:S(2)}) copy-start(f32[128]{0:T(128)S(1)} %get-tuple-element.150) | copy-start | bytes 1540
  41.8 7.0 collective-permute-start.12
  48.8 6.4 collective-permute-start.7
  55.1 3.7 collective-permute-start.8
  58.8 6.7 collective-permute-start.9
  65.6 29.6 %collective-permute-start.4 = (bf16[1,6,48,128]{3,2,1,0:T(8,128)(2,1)S(1)}, bf16[1,6,48,128]{3,2,1,0:T(8,128)(2,1)S(1)}, u32[]{:S(2)}, u32[]{:S(2)}) collective-permute-start(bf16[1,6,48,128]{3,2,1,0:T(8,128)(2,1)S(1)} %get-tuple-element.88), channel_id=1, source_target_pairs={{2,0},{3,1},{4,2},{5,3},{6,4},{7,5},{8,6},{9,7},{10,8},{11,9},{12,... | collective-permute-start | bytes 221192 | tf_op jit(solution)/shard_map/ppermute | solution.py:22
  66.9 7.8 collective-permute-start.18
  74.7 21.8 %collective-permute-start.5 = (bf16[1,6,48,128]{3,2,1,0:T(8,128)(2,1)S(1)}, bf16[1,6,48,128]{3,2,1,0:T(8,128)(2,1)S(1)}, u32[]{:S(2)}, u32[]{:S(2)}) collective-permute-start(bf16[1,6,48,128]{3,2,1,0:T(8,128)(2,1)S(1)} %get-tuple-element.88), channel_id=1, source_target_pairs={{3,0},{4,1},{5,2},{6,3},{7,4},{8,5},{9,6},{10,7},{11,8},{12,9},{13... | collective-permute-start | bytes 221192 | tf_op jit(solution)/shard_map/ppermute | solution.py:22
  76.0 21.8 %collective-permute-start.19 = (bf16[1,6,48,128]{3,2,1,0:T(8,128)(2,1)S(1)}, bf16[1,6,48,128]{3,2,1,0:T(8,128)(2,1)S(1)}, u32[]{:S(2)}, u32[]{:S(2)}) collective-permute-start(bf16[1,6,48,128]{3,2,1,0:T(8,128)(2,1)S(1)} %get-tuple-element.89), channel_id=1, source_target_pairs={{0,2},{1,3},{2,4},{3,5},{4,6},{5,7},{6,8},{7,9},{8,10},{9,11},{10,... | collective-permute-start | bytes 221192 | tf_op jit(solution)/shard_map/ppermute | solution.py:22
  81.1 9.1 %collective-permute-start.10 = (bf16[1,48,6,128]{3,2,1,0:T(8,128)(2,1)S(1)}, bf16[1,48,6,128]{3,2,1,0:T(8,128)(2,1)S(1)}, u32[]{:S(2)}, u32[]{:S(2)}) collective-permute-start(bf16[1,48,6,128]{3,2,1,0:T(8,128)(2,1)S(1)} %get-tuple-element.90), channel_id=1, source_target_pairs={{2,0},{3,1},{4,2},{5,3},{6,4},{7,5},{8,6},{9,7},{10,8},{11,9},{12,... | collective-permute-start | bytes 221192 | tf_op jit(solution)/shard_map/ppermute | solution.py:22
  90.2 9.0 %collective-permute-start.20 = (bf16[1,6,48,128]{3,2,1,0:T(8,128)(2,1)S(1)}, bf16[1,6,48,128]{3,2,1,0:T(8,128)(2,1)S(1)}, u32[]{:S(2)}, u32[]{:S(2)}) collective-permute-start(bf16[1,6,48,128]{3,2,1,0:T(8,128)(2,1)S(1)} %get-tuple-element.89), channel_id=1, source_target_pairs={{0,1},{1,2},{2,3},{3,4},{4,5},{5,6},{6,7},{7,8},{8,9},{9,10},{10,1... | collective-permute-start | bytes 221192 | tf_op jit(solution)/shard_map/ppermute | solution.py:22
  93.8 19.8 %collective-permute-start.21 = (bf16[1,6,48,128]{3,2,1,0:T(8,128)(2,1)S(1)}, bf16[1,6,48,128]{3,2,1,0:T(8,128)(2,1)S(1)}, u32[]{:S(2)}, u32[]{:S(2)}) collective-permute-start(bf16[1,6,48,128]{3,2,1,0:T(8,128)(2,1)S(1)} %get-tuple-element.89), channel_id=1, source_target_pairs={{1,0},{2,1},{3,2},{4,3},{5,4},{6,5},{7,6},{8,7},{9,8},{10,9},{11,1... | collective-permute-start | bytes 221192 | tf_op jit(solution)/shard_map/ppermute | solution.py:22
  95.2 19.8 %collective-permute-start.22 = (bf16[1,6,48,128]{3,2,1,0:T(8,128)(2,1)S(1)}, bf16[1,6,48,128]{3,2,1,0:T(8,128)(2,1)S(1)}, u32[]{:S(2)}, u32[]{:S(2)}) collective-permute-start(bf16[1,6,48,128]{3,2,1,0:T(8,128)(2,1)S(1)} %get-tuple-element.89), channel_id=1, source_target_pairs={{2,0},{3,1},{4,2},{5,3},{6,4},{7,5},{8,6},{9,7},{10,8},{11,9},{12,... | collective-permute-start | bytes 221192 | tf_op jit(solution)/shard_map/ppermute | solution.py:22
  96.5 19.8 %collective-permute-start.23 = (bf16[1,6,48,128]{3,2,1,0:T(8,128)(2,1)S(1)}, bf16[1,6,48,128]{3,2,1,0:T(8,128)(2,1)S(1)}, u32[]{:S(2)}, u32[]{:S(2)}) collective-permute-start(bf16[1,6,48,128]{3,2,1,0:T(8,128)(2,1)S(1)} %get-tuple-element.89), channel_id=1, source_target_pairs={{3,0},{4,1},{5,2},{6,3},{7,4},{8,5},{9,6},{10,7},{11,8},{12,9},{13... | collective-permute-start | bytes 221192 | tf_op jit(solution)/shard_map/ppermute | solution.py:22
  97.8 10.7 %collective-permute-start.11 = (bf16[1,48,6,128]{3,2,1,0:T(8,128)(2,1)S(1)}, bf16[1,48,6,128]{3,2,1,0:T(8,128)(2,1)S(1)}, u32[]{:S(2)}, u32[]{:S(2)}) collective-permute-start(bf16[1,48,6,128]{3,2,1,0:T(8,128)(2,1)S(1)} %get-tuple-element.90), channel_id=1, source_target_pairs={{3,0},{4,1},{5,2},{6,3},{7,4},{8,5},{9,6},{10,7},{11,8},{12,9},{13... | collective-permute-start | bytes 221192 | tf_op jit(solution)/shard_map/ppermute | solution.py:22
  99.1 18.4 %collective-permute-start.13 = (bf16[1,48,6,128]{3,2,1,0:T(8,128)(2,1)S(1)}, bf16[1,48,6,128]{3,2,1,0:T(8,128)(2,1)S(1)}, u32[]{:S(2)}, u32[]{:S(2)}) collective-permute-start(bf16[1,48,6,128]{3,2,1,0:T(8,128)(2,1)S(1)} %get-tuple-element.91), channel_id=1, source_target_pairs={{0,2},{1,3},{2,4},{3,5},{4,6},{5,7},{6,8},{7,9},{8,10},{9,11},{10,... | collective-permute-start | bytes 221192 | tf_op jit(solution)/shard_map/ppermute | solution.py:22
  108.5 9.2 %collective-permute-start.14 = (bf16[1,48,6,128]{3,2,1,0:T(8,128)(2,1)S(1)}, bf16[1,48,6,128]{3,2,1,0:T(8,128)(2,1)S(1)}, u32[]{:S(2)}, u32[]{:S(2)}) collective-permute-start(bf16[1,48,6,128]{3,2,1,0:T(8,128)(2,1)S(1)} %get-tuple-element.91), channel_id=1, source_target_pairs={{0,1},{1,2},{2,3},{3,4},{4,5},{5,6},{6,7},{7,8},{8,9},{9,10},{10,1... | collective-permute-start | bytes 221192 | tf_op jit(solution)/shard_map/ppermute | solution.py:22
  113.6 5.4 collective-permute-start.15
  114.9 7.2 collective-permute-start.16
  116.3 9.0 %collective-permute-start.17 = (bf16[1,48,6,128]{3,2,1,0:T(8,128)(2,1)S(1)}, bf16[1,48,6,128]{3,2,1,0:T(8,128)(2,1)S(1)}, u32[]{:S(2)}, u32[]{:S(2)}) collective-permute-start(bf16[1,48,6,128]{3,2,1,0:T(8,128)(2,1)S(1)} %get-tuple-element.91), channel_id=1, source_target_pairs={{3,0},{4,1},{5,2},{6,3},{7,4},{8,5},{9,6},{10,7},{11,8},{12,9},{13... | collective-permute-start | bytes 221192 | tf_op jit(solution)/shard_map/ppermute | solution.py:22
  177.5 142.3 %copy-start.9 = (bf16[1,1,48,48,128]{4,3,2,1,0:T(8,128)(2,1)S(1)}, bf16[1,1,48,48,128]{4,3,2,1,0:T(8,128)(2,1)}, u32[]{:S(2)}) copy-start(bf16[1,1,48,48,128]{4,3,2,1,0:T(8,128)(2,1)} %param.10) | copy-start | bytes 1769476
  178.0 141.7 %copy-start.6 = (f32[2304,128]{1,0:T(8,128)S(1)}, f32[2304,128]{1,0:T(8,128)}, u32[]{:S(2)}) copy-start(f32[2304,128]{1,0:T(8,128)} %get-tuple-element.166) | copy-start | bytes 3538948
  178.1 141.7 %copy-start.63 = (f32[128]{0:T(128)S(1)}, f32[128]{0:T(128)}, u32[]{:S(2)}) copy-start(f32[128]{0:T(128)} %param.19) | copy-start | bytes 1540
  178.1 212.1 %collective-permute-start.42 = (bf16[1,6,48,128]{3,2,1,0:T(8,128)(2,1)S(1)}, bf16[1,6,48,128]{3,2,1,0:T(8,128)(2,1)S(1)}, u32[]{:S(2)}, u32[]{:S(2)}) collective-permute-start(bf16[1,6,48,128]{3,2,1,0:T(8,128)(2,1)S(1)} %get-tuple-element.85), channel_id=1, source_target_pairs={{0,3},{1,4},{2,5},{3,6},{4,7},{5,8},{6,9},{7,10},{8,11},{9,12},{10... | collective-permute-start | bytes 221192 | tf_op jit(solution)/shard_map/ppermute | solution.py:22
  183.9 217.6 %collective-permute-start.43 = (bf16[1,6,48,128]{3,2,1,0:T(8,128)(2,1)S(1)}, bf16[1,6,48,128]{3,2,1,0:T(8,128)(2,1)S(1)}, u32[]{:S(2)}, u32[]{:S(2)}) collective-permute-start(bf16[1,6,48,128]{3,2,1,0:T(8,128)(2,1)S(1)} %get-tuple-element.85), channel_id=1, source_target_pairs={{0,2},{1,3},{2,4},{3,5},{4,6},{5,7},{6,8},{7,9},{8,10},{9,11},{10,... | collective-permute-start | bytes 221192 | tf_op jit(solution)/shard_map/ppermute | solution.py:22
  188.9 214.0 %collective-permute-start.44 = (bf16[1,6,48,128]{3,2,1,0:T(8,128)(2,1)S(1)}, bf16[1,6,48,128]{3,2,1,0:T(8,128)(2,1)S(1)}, u32[]{:S(2)}, u32[]{:S(2)}) collective-permute-start(bf16[1,6,48,128]{3,2,1,0:T(8,128)(2,1)S(1)} %get-tuple-element.85), channel_id=1, source_target_pairs={{0,1},{1,2},{2,3},{3,4},{4,5},{5,6},{6,7},{7,8},{8,9},{9,10},{10,1... | collective-permute-start | bytes 221192 | tf_op jit(solution)/shard_map/ppermute | solution.py:22
  191.4 224.1 %collective-permute-start.45 = (bf16[1,6,48,128]{3,2,1,0:T(8,128)(2,1)S(1)}, bf16[1,6,48,128]{3,2,1,0:T(8,128)(2,1)S(1)}, u32[]{:S(2)}, u32[]{:S(2)}) collective-permute-start(bf16[1,6,48,128]{3,2,1,0:T(8,128)(2,1)S(1)} %get-tuple-element.85), channel_id=1, source_target_pairs={{1,0},{2,1},{3,2},{4,3},{5,4},{6,5},{7,6},{8,7},{9,8},{10,9},{11,1... | collective-permute-start | bytes 221192 | tf_op jit(solution)/shard_map/ppermute | solution.py:22
  316.9 4.7 collective-permute-start.24
  321.5 9.3 %collective-permute-start.30 = (bf16[1,48,6,128]{3,2,1,0:T(8,128)(2,1)S(1)}, bf16[1,48,6,128]{3,2,1,0:T(8,128)(2,1)S(1)}, u32[]{:S(2)}, u32[]{:S(2)}) collective-permute-start(bf16[1,48,6,128]{3,2,1,0:T(8,128)(2,1)S(1)} %get-tuple-element.87), channel_id=1, source_target_pairs={{0,3},{1,4},{2,5},{3,6},{4,7},{5,8},{6,9},{7,10},{8,11},{9,12},{10... | collective-permute-start | bytes 221192 | tf_op jit(solution)/shard_map/ppermute | solution.py:22
  330.9 2.9 collective-permute-start.25
  333.8 8.4 %collective-permute-start.26 = (bf16[1,48,6,128]{3,2,1,0:T(8,128)(2,1)S(1)}, bf16[1,48,6,128]{3,2,1,0:T(8,128)(2,1)S(1)}, u32[]{:S(2)}, u32[]{:S(2)}) collective-permute-start(bf16[1,48,6,128]{3,2,1,0:T(8,128)(2,1)S(1)} %get-tuple-element.86), channel_id=1, source_target_pairs={{0,1},{1,2},{2,3},{3,4},{4,5},{5,6},{6,7},{7,8},{8,9},{9,10},{10,1... | collective-permute-start | bytes 221192 | tf_op jit(solution)/shard_map/ppermute | solution.py:22
  342.2 6.1 collective-permute-start.27
  348.3 6.2 collective-permute-start.28
  354.6 8.8 %collective-permute-start.29 = (bf16[1,48,6,128]{3,2,1,0:T(8,128)(2,1)S(1)}, bf16[1,48,6,128]{3,2,1,0:T(8,128)(2,1)S(1)}, u32[]{:S(2)}, u32[]{:S(2)}) collective-permute-start(bf16[1,48,6,128]{3,2,1,0:T(8,128)(2,1)S(1)} %get-tuple-element.86), channel_id=1, source_target_pairs={{3,0},{4,1},{5,2},{6,3},{7,4},{8,5},{9,6},{10,7},{11,8},{12,9},{13... | collective-permute-start | bytes 221192 | tf_op jit(solution)/shard_map/ppermute | solution.py:22
  363.4 6.8 collective-permute-start.31
  370.2 5.4 collective-permute-start.32
  375.6 6.5 collective-permute-start.33
  382.1 6.7 collective-permute-start.34
  388.9 28.0 %collective-permute-start.46 = (bf16[1,6,48,128]{3,2,1,0:T(8,128)(2,1)S(1)}, bf16[1,6,48,128]{3,2,1,0:T(8,128)(2,1)S(1)}, u32[]{:S(2)}, u32[]{:S(2)}) collective-permute-start(bf16[1,6,48,128]{3,2,1,0:T(8,128)(2,1)S(1)} %get-tuple-element.85), channel_id=1, source_target_pairs={{2,0},{3,1},{4,2},{5,3},{6,4},{7,5},{8,6},{9,7},{10,8},{11,9},{12,... | collective-permute-start | bytes 221192 | tf_op jit(solution)/shard_map/ppermute | solution.py:22
  390.2 10.0 %collective-permute-start.36 = (bf16[1,6,48,128]{3,2,1,0:T(8,128)(2,1)S(1)}, bf16[1,6,48,128]{3,2,1,0:T(8,128)(2,1)S(1)}, u32[]{:S(2)}, u32[]{:S(2)}) collective-permute-start(bf16[1,6,48,128]{3,2,1,0:T(8,128)(2,1)S(1)} %get-tuple-element.84), channel_id=1, source_target_pairs={{0,3},{1,4},{2,5},{3,6},{4,7},{5,8},{6,9},{7,10},{8,11},{9,12},{10... | collective-permute-start | bytes 221192 | tf_op jit(solution)/shard_map/ppermute | solution.py:22
  400.2 18.0 %collective-permute-start.47 = (bf16[1,6,48,128]{3,2,1,0:T(8,128)(2,1)S(1)}, bf16[1,6,48,128]{3,2,1,0:T(8,128)(2,1)S(1)}, u32[]{:S(2)}, u32[]{:S(2)}) collective-permute-start(bf16[1,6,48,128]{3,2,1,0:T(8,128)(2,1)S(1)} %get-tuple-element.85), channel_id=1, source_target_pairs={{3,0},{4,1},{5,2},{6,3},{7,4},{8,5},{9,6},{10,7},{11,8},{12,9},{13... | collective-permute-start | bytes 221192 | tf_op jit(solution)/shard_map/ppermute | solution.py:22
  401.5 8.0 %collective-permute-start.35 = (bf16[1,48,6,128]{3,2,1,0:T(8,128)(2,1)S(1)}, bf16[1,48,6,128]{3,2,1,0:T(8,128)(2,1)S(1)}, u32[]{:S(2)}, u32[]{:S(2)}) collective-permute-start(bf16[1,48,6,128]{3,2,1,0:T(8,128)(2,1)S(1)} %get-tuple-element.87), channel_id=1, source_target_pairs={{3,0},{4,1},{5,2},{6,3},{7,4},{8,5},{9,6},{10,7},{11,8},{12,9},{13... | collective-permute-start | bytes 221192 | tf_op jit(solution)/shard_map/ppermute | solution.py:22
  402.9 16.8 %collective-permute-start.37 = (bf16[1,6,48,128]{3,2,1,0:T(8,128)(2,1)S(1)}, bf16[1,6,48,128]{3,2,1,0:T(8,128)(2,1)S(1)}, u32[]{:S(2)}, u32[]{:S(2)}) collective-permute-start(bf16[1,6,48,128]{3,2,1,0:T(8,128)(2,1)S(1)} %get-tuple-element.84), channel_id=1, source_target_pairs={{0,2},{1,3},{2,4},{3,5},{4,6},{5,7},{6,8},{7,9},{8,10},{9,11},{10,... | collective-permute-start | bytes 221192 | tf_op jit(solution)/shard_map/ppermute | solution.py:22
  409.5 10.2 %collective-permute-start.38 = (bf16[1,6,48,128]{3,2,1,0:T(8,128)(2,1)S(1)}, bf16[1,6,48,128]{3,2,1,0:T(8,128)(2,1)S(1)}, u32[]{:S(2)}, u32[]{:S(2)}) collective-permute-start(bf16[1,6,48,128]{3,2,1,0:T(8,128)(2,1)S(1)} %get-tuple-element.84), channel_id=1, source_target_pairs={{0,1},{1,2},{2,3},{3,4},{4,5},{5,6},{6,7},{7,8},{8,9},{9,10},{10,1... | collective-permute-start | bytes 221192 | tf_op jit(solution)/shard_map/ppermute | solution.py:22
  415.5 6.3 collective-permute-start.39
  416.9 9.0 %collective-permute-start.40 = (bf16[1,6,48,128]{3,2,1,0:T(8,128)(2,1)S(1)}, bf16[1,6,48,128]{3,2,1,0:T(8,128)(2,1)S(1)}, u32[]{:S(2)}, u32[]{:S(2)}) collective-permute-start(bf16[1,6,48,128]{3,2,1,0:T(8,128)(2,1)S(1)} %get-tuple-element.84), channel_id=1, source_target_pairs={{2,0},{3,1},{4,2},{5,3},{6,4},{7,5},{8,6},{9,7},{10,8},{11,9},{12,... | collective-permute-start | bytes 221192 | tf_op jit(solution)/shard_map/ppermute | solution.py:22
  418.2 10.3 %collective-permute-start.41 = (bf16[1,6,48,128]{3,2,1,0:T(8,128)(2,1)S(1)}, bf16[1,6,48,128]{3,2,1,0:T(8,128)(2,1)S(1)}, u32[]{:S(2)}, u32[]{:S(2)}) collective-permute-start(bf16[1,6,48,128]{3,2,1,0:T(8,128)(2,1)S(1)} %get-tuple-element.84), channel_id=1, source_target_pairs={{3,0},{4,1},{5,2},{6,3},{7,4},{8,5},{9,6},{10,7},{11,8},{12,9},{13... | collective-permute-start | bytes 221192 | tf_op jit(solution)/shard_map/ppermute | solution.py:22
  (50 other events, 704.9 us)
Sparse Core Ops, SparseCore 0:
  319.9 454.0 all-reduce.3
where the time goes:
time: 787 us; the launch traced here: 784 us
  waiting for transfers between devices  410 us (52%)
  starting transfers between devices  150 us (19%)
  blocking collectives  122 us (16%)
  other arithmetic  46.8 us (6%)
  between operations  26.6 us (3%)
  matrix products  24 us (3%)
    psum x1, waiting for transfers between devices, local(): lax.psum((partials[0], partials[1], partials[2], partials[3], partials[4]...  334 us
    ppermute x48, starting transfers between devices, shifted(): lax.ppermute(value, axis, [(source, source + steps) for source in range(l...  150 us
    psum x1, blocking collectives, local(): lax.psum((partials[0], partials[1], partials[2], partials[3], partials[4]...  122 us
    ppermute x48, waiting for transfers between devices, shifted(): lax.ppermute(value, axis, [(source, source + steps) for source in range(l...  76.8 us
  transfers between devices with their start and end apart: 49, of which 26 were waited for; matrix products, arithmetic and copies ran while one was open for 2% of the time, Pallas kernels for 0%

commit v1 on v0

--- a/solution.py
+++ b/solution.py
@@ -22,60 +22,63 @@
     return lax.ppermute(value, axis, [(source, source + steps) for source in range(leading, last)])
 
 
-def gather_rims(centre):
-    top_rows = centre[:, :HALO]
-    bottom_rows = centre[:, -HALO:]
-    left_columns = centre[:, :, :HALO]
-    right_columns = centre[:, :, -HALO:]
-    zero_rows = jnp.zeros_like(top_rows)
-    zero_columns = jnp.zeros_like(left_columns)
-    north_pool = []
-    south_pool = []
-    west_pool = []
-    east_pool = []
-    for offset in range(-REACH, REACH + 1):
-        if offset == 0:
-            north_pool.append(zero_rows)
-            south_pool.append(zero_rows)
-            west_pool.append(zero_columns)
-            east_pool.append(zero_columns)
-        else:
-            received = shifted(
-                (top_rows, bottom_rows, left_columns, right_columns), "space", -offset
-            )
-            south_pool.append(received[0])
-            north_pool.append(received[1])
-            east_pool.append(received[2])
-            west_pool.append(received[3])
-    return (
-        jnp.stack(north_pool),
-        jnp.stack(south_pool),
-        jnp.stack(west_pool),
-        jnp.stack(east_pool),
-    )
-
-
-def choose_strip(stacked, beside_ids, position, direction):
-    source = beside_ids[direction]
-    slot_index = jnp.clip(source - position + REACH, 0, 2 * REACH)
-    strip = lax.dynamic_index_in_dim(stacked, slot_index, 0, keepdims=False)
-    return jnp.where(source >= 0, strip, jnp.zeros_like(strip))
-
-
 def extend_tiles(centre, beside_ids, position):
-    north_pool, south_pool, west_pool, east_pool = gather_rims(centre)
-    north = choose_strip(north_pool, beside_ids, position, 0)
-    south = choose_strip(south_pool, beside_ids, position, 1)
-    west = choose_strip(west_pool, beside_ids, position, 2)
-    east = choose_strip(east_pool, beside_ids, position, 3)
-    north_west = choose_strip(north_pool, beside_ids, position, 4)[:, :, -HALO:]
-    north_east = choose_strip(north_pool, beside_ids, position, 5)[:, :, :HALO]
-    south_west = choose_strip(south_pool, beside_ids, position, 6)[:, :, -HALO:]
-    south_east = choose_strip(south_pool, beside_ids, position, 7)[:, :, :HALO]
+    lead, rows, cols, channels = centre.shape
+    top = centre[:, :HALO].reshape(lead, HALO * cols, channels)
+    bottom = centre[:, -HALO:].reshape(lead, HALO * cols, channels)
+    left = centre[:, :, :HALO].reshape(lead, rows * HALO, channels)
+    right = centre[:, :, -HALO:].reshape(lead, rows * HALO, channels)
+    west_step = beside_ids[2] - position
+    east_step = beside_ids[3] - position
+    has_west = beside_ids[2] >= 0
+    has_east = beside_ids[3] >= 0
+    received = []
+    for step in (-3, -2, -1, 1, 2, 3):
+        outgoing = top if step < 0 else bottom
+        if abs(step) == 1:
+            outgoing = jnp.where(has_west & (west_step == step), left, outgoing)
+            outgoing = jnp.where(has_east & (east_step == step), right, outgoing)
+        received.append((step, shifted(outgoing, "space", step)))
+    pool = {-step: value for step, value in received}
+
+    def choose(direction, steps):
+        source = beside_ids[direction]
+        strip = jnp.zeros_like(top)
+        for step in steps:
+            strip = jnp.where((source >= 0) & (source - position == step), pool[step], strip)
+        return strip
+
+    def as_rows(strip):
+        return strip.reshape(lead, HALO, cols, channels)
+
+    def as_cols(strip):
+        return strip.reshape(lead, rows, HALO, channels)
+
+    below, above = (-1, -2, -3), (1, 2, 3)
+    north = as_rows(choose(0, below))
+    south = as_rows(choose(1, above))
+    west = as_cols(choose(2, (-1, 1)))
+    east = as_cols(choose(3, (-1, 1)))
+    north_west = as_rows(choose(4, below))[:, :, -HALO:]
+    north_east = as_rows(choose(5, below))[:, :, :HALO]
+    south_west = as_rows(choose(6, above))[:, :, -HALO:]
+    south_east = as_rows(choose(7, above))[:, :, :HALO]
     upper = jnp.concatenate([north_west, north, north_east], axis=2)
     middle = jnp.concatenate([west, centre, east], axis=2)
     lower = jnp.concatenate([south_west, south, south_east], axis=2)
     return jnp.concatenate([upper, middle, lower], axis=1)
+
+
+def summed_everywhere(flat):
+    rows, lanes = flat.shape
+    dp, space = lax.axis_size("dp"), lax.axis_size("space")
+    part = lax.all_to_all(flat.reshape(dp, rows // dp, lanes), "dp", 0, 0, tiled=True)
+    part = jnp.sum(part, axis=0).reshape(space, -1)
+    part = jnp.sum(lax.all_to_all(part, "space", 0, 0, tiled=True), axis=0)
+    part = jnp.broadcast_to(part, (space,) + part.shape)
+    part = lax.all_to_all(part, "space", 0, 0, tiled=True).reshape(rows // dp, lanes)
+    part = jnp.broadcast_to(part, (dp,) + part.shape)
+    return lax.all_to_all(part, "dp", 0, 0, tiled=True).reshape(rows, lanes)
 
 
 def depthwise(extended, conv_kernel):
@@ -234,10 +237,16 @@
         down_weight,
         layer_scale,
     )
-    totals = lax.psum(
-        (partials[0], partials[1], partials[2], partials[3], partials[4], partials[5]),
-        ("dp", "space"),
-    )
+    leaves = [leaf.reshape(-1, 128) for leaf in partials]
+    counts = [leaf.shape[0] for leaf in leaves]
+    unit = lax.axis_size("dp") * 4
+    spare = -sum(counts) % unit
+    flat = jnp.concatenate(leaves + [jnp.zeros((spare, 128), jnp.float32)], axis=0)
+    flat = summed_everywhere(flat)
+    totals, at = [], 0
+    for leaf, count in zip(partials, counts):
+        totals.append(flat[at : at + count].reshape(leaf.shape))
+        at += count
     cell_count = (
         fields.shape[0]
         * lax.axis_size("dp")

time: 787 us -> 205 us (0.26)
  waiting for transfers between devices: 410 us -> 34.2 us
  blocking collectives: 122 us -> 0 us
  starting transfers between devices: 150 us -> 79.5 us
  between operations: 26.6 us -> 13.3 us
    psum x1 -> x0, waiting for transfers between devices: 334 us -> none  [local(): lax.psum((partials[0], partials[1], partials[2], partials[3], partials[4]...]
    psum x1 -> x0, blocking collectives: 122 us -> none  [local(): lax.psum((partials[0], partials[1], partials[2], partials[3], partials[4]...]
    ppermute x48 -> x12, starting transfers between devices: 150 us -> 36 us  [shifted(): lax.ppermute(value, axis, [(source, source + steps) for source in range(l...]
    ppermute x48 -> x12, waiting for transfers between devices: 76.8 us -> 8.52 us  [shifted(): lax.ppermute(value, axis, [(source, source + steps) for source in range(l...]
    all_to_all x0 -> x4, starting transfers between devices: none -> 43.5 us  [the longest x1 19 us: summed_everywhere(): part = jnp.sum(lax.all_to_all(part, 'space', 0, 0, tiled=True), axis=0)]
    all_to_all x0 -> x4, waiting for transfers between devices: none -> 25.7 us  [the longest x1 12.2 us: summed_everywhere(): part = jnp.sum(lax.all_to_all(part, 'space', 0, 0, tiled=True), axis=0)]
  transfers between devices with their start and end apart: 49 -> 16, of which waited for: 26 -> 6; matrix products, arithmetic and copies ran while one was open for 2% -> 9% of each run, Pallas kernels for 0% -> 0%
where the time goes in v1:
time: 205 us; the launch traced here: 203 us
  starting transfers between devices  79.5 us (39%)
  other arithmetic  46.1 us (22%)
  waiting for transfers between devices  34.2 us (17%)
  matrix products  19.2 us (9%)
  between operations  13.3 us (6%)
  local copies, waits for them, and re-layouts  11 us (5%)
    ppermute x12, starting transfers between devices, shifted(): lax.ppermute(value, axis, [(source, source + steps) for source in range(l...  36 us
    all_to_all x1, starting transfers between devices, summed_everywhere(): part = jnp.sum(lax.all_to_all(part, 'space', 0, 0, tiled=True), axis=0)  19 us
    all_to_all x1, waiting for transfers between devices, summed_everywhere(): part = jnp.sum(lax.all_to_all(part, 'space', 0, 0, tiled=True), axis=0)  12.2 us
    reduce_sum x4, other arithmetic, kernel_sums(): jnp.sum(upstream * window.astype(jnp.float32), axis=lead_axes)  11.6 us
    all_to_all x1, waiting for transfers between devices, summed_everywhere(): lax.all_to_all(part, 'space', 0, 0, tiled=True).reshape(rows // dp, lanes)  11.6 us
    reduce_sum x1, other arithmetic, block_pass(): chan_mean = jnp.mean(conv, axis=-1, keepdims=True)  11.4 us
    broadcast_in_dim x1, other arithmetic, local(): fields_grad[:, None]  11 us
    dot_general x1, matrix products, block_pass(): jnp.dot(normed, up_weight, preferred_element_type=jnp.float32) + up_bias  10.9 us
  transfers between devices with their start and end apart: 16, of which 6 were waited for; matrix products, arithmetic and copies ran while one was open for 9% of the time, Pallas kernels for 0%

profile of v1, /device:TPU:1, one launch (start us, length us, event | category | flops | bytes accessed | tf_op | source)
XLA Modules:
  0.0 203.4 jit_solution(3318624659379727672)
XLA Ops:
  0.7 1.4 fusion.159
  2.1 1.4 bitcast_multiply_fusion.2
  3.6 5.3 %collective-permute-start = (bf16[1,288,128]{2,1,0:T(8,128)(2,1)S(1)}, bf16[1,288,128]{2,1,0:T(8,128)(2,1)S(1)}, u32[]{:S(2)}, u32[]{:S(2)}) collective-permute-start(bf16[1,288,128]{2,1,0:T(8,128)(2,1)S(1)} %bitcast.247), channel_id=1, source_target_pairs={{0,3},{1,4},{2,5},{3,6},{4,7},{5,8},{6,9},{7,10},{8,11},{9,12},{10... | collective-permute-start | bytes 221192 | tf_op jit(solution)/shard_map/ppermute | solution.py:22
  8.9 3.5 %collective-permute-start.1 = (bf16[1,288,128]{2,1,0:T(8,128)(2,1)S(1)}, bf16[1,288,128]{2,1,0:T(8,128)(2,1)S(1)}, u32[]{:S(2)}, u32[]{:S(2)}) collective-permute-start(bf16[1,288,128]{2,1,0:T(8,128)(2,1)S(1)} %bitcast.248), channel_id=1, source_target_pairs={{0,2},{1,3},{2,4},{3,5},{4,6},{5,7},{6,8},{7,9},{8,10},{9,11},{10,... | collective-permute-start | bytes 221192 | tf_op jit(solution)/shard_map/ppermute | solution.py:22
  12.4 0.7 fusion.160
  15.9 1.3 collective-permute-start.3
  17.2 4.1 %collective-permute-start.2 = (bf16[1,288,128]{2,1,0:T(8,128)(2,1)S(1)}, bf16[1,288,128]{2,1,0:T(8,128)(2,1)S(1)}, u32[]{:S(2)}, u32[]{:S(2)}) collective-permute-start(bf16[1,288,128]{2,1,0:T(8,128)(2,1)S(1)} %get-tuple-element.108), channel_id=1, source_target_pairs={{0,1},{1,2},{2,3},{3,4},{4,5},{5,6},{6,7},{7,8},{8,9},{9,10},{10,1... | collective-permute-start | bytes 221192 | tf_op jit(solution)/shard_map/ppermute | solution.py:22
  21.4 1.3 collective-permute-start.4
  23.1 0.6 slice_bitcast_fusion.46
  31.5 0.1 mul.1352
  31.5 1.3 collective-permute-start.5
  32.9 0.1 select_select_fusion.18
  33.0 5.0 %collective-permute-done.5 = bf16[1,288,128]{2,1,0:T(8,128)(2,1)S(1)} collective-permute-done((bf16[1,288,128]{2,1,0:T(8,128)(2,1)S(1)}, bf16[1,288,128]{2,1,0:T(8,128)(2,1)S(1)}, u32[]{:S(2)}, u32[]{:S(2)}) %collective-permute-start.5) | collective-permute-done | bytes 73760 | tf_op jit(solution)/shard_map/ppermute | solution.py:22
  38.1 0.5 maximum_maximum_fusion
  39.0 11.4 %fusion.153 = (f32[48,48]{1,0:T(8,128)S(1)}, f32[1,48,48,128]{3,2,1,0:T(8,128)S(1)}) fusion(bf16[1,54,60,128]{3,2,1,0:T(8,128)(2,1)S(1)} %get-tuple-element.75, f32[128]{0:T(128)} %get-tuple-element.161, f32[128]{0:T(128)} %get-tuple-element.162, f32[128]{0:T(128)S(1)} %get-tuple-element.115, f32[128]{0:T(128)S(1)} %get-tuple-element.116, ...), kind=kLoop, calls=%fused_computation.389 | loop fusion | flops 48658176 | bytes 26723840 | tf_op jit(solution)/shard_map/reduce_sum | solution.py:155
  50.5 0.7 multiply_reduce_fusion.3
  51.2 0.8 multiply_convert_fusion.1
  52.1 10.9 %fusion.2 = (bf16[2304,512]{1,0:T(8,128)(2,1)S(1)}, f32[2304,512]{1,0:T(8,128)S(1)}) fusion(f32[512]{0:T(512)S(1)} %copy-done.114, bf16[2304,128]{1,0:T(8,128)(2,1)S(1)} %bitcast.239, bf16[128,512]{1,0:T(8,128)(2,1)S(1)} %copy-done), kind=kOutput, calls=%fused_computation.56 | convolution fusion | flops 379846656 | bytes 7800832 | tf_op jit(solution)/shard_map/dot_general | solution.py:160
  63.0 2.3 %fusion.140 = (f32[128]{0:T(128)}, bf16[2304,128]{1,0:T(8,128)(2,1)S(1)}, f32[2304,128]{1,0:T(8,128)}) fusion(bf16[1,1,48,48,128]{4,3,2,1,0:T(8,128)(2,1)S(1)} %copy-done.7, f32[2304]{0:T(1024)S(1)} %mul.1352, f32[128]{0:T(128)S(1)} %copy-done.112, bf16[2304,512]{1,0:T(8,128)(2,1)S(1)} %get-tuple-element.174, bf16[512,128]{1,0:T(8,128)(2,1)S(1)} %copy-done.14), kind=kOutput, calls=%fused_computation.255 | convolution fusion | flops 304054144 | bytes 4859904 | tf_op jit(solution)/shard_map/dot_general | solution.py:162
  65.3 0.8 fusion.162
  66.1 3.1 %convert_reduce_fusion = (f32[512]{0:T(512)}, bf16[2304,512]{1,0:T(8,128)(2,1)S(1)}) fusion(f32[2304,512]{1,0:T(8,128)S(1)} %get-tuple-element.175, bf16[2304,128]{1,0:T(8,128)(2,1)S(1)} %get-tuple-element.77, bf16[512,128]{1,0:T(8,128)(2,1)S(1)} %copy-done.14), kind=kOutput, calls=%fused_computation.61 | convolution fusion | flops 316145152 | bytes 7800832 | tf_op jit(solution)/shard_map/dot_general | solution.py:170
  69.2 1.2 fusion.161
  70.5 0.9 multiply_reduce_fusion.2
  71.3 1.0 copy-done.5
  72.4 1.6 multiply_reduce_fusion
  74.0 0.6 broadcast_multiply_fusion
  74.6 0.7 div.17
  75.3 6.0 %fusion.136 = (f32[128]{0:T(128)S(1)}, f32[128]{0:T(128)}, f32[128]{0:T(128)}, f32[128]{0:T(128)}, f32[128]{0:T(128)}, /*index=5*/f32[128]{0:T(128)}, f32[128]{0...) fusion(bf16[1,54,60,128]{3,2,1,0:T(8,128)(2,1)S(1)} %get-tuple-, ...), kind=kLoop, calls=%fused_computation.248 | loop fusion | flops 18577152 | bytes 13612544 | tf_op jit(solution)/shard_map/reduce_sum | solution.py:134
  81.3 2.1 %fusion.135 = (f32[128]{0:T(128)S(1)}, f32[128]{0:T(128)S(1)}, f32[128]{0:T(128)S(1)}, f32[128]{0:T(128)S(1)}, f32[128]{0:T(128)S(1)}, /*index=5*/f32[128]{0:T(1...) fusion(bf16[1,48,48,128]{3,2,1,0:T(8,128)(2,1)S(1)} %get-tuple-element.69, ...), kind=kLoop, calls=%fused_computation.247 | loop fusion | flops 14449408 | bytes 3101696 | tf_op jit(solution)/shard_map/reduce_sum | solution.py:134
  83.4 3.0 %fusion.108 = (f32[128]{0:T(128)S(1)}, f32[128]{0:T(128)S(1)}, f32[128]{0:T(128)S(1)}, f32[128]{0:T(128)S(1)}, f32[128]{0:T(128)S(1)}, /*index=5*/f32[128]{0:T(1...) fusion(bf16[1,48,48,128]{3,2,1,0:T(8,128)(2,1)S(1)} %get-tuple-, ...), kind=kLoop, calls=%fused_computation.220 | loop fusion | flops 16217856 | bytes 11215872 | tf_op jit(solution)/shard_map/reduce_sum | solution.py:134
  86.4 0.5 fusion.91
  87.2 6.2 %collective-permute-start.10 = (bf16[1,288,128]{2,1,0:T(8,128)(2,1)S(1)}, bf16[1,288,128]{2,1,0:T(8,128)(2,1)S(1)}, u32[]{:S(2)}, u32[]{:S(2)}) collective-permute-start(bf16[1,288,128]{2,1,0:T(8,128)(2,1)S(1)} %bitcast.251), channel_id=1, source_target_pairs={{0,3},{1,4},{2,5},{3,6},{4,7},{5,8},{6,9},{7,10},{8,11},{9,12},{10... | collective-permute-start | bytes 221192 | tf_op jit(solution)/shard_map/ppermute | solution.py:22
  93.5 5.4 %collective-permute-start.11 = (bf16[1,288,128]{2,1,0:T(8,128)(2,1)S(1)}, bf16[1,288,128]{2,1,0:T(8,128)(2,1)}, u32[]{:S(2)}, u32[]{:S(2)}) collective-permute-start(bf16[1,288,128]{2,1,0:T(8,128)(2,1)S(1)} %bitcast.252), channel_id=1, source_target_pairs={{0,2},{1,3},{2,4},{3,5},{4,6},{5,7},{6,8},{7,9},{8,10},{9,11},{10,... | collective-permute-start | bytes 221192 | tf_op jit(solution)/shard_map/ppermute | solution.py:22
  98.8 1.3 collective-permute-start.8
  100.1 1.3 collective-permute-start.9
  101.9 1.1 concatenate.149
  103.1 0.9 reshape.626
  103.9 10.3 %all-to-all-start = ((f32[16,68,128]{2,1,0:T(8,128)}), f32[16,68,128]{2,1,0:T(8,128)S(1)}, u32[]{:S(2)}, u32[]{:S(2)}) async-start(f32[16,68,128]{2,1,0:T(8,128)} %reshape.626), calls=%async_computation | async-start | bytes 1179648 | tf_op jit(solution)/shard_map/all_to_all | solution.py:75
  114.3 3.6 %collective-permute-start.7 = (bf16[1,288,128]{2,1,0:T(8,128)(2,1)S(1)}, bf16[1,288,128]{2,1,0:T(8,128)(2,1)S(1)}, u32[]{:S(2)}, u32[]{:S(2)}) collective-permute-start(bf16[1,288,128]{2,1,0:T(8,128)(2,1)S(1)} %get-tuple-element.104), channel_id=1, source_target_pairs={{0,1},{1,2},{2,3},{3,4},{4,5},{5,6},{6,7},{7,8},{8,9},{9,10},{10,1... | collective-permute-start | bytes 221192 | tf_op jit(solution)/shard_map/ppermute | solution.py:22
  118.0 1.2 add_convert_fusion
  119.2 3.5 %collective-permute-done.7 = bf16[1,288,128]{2,1,0:T(8,128)(2,1)S(1)} collective-permute-done((bf16[1,288,128]{2,1,0:T(8,128)(2,1)S(1)}, bf16[1,288,128]{2,1,0:T(8,128)(2,1)S(1)}, u32[]{:S(2)}, u32[]{:S(2)}) %collective-permute-start.7) | collective-permute-done | bytes 73760 | tf_op jit(solution)/shard_map/ppermute | solution.py:22
  122.7 1.3 collective-permute-start.6
  124.0 0.9 select_select_fusion.2
  125.0 1.3 all-to-all-done
  126.3 0.7 all_to_all.17
  127.0 19.0 %all-to-all-start.1 = ((f32[32,1,272]{2,1,0:T(1,128)}), f32[32,1,272]{2,1,0:T(1,128)S(1)}, u32[]{:S(2)}, u32[]{:S(2)}) async-start(f32[32,1,272]{2,1,0:T(1,128)} %all_to_all.17), calls=%async_computation.1 | async-start | bytes 98304 | tf_op jit(solution)/shard_map/all_to_all | solution.py:77
  146.2 12.2 %all-to-all-done.1 = f32[32,1,272]{2,1,0:T(1,128)S(1)} async-done(((f32[32,1,272]{2,1,0:T(1,128)}), f32[32,1,272]{2,1,0:T(1,128)S(1)}, u32[]{:S(2)}, u32[]{:S(2)}) %all-to-all-start.1) | async-done | bytes 34848 | tf_op jit(solution)/shard_map/all_to_all | solution.py:77
  158.4 0.1 reduce_sum.579
  158.5 0.6 broadcast_in_dim.10
  159.1 3.9 %all-to-all-start.2 = ((f32[32,1,272]{2,1,0:T(1,128)}), f32[32,1,272]{2,1,0:T(1,128)S(1)}, u32[]{:S(2)}, u32[]{:S(2)}) async-start(f32[32,1,272]{2,1,0:T(1,128)} %broadcast_in_dim.10), calls=%async_computation.2 | async-start | bytes 98304 | tf_op jit(solution)/shard_map/all_to_all | solution.py:79
  163.0 0.5 maximum_maximum_fusion.2
  164.0 11.6 %all-to-all-done.2 = f32[32,1,272]{2,1,0:T(1,128)S(1)} async-done(((f32[32,1,272]{2,1,0:T(1,128)}), f32[32,1,272]{2,1,0:T(1,128)S(1)}, u32[]{:S(2)}, u32[]{:S(2)}) %all-to-all-start.2) | async-done | bytes 34848 | tf_op jit(solution)/shard_map/all_to_all | solution.py:79
  175.5 0.1 reduce.6
  175.6 0.1 reshape.627
  175.7 0.8 broadcast_in_dim.11
  176.6 10.3 %all-to-all-start.3 = ((f32[16,68,128]{2,1,0:T(8,128)}), f32[16,68,128]{2,1,0:T(8,128)}, u32[]{:S(2)}, u32[]{:S(2)}) async-start(f32[16,68,128]{2,1,0:T(8,128)} %broadcast_in_dim.11), calls=%async_computation.3 | async-start | bytes 1179648 | tf_op jit(solution)/shard_map/all_to_all | solution.py:81
  187.3 11.0 %fusion.149 = bf16[1,1,48,48,128]{4,3,2,1,0:T(8,128)(2,1)} fusion(bf16[1,54,60,128]{3,2,1,0:T(8,128)(2,1)S(1)} %get-tuple-element.73, f32[128]{0:T(128)} %get-tuple-element.161, f32[128]{0:T(128)} %get-tuple-element.162, f32[128]{0:T(128)S(1)} %copy-done.21, f32[128]{0:T(128)S(1)} %copy-done.23, f32[128]{0:T(128)S(1)} %copy-done.25, f32[128]{0:T(128)S(1)} %copy-done.27, ...), kind=kLoop, calls=%fused_computation.297 | loop fusion | flops 49545216 | bytes 26723840 | tf_op jit(solution)/shard_map/broadcast_in_dim | solution.py:260
  198.4 0.7 all-to-all-done.3
  199.0 1.1 reshape.628
  200.1 0.8 slice_multiply_fusion
  200.9 0.6 fusion.150
  201.5 0.5 fusion.151
  202.0 0.7 mul.1482
  202.8 0.6 mul.1477
  (287 shorter events, 1.4 us)
Async XLA Ops:
  0.6 51.4 %copy-start = (bf16[128,512]{1,0:T(8,128)(2,1)S(1)}, bf16[128,512]{1,0:T(8,128)(2,1)}, u32[]{:S(2)}) copy-start(bf16[128,512]{1,0:T(8,128)(2,1)} %param.16) | copy-start | bytes 393220
  2.1 20.6 %copy-start.16 = (f32[7,7,128]{2,1,0:T(8,128)S(1)}, f32[7,7,128]{2,1,0:T(8,128)}, u32[]{:S(2)}) copy-start(f32[7,7,128]{2,1,0:T(8,128)} %param.14) | copy-start | bytes 75268
  3.5 34.6 %copy-start.3 = (bf16[1,48,48,128]{3,2,1,0:T(8,128)(2,1)}, bf16[1,48,48,128]{3,2,1,0:T(8,128)(2,1)S(1)}, u32[]{:S(2)}) copy-start(bf16[1,48,48,128]{3,2,1,0:T(8,128)(2,1)S(1)} %bitcast_multiply_fusion.2) | copy-start | bytes 1769476
  3.6 29.3 %collective-permute-start = (bf16[1,288,128]{2,1,0:T(8,128)(2,1)S(1)}, bf16[1,288,128]{2,1,0:T(8,128)(2,1)S(1)}, u32[]{:S(2)}, u32[]{:S(2)}) collective-permute-start(bf16[1,288,128]{2,1,0:T(8,128)(2,1)S(1)} %bitcast.247), channel_id=1, source_target_pairs={{0,3},{1,4},{2,5},{3,6},{4,7},{5,8},{6,9},{7,10},{8,11},{9,12},{10... | collective-permute-start | bytes 221192 | tf_op jit(solution)/shard_map/ppermute | solution.py:22
  8.9 24.0 %collective-permute-start.1 = (bf16[1,288,128]{2,1,0:T(8,128)(2,1)S(1)}, bf16[1,288,128]{2,1,0:T(8,128)(2,1)S(1)}, u32[]{:S(2)}, u32[]{:S(2)}) collective-permute-start(bf16[1,288,128]{2,1,0:T(8,128)(2,1)S(1)} %bitcast.248), channel_id=1, source_target_pairs={{0,2},{1,3},{2,4},{3,5},{4,6},{5,7},{6,8},{7,9},{8,10},{9,11},{10,... | collective-permute-start | bytes 221192 | tf_op jit(solution)/shard_map/ppermute | solution.py:22
  15.9 15.6 %collective-permute-start.3 = (bf16[1,288,128]{2,1,0:T(8,128)(2,1)S(1)}, bf16[1,288,128]{2,1,0:T(8,128)(2,1)S(1)}, u32[]{:S(2)}, u32[]{:S(2)}) collective-permute-start(bf16[1,288,128]{2,1,0:T(8,128)(2,1)S(1)} %get-tuple-element.109), channel_id=1, source_target_pairs={{1,0},{2,1},{3,2},{4,3},{5,4},{6,5},{7,6},{8,7},{9,8},{10,9},{11,1... | collective-permute-start | bytes 221192 | tf_op jit(solution)/shard_map/ppermute | solution.py:22
  17.2 15.6 %collective-permute-start.2 = (bf16[1,288,128]{2,1,0:T(8,128)(2,1)S(1)}, bf16[1,288,128]{2,1,0:T(8,128)(2,1)S(1)}, u32[]{:S(2)}, u32[]{:S(2)}) collective-permute-start(bf16[1,288,128]{2,1,0:T(8,128)(2,1)S(1)} %get-tuple-element.108), channel_id=1, source_target_pairs={{0,1},{1,2},{2,3},{3,4},{4,5},{5,6},{6,7},{7,8},{8,9},{9,10},{10,1... | collective-permute-start | bytes 221192 | tf_op jit(solution)/shard_map/ppermute | solution.py:22
  21.4 11.7 %collective-permute-start.4 = (bf16[1,288,128]{2,1,0:T(8,128)(2,1)S(1)}, bf16[1,288,128]{2,1,0:T(8,128)(2,1)S(1)}, u32[]{:S(2)}, u32[]{:S(2)}) collective-permute-start(bf16[1,288,128]{2,1,0:T(8,128)(2,1)S(1)} %bitcast.245), channel_id=1, source_target_pairs={{3,0},{4,1},{5,2},{6,3},{7,4},{8,5},{9,6},{10,7},{11,8},{12,9},{13... | collective-permute-start | bytes 221192 | tf_op jit(solution)/shard_map/ppermute | solution.py:22
  22.7 16.0 %copy-start.18 = (f32[128]{0:T(128)}, f32[128]{0:T(128)S(1)}, u32[]{:S(2)}) copy-start(f32[128]{0:T(128)S(1)} %get-tuple-element.114) | copy-start | bytes 1540
  22.7 16.0 %copy-start.20 = (f32[128]{0:T(128)}, f32[128]{0:T(128)S(1)}, u32[]{:S(2)}) copy-start(f32[128]{0:T(128)S(1)} %get-tuple-element.115) | copy-start | bytes 1540
  22.7 16.0 %copy-start.22 = (f32[128]{0:T(128)}, f32[128]{0:T(128)S(1)}, u32[]{:S(2)}) copy-start(f32[128]{0:T(128)S(1)} %get-tuple-element.116) | copy-start | bytes 1540
  31.5 6.5 %collective-permute-start.5 = (bf16[1,288,128]{2,1,0:T(8,128)(2,1)S(1)}, bf16[1,288,128]{2,1,0:T(8,128)(2,1)S(1)}, u32[]{:S(2)}, u32[]{:S(2)}) collective-permute-start(bf16[1,288,128]{2,1,0:T(8,128)(2,1)S(1)} %bitcast.246), channel_id=1, source_target_pairs={{2,0},{3,1},{4,2},{5,3},{6,4},{7,5},{8,6},{9,7},{10,8},{11,9},{12,... | collective-permute-start | bytes 221192 | tf_op jit(solution)/shard_map/ppermute | solution.py:22
  50.5 20.9 %copy-start.11 = (f32[48,48]{1,0:T(8,128)}, f32[48,48]{1,0:T(8,128)S(1)}, u32[]{:S(2)}) copy-start(f32[48,48]{1,0:T(8,128)S(1)} %broadcast_multiply_fusion.1) | copy-start | bytes 27652
  51.2 20.1 %copy-start.12 = (f32[48,48]{1,0:T(8,128)}, f32[48,48]{1,0:T(8,128)S(1)}, u32[]{:S(2)}) copy-start(f32[48,48]{1,0:T(8,128)S(1)} %add_rsqrt_fusion) | copy-start | bytes 27652
  87.2 36.8 %collective-permute-start.10 = (bf16[1,288,128]{2,1,0:T(8,128)(2,1)S(1)}, bf16[1,288,128]{2,1,0:T(8,128)(2,1)S(1)}, u32[]{:S(2)}, u32[]{:S(2)}) collective-permute-start(bf16[1,288,128]{2,1,0:T(8,128)(2,1)S(1)} %bitcast.251), channel_id=1, source_target_pairs={{0,3},{1,4},{2,5},{3,6},{4,7},{5,8},{6,9},{7,10},{8,11},{9,12},{10... | collective-permute-start | bytes 221192 | tf_op jit(solution)/shard_map/ppermute | solution.py:22
  93.5 30.5 %collective-permute-start.11 = (bf16[1,288,128]{2,1,0:T(8,128)(2,1)S(1)}, bf16[1,288,128]{2,1,0:T(8,128)(2,1)}, u32[]{:S(2)}, u32[]{:S(2)}) collective-permute-start(bf16[1,288,128]{2,1,0:T(8,128)(2,1)S(1)} %bitcast.252), channel_id=1, source_target_pairs={{0,2},{1,3},{2,4},{3,5},{4,6},{5,7},{6,8},{7,9},{8,10},{9,11},{10,... | collective-permute-start | bytes 221192 | tf_op jit(solution)/shard_map/ppermute | solution.py:22
  98.8 47.2 %collective-permute-start.8 = (bf16[1,288,128]{2,1,0:T(8,128)(2,1)S(1)}, bf16[1,288,128]{2,1,0:T(8,128)(2,1)S(1)}, u32[]{:S(2)}, u32[]{:S(2)}) collective-permute-start(bf16[1,288,128]{2,1,0:T(8,128)(2,1)S(1)} %bitcast.249), channel_id=1, source_target_pairs={{3,0},{4,1},{5,2},{6,3},{7,4},{8,5},{9,6},{10,7},{11,8},{12,9},{13... | collective-permute-start | bytes 221192 | tf_op jit(solution)/shard_map/ppermute | solution.py:22
  100.1 45.9 %collective-permute-start.9 = (bf16[1,288,128]{2,1,0:T(8,128)(2,1)S(1)}, bf16[1,288,128]{2,1,0:T(8,128)(2,1)S(1)}, u32[]{:S(2)}, u32[]{:S(2)}) collective-permute-start(bf16[1,288,128]{2,1,0:T(8,128)(2,1)S(1)} %bitcast.250), channel_id=1, source_target_pairs={{2,0},{3,1},{4,2},{5,3},{6,4},{7,5},{8,6},{9,7},{10,8},{11,9},{12,... | collective-permute-start | bytes 221192 | tf_op jit(solution)/shard_map/ppermute | solution.py:22
  103.9 22.3 %all-to-all-start = ((f32[16,68,128]{2,1,0:T(8,128)}), f32[16,68,128]{2,1,0:T(8,128)S(1)}, u32[]{:S(2)}, u32[]{:S(2)}) async-start(f32[16,68,128]{2,1,0:T(8,128)} %reshape.626), calls=%async_computation | async-start | bytes 1179648 | tf_op jit(solution)/shard_map/all_to_all | solution.py:75
  114.3 8.3 %collective-permute-start.7 = (bf16[1,288,128]{2,1,0:T(8,128)(2,1)S(1)}, bf16[1,288,128]{2,1,0:T(8,128)(2,1)S(1)}, u32[]{:S(2)}, u32[]{:S(2)}) collective-permute-start(bf16[1,288,128]{2,1,0:T(8,128)(2,1)S(1)} %get-tuple-element.104), channel_id=1, source_target_pairs={{0,1},{1,2},{2,3},{3,4},{4,5},{5,6},{6,7},{7,8},{8,9},{9,10},{10,1... | collective-permute-start | bytes 221192 | tf_op jit(solution)/shard_map/ppermute | solution.py:22
  122.7 23.4 %collective-permute-start.6 = (bf16[1,288,128]{2,1,0:T(8,128)(2,1)S(1)}, bf16[1,288,128]{2,1,0:T(8,128)(2,1)S(1)}, u32[]{:S(2)}, u32[]{:S(2)}) collective-permute-start(bf16[1,288,128]{2,1,0:T(8,128)(2,1)S(1)} %get-tuple-element.105), channel_id=1, source_target_pairs={{1,0},{2,1},{3,2},{4,3},{5,4},{6,5},{7,6},{8,7},{9,8},{10,9},{11,1... | collective-permute-start | bytes 221192 | tf_op jit(solution)/shard_map/ppermute | solution.py:22
  124.9 38.1 %copy-start.2 = (bf16[1,48,48,128]{3,2,1,0:T(8,128)(2,1)S(1)}, bf16[1,48,48,128]{3,2,1,0:T(8,128)(2,1)}, u32[]{:S(2)}) copy-start(bf16[1,48,48,128]{3,2,1,0:T(8,128)(2,1)} %copy-done.1) | copy-start | bytes 1769476
  127.0 31.4 %all-to-all-start.1 = ((f32[32,1,272]{2,1,0:T(1,128)}), f32[32,1,272]{2,1,0:T(1,128)S(1)}, u32[]{:S(2)}, u32[]{:S(2)}) async-start(f32[32,1,272]{2,1,0:T(1,128)} %all_to_all.17), calls=%async_computation.1 | async-start | bytes 98304 | tf_op jit(solution)/shard_map/all_to_all | solution.py:77
  159.1 16.4 %all-to-all-start.2 = ((f32[32,1,272]{2,1,0:T(1,128)}), f32[32,1,272]{2,1,0:T(1,128)S(1)}, u32[]{:S(2)}, u32[]{:S(2)}) async-start(f32[32,1,272]{2,1,0:T(1,128)} %broadcast_in_dim.10), calls=%async_computation.2 | async-start | bytes 98304 | tf_op jit(solution)/shard_map/all_to_all | solution.py:79
  163.6 23.4 %copy-start.8 = (bf16[1,1,48,48,128]{4,3,2,1,0:T(8,128)(2,1)S(1)}, bf16[1,1,48,48,128]{4,3,2,1,0:T(8,128)(2,1)}, u32[]{:S(2)}) copy-start(bf16[1,1,48,48,128]{4,3,2,1,0:T(8,128)(2,1)} %param.11) | copy-start | bytes 1769476
  163.6 23.4 %copy-start.19 = (f32[128]{0:T(128)S(1)}, f32[128]{0:T(128)}, u32[]{:S(2)}) copy-start(f32[128]{0:T(128)} %copy-done.18) | copy-start | bytes 1540
  163.6 23.4 %copy-start.21 = (f32[128]{0:T(128)S(1)}, f32[128]{0:T(128)}, u32[]{:S(2)}) copy-start(f32[128]{0:T(128)} %copy-done.20) | copy-start | bytes 1540
  163.6 23.4 %copy-start.23 = (f32[128]{0:T(128)S(1)}, f32[128]{0:T(128)}, u32[]{:S(2)}) copy-start(f32[128]{0:T(128)} %copy-done.22) | copy-start | bytes 1540
  163.6 23.4 %copy-start.25 = (f32[128]{0:T(128)S(1)}, f32[128]{0:T(128)}, u32[]{:S(2)}) copy-start(f32[128]{0:T(128)} %copy-done.24) | copy-start | bytes 1540
  163.6 23.4 %copy-start.27 = (f32[128]{0:T(128)S(1)}, f32[128]{0:T(128)}, u32[]{:S(2)}) copy-start(f32[128]{0:T(128)} %copy-done.26) | copy-start | bytes 1540
  163.6 23.4 %copy-start.29 = (f32[128]{0:T(128)S(1)}, f32[128]{0:T(128)}, u32[]{:S(2)}) copy-start(f32[128]{0:T(128)} %copy-done.28) | copy-start | bytes 1540
  163.6 23.4 %copy-start.31 = (f32[128]{0:T(128)S(1)}, f32[128]{0:T(128)}, u32[]{:S(2)}) copy-start(f32[128]{0:T(128)} %copy-done.30) | copy-start | bytes 1540
  163.7 23.4 %copy-start.33 = (f32[128]{0:T(128)S(1)}, f32[128]{0:T(128)}, u32[]{:S(2)}) copy-start(f32[128]{0:T(128)} %copy-done.32) | copy-start | bytes 1540
  163.7 23.4 %copy-start.35 = (f32[128]{0:T(128)S(1)}, f32[128]{0:T(128)}, u32[]{:S(2)}) copy-start(f32[128]{0:T(128)} %copy-done.34) | copy-start | bytes 1540
  163.7 23.4 %copy-start.37 = (f32[128]{0:T(128)S(1)}, f32[128]{0:T(128)}, u32[]{:S(2)}) copy-start(f32[128]{0:T(128)} %copy-done.36) | copy-start | bytes 1540
  163.7 23.4 %copy-start.39 = (f32[128]{0:T(128)S(1)}, f32[128]{0:T(128)}, u32[]{:S(2)}) copy-start(f32[128]{0:T(128)} %copy-done.38) | copy-start | bytes 1540
  163.7 23.4 %copy-start.41 = (f32[128]{0:T(128)S(1)}, f32[128]{0:T(128)}, u32[]{:S(2)}) copy-start(f32[128]{0:T(128)} %copy-done.40) | copy-start | bytes 1540
  163.7 23.4 %copy-start.43 = (f32[128]{0:T(128)S(1)}, f32[128]{0:T(128)}, u32[]{:S(2)}) copy-start(f32[128]{0:T(128)} %copy-done.42) | copy-start | bytes 1540
  163.7 23.4 %copy-start.45 = (f32[128]{0:T(128)S(1)}, f32[128]{0:T(128)}, u32[]{:S(2)}) copy-start(f32[128]{0:T(128)} %copy-done.44) | copy-start | bytes 1540
  163.7 23.4 %copy-start.47 = (f32[128]{0:T(128)S(1)}, f32[128]{0:T(128)}, u32[]{:S(2)}) copy-start(f32[128]{0:T(128)} %copy-done.46) | copy-start | bytes 1540
  163.7 23.4 %copy-start.49 = (f32[128]{0:T(128)S(1)}, f32[128]{0:T(128)}, u32[]{:S(2)}) copy-start(f32[128]{0:T(128)} %copy-done.48) | copy-start | bytes 1540
  163.7 23.4 %copy-start.51 = (f32[128]{0:T(128)S(1)}, f32[128]{0:T(128)}, u32[]{:S(2)}) copy-start(f32[128]{0:T(128)} %copy-done.50) | copy-start | bytes 1540
  163.8 23.4 %copy-start.53 = (f32[128]{0:T(128)S(1)}, f32[128]{0:T(128)}, u32[]{:S(2)}) copy-start(f32[128]{0:T(128)} %copy-done.52) | copy-start | bytes 1540
  163.8 23.4 %copy-start.55 = (f32[128]{0:T(128)S(1)}, f32[128]{0:T(128)}, u32[]{:S(2)}) copy-start(f32[128]{0:T(128)} %copy-done.54) | copy-start | bytes 1540
  163.8 23.4 %copy-start.57 = (f32[128]{0:T(128)S(1)}, f32[128]{0:T(128)}, u32[]{:S(2)}) copy-start(f32[128]{0:T(128)} %copy-done.56) | copy-start | bytes 1540
  163.8 23.4 %copy-start.59 = (f32[128]{0:T(128)S(1)}, f32[128]{0:T(128)}, u32[]{:S(2)}) copy-start(f32[128]{0:T(128)} %copy-done.58) | copy-start | bytes 1540
  163.8 23.4 %copy-start.61 = (f32[128]{0:T(128)S(1)}, f32[128]{0:T(128)}, u32[]{:S(2)}) copy-start(f32[128]{0:T(128)} %copy-done.60) | copy-start | bytes 1540
  163.8 23.4 %copy-start.63 = (f32[128]{0:T(128)S(1)}, f32[128]{0:T(128)}, u32[]{:S(2)}) copy-start(f32[128]{0:T(128)} %copy-done.62) | copy-start | bytes 1540
  163.8 23.4 %copy-start.65 = (f32[128]{0:T(128)S(1)}, f32[128]{0:T(128)}, u32[]{:S(2)}) copy-start(f32[128]{0:T(128)} %copy-done.64) | copy-start | bytes 1540
  163.8 23.4 %copy-start.67 = (f32[128]{0:T(128)S(1)}, f32[128]{0:T(128)}, u32[]{:S(2)}) copy-start(f32[128]{0:T(128)} %copy-done.66) | copy-start | bytes 1540
  163.8 23.4 %copy-start.69 = (f32[128]{0:T(128)S(1)}, f32[128]{0:T(128)}, u32[]{:S(2)}) copy-start(f32[128]{0:T(128)} %copy-done.68) | copy-start | bytes 1540
  163.8 23.4 %copy-start.71 = (f32[128]{0:T(128)S(1)}, f32[128]{0:T(128)}, u32[]{:S(2)}) copy-start(f32[128]{0:T(128)} %copy-done.70) | copy-start | bytes 1540
  163.9 23.4 %copy-start.73 = (f32[128]{0:T(128)S(1)}, f32[128]{0:T(128)}, u32[]{:S(2)}) copy-start(f32[128]{0:T(128)} %copy-done.72) | copy-start | bytes 1540
  163.9 23.4 %copy-start.75 = (f32[128]{0:T(128)S(1)}, f32[128]{0:T(128)}, u32[]{:S(2)}) copy-start(f32[128]{0:T(128)} %copy-done.74) | copy-start | bytes 1540
  163.9 23.4 %copy-start.77 = (f32[128]{0:T(128)S(1)}, f32[128]{0:T(128)}, u32[]{:S(2)}) copy-start(f32[128]{0:T(128)} %copy-done.76) | copy-start | bytes 1540
  163.9 23.4 %copy-start.79 = (f32[128]{0:T(128)S(1)}, f32[128]{0:T(128)}, u32[]{:S(2)}) copy-start(f32[128]{0:T(128)} %copy-done.78) | copy-start | bytes 1540
  163.9 23.4 %copy-start.81 = (f32[128]{0:T(128)S(1)}, f32[128]{0:T(128)}, u32[]{:S(2)}) copy-start(f32[128]{0:T(128)} %copy-done.80) | copy-start | bytes 1540
  163.9 23.4 %copy-start.83 = (f32[128]{0:T(128)S(1)}, f32[128]{0:T(128)}, u32[]{:S(2)}) copy-start(f32[128]{0:T(128)} %copy-done.82) | copy-start | bytes 1540
  163.9 23.4 %copy-start.85 = (f32[128]{0:T(128)S(1)}, f32[128]{0:T(128)}, u32[]{:S(2)}) copy-start(f32[128]{0:T(128)} %copy-done.84) | copy-start | bytes 1540
  163.9 23.4 %copy-start.87 = (f32[128]{0:T(128)S(1)}, f32[128]{0:T(128)}, u32[]{:S(2)}) copy-start(f32[128]{0:T(128)} %copy-done.86) | copy-start | bytes 1540
  163.9 23.4 %copy-start.89 = (f32[128]{0:T(128)S(1)}, f32[128]{0:T(128)}, u32[]{:S(2)}) copy-start(f32[128]{0:T(128)} %copy-done.88) | copy-start | bytes 1540
  163.9 23.4 %copy-start.91 = (f32[128]{0:T(128)S(1)}, f32[128]{0:T(128)}, u32[]{:S(2)}) copy-start(f32[128]{0:T(128)} %copy-done.90) | copy-start | bytes 1540
  164.0 23.4 %copy-start.93 = (f32[128]{0:T(128)S(1)}, f32[128]{0:T(128)}, u32[]{:S(2)}) copy-start(f32[128]{0:T(128)} %copy-done.92) | copy-start | bytes 1540
  176.6 22.5 %all-to-all-start.3 = ((f32[16,68,128]{2,1,0:T(8,128)}), f32[16,68,128]{2,1,0:T(8,128)}, u32[]{:S(2)}, u32[]{:S(2)}) async-start(f32[16,68,128]{2,1,0:T(8,128)} %broadcast_in_dim.11), calls=%async_computation.3 | async-start | bytes 1179648 | tf_op jit(solution)/shard_map/all_to_all | solution.py:81
  (67 other events, 953.5 us)

commit v2 on v0

v2 whole, which is shorter than its diff:
```python
import math

import jax
import jax.numpy as jnp
from jax import lax
from jax.experimental import pallas as pl
from jax.experimental.pallas import tpu as pltpu
from jax.sharding import PartitionSpec as P

KERNEL = 7
DILATION = 2
HALO = 6
TAPS = KERNEL * KERNEL
TILE = 48
LANES = 128
PAD = 2
EXT_ROWS = TILE + 2 * HALO
EXT_COLS = 64
CHUNK = 8
CELLS_IN_CHUNK = CHUNK * TILE
GROUPS = TILE // 8
STEPS = (-3, -2, -1, 1, 2, 3)

norm_eps = 1e-06
inv_sqrt_two_pi = 0.3989422804014327
TAIL_RATE = 0.3889087296526013
TAIL_TERMS = (
    0.15079174476614957,
    0.19542085643011212,
    -0.02071252121020706,
    0.379856419408137,
    -0.25901857729927547,
    0.05366208632016299,
)

f32 = jnp.float32
bf16 = jnp.bfloat16
VMEM = pl.BlockSpec(memory_space=pltpu.VMEM)
SMEM = pl.BlockSpec(memory_space=pltpu.SMEM)


def pack_strips(flat, beside, where, top, bottom, to_before, to_after):
    position = where[0]
    upper = flat[0 : HALO * TILE, :].astype(bf16).reshape(HALO, TILE, LANES)
    lower = flat[(TILE - HALO) * TILE :, :].astype(bf16).reshape(HALO, TILE, LANES)
    top[...] = upper
    bottom[...] = lower
    to_before[...] = upper
    to_after[...] = lower

    def columns(out, first):
        for c in range(HALO):
            parts = [
                flat[pl.ds(8 * g * TILE + first + c, 8, stride=TILE), :] for g in range(GROUPS)
            ]
            out[c] = jnp.concatenate(parts, axis=0).astype(bf16)

    for out, step in ((to_before, -1), (to_after, 1)):
        for direction, first in ((2, 0), (3, TILE - HALO)):
            source = beside[direction]

            @pl.when((source >= 0) & (source - position == step))
            def _(out=out, first=first):
                columns(out, first)


def place_rims(ext, ext_flat, beside, where, strips):
    position = where[0]
    zero_rows = jnp.zeros((HALO, EXT_COLS, LANES), f32)
    zero_cols = jnp.zeros((TILE, 8, LANES), f32)
    ext[0:HALO] = zero_rows
    ext[HALO + TILE :] = zero_rows
    ext[HALO : HALO + TILE, 0:8, :] = zero_cols
    ext[HALO : HALO + TILE, 8 + TILE :, :] = zero_cols
    last = TILE - 8

    def put_rows(first):
        def put(strip):
            ext[first : first + HALO, 8 : 8 + TILE, :] = strip.astype(f32)

        return put

    def put_corner(first, east):
        def put(strip):
            wide = strip.astype(f32)
            if east:
                ext[first : first + HALO, 8 + TILE :, :] = wide[:, 0:8]
            else:
                ext[first : first + HALO, 0:8, :] = wide[:, last:]

        return put

    def put_columns(first):
        def put(strip):
            wide = strip.astype(f32)
            for c in range(HALO):
                for g in range(GROUPS):
                    at = (HALO + 8 * g) * EXT_COLS + first + c
                    ext_flat[pl.ds(at, 8, stride=EXT_COLS), :] = wide[c, 8 * g : 8 * g + 8]

        return put

    south_row = HALO + TILE
    before, after = (-1, -2, -3), (1, 2, 3)
    for direction, steps, put in (
        (4, before, put_corner(0, False)),
        (5, before, put_corner(0, True)),
        (6, after, put_corner(south_row, False)),
        (7, after, put_corner(south_row, True)),
        (0, before, put_rows(0)),
        (1, after, put_rows(south_row)),
        (2, (-1, 1), put_columns(PAD)),
        (3, (-1, 1), put_columns(8 + TILE)),
    ):
        source = beside[direction]
        for step in steps:

            @pl.when((source >= 0) & (source - position == step))
            def _(step=step, put=put):
                put(strips[STEPS.index(step)][...])


def conv_group(ext, weights, first_row, g):
    sums = [None] * CHUNK
    for b in range(KERNEL):
        taps = [
            jnp.broadcast_to(weights[a * KERNEL + b : a * KERNEL + b + 1, :], (8, LANES))
            for a in range(KERNEL)
        ]
        column = PAD + 8 * g + DILATION * b
        for i in range(CHUNK + 2 * HALO):
            window = ext[first_row + i, pl.ds(column, 8), :]
            for a in range(KERNEL):
                row = i - DILATION * a
                if 0 <= row < CHUNK:
                    term = taps[a] * window
                    sums[row] = term if sums[row] is None else sums[row] + term
    return sums


def pack_kernel(beside, where, fields, mask, top, bottom, to_before, to_after, flat):
    def rows(i, _):
        cells = pl.ds(pl.multiple_of(i * TILE, TILE), TILE)
        flat[cells, :] = fields[i].astype(f32) * mask[i].astype(f32)
        return 0

    lax.fori_loop(0, TILE, rows, 0, unroll=4)
    pack_strips(flat, beside, where, top, bottom, to_before, to_after)


def block_kernel(
    beside,
    where,
    fields,
    cotangent,
    mask,
    s0,
    s1,
    s2,
    s3,
    s4,
    s5,
    weights,
    gain,
    up_weight,
    up_bias,
    down_weight,
    scale,
    block_out,
    conv_grad,
    top,
    bottom,
    to_before,
    to_after,
    sums,
    ext,
    grad_flat,
    standard,
    inv_std,
    normed,
    branch_grad,
    hidden,
    active_grad,
    active,
    hidden_grad,
    up_sum,
    down_sum,
    bias_sum,
    tap_sums,
    row_sums,
):
    ext_flat = ext.reshape(EXT_ROWS * EXT_COLS, LANES)

    def centre(i, _):
        ext[HALO + i, pl.ds(8, TILE), :] = fields[i].astype(f32) * mask[i].astype(f32)
        return 0

    lax.fori_loop(0, TILE, centre, 0, unroll=4)
    place_rims(ext, ext_flat, beside, where, (s0, s1, s2, s3, s4, s5))
    up_sum[...] = jnp.zeros_like(up_sum)
    down_sum[...] = jnp.zeros_like(down_sum)
    bias_sum[...] = jnp.zeros_like(bias_sum)
    tap_sums[...] = jnp.zeros_like(tap_sums)
    row_sums[...] = jnp.zeros_like(row_sums)
    ones = jnp.ones((8, CELLS_IN_CHUNK), bf16)

    def chunk(step, _):
        first = pl.multiple_of(step * CHUNK, CHUNK)
        for g in range(GROUPS):
            values = conv_group(ext, weights, first, g)
            for row in range(CHUNK):
                standard[pl.ds(row * TILE + 8 * g, 8), :] = values[row]

        def normalise(row, _):
            cells = pl.ds(pl.multiple_of(row * TILE, TILE), TILE)
            conv = standard[cells, :]
            centered = conv - jnp.mean(conv, axis=-1, keepdims=True)
            inv = lax.rsqrt(jnp.mean(centered * centered, axis=-1, keepdims=True) + norm_eps)
            unit = centered * inv
            standard[cells, :] = unit
            inv_std[cells, :] = jnp.broadcast_to(inv, (TILE, LANES))
            normed[cells, :] = (unit * gain[...]).astype(bf16)
            weighted = mask[first + row].astype(f32) * scale[...]
            branch_grad[cells, :] = (weighted * cotangent[first + row].astype(f32)).astype(bf16)
            return 0

        lax.fori_loop(0, CHUNK, normalise, 0, unroll=2)
        hidden[...] = jnp.dot(normed[...], up_weight[...], preferred_element_type=f32)
        active_grad[...] = lax.dot_general(
            branch_grad[...],
            down_weight[...],
            (((1,), (1,)), ((), ())),
            preferred_element_type=f32,
        )

        def activate(i, _):
            cells = pl.ds(pl.multiple_of(i * 16, 16), 16)
            h = hidden[cells, :] + up_bias[...]
            t = pl.reciprocal(1.0 + TAIL_RATE * jnp.abs(h), approx=False)
            tail = TAIL_TERMS[-1] * t + TAIL_TERMS[-2]
            for term in TAIL_TERMS[-3::-1]:
                tail = tail * t + term
            bell = jnp.exp(-0.5 * h * h)
            tail = tail * t * bell
            phi = jnp.where(h >= 0, 1.0 - tail, tail)
            active[cells, :] = (h * phi).astype(bf16)
            slope = phi + h * (bell * inv_sqrt_two_pi)
            hidden_grad[cells, :] = (active_grad[cells, :] * slope).astype(bf16)
            return 0

        lax.fori_loop(0, CELLS_IN_CHUNK // 16, activate, 0, unroll=2)
        hidden[:, 0:LANES] = jnp.dot(active[...], down_weight[...], preferred_element_type=f32)
        active_grad[:, 0:LANES] = lax.dot_general(
            hidden_grad[...], up_weight[...], (((1,), (1,)), ((), ())), preferred_element_type=f32
        )
        over_cells = (((0,), (0,)), ((), ()))
        down_sum[...] += lax.dot_general(
            branch_grad[...], active[...], over_cells, preferred_element_type=f32
        )
        up_sum[...] += lax.dot_general(
            normed[...], hidden_grad[...], over_cells, preferred_element_type=f32
        )
        bias_sum[...] += jnp.dot(ones, hidden_grad[...], preferred_element_type=f32)

        def finish(row, _):
            cells = pl.ds(pl.multiple_of(row * TILE, TILE), TILE)
            at = first + row
            masked_branch = mask[at].astype(f32) * hidden[cells, 0:LANES]
            block_out[at] = (fields[at].astype(f32) + masked_branch * scale[...]).astype(bf16)
            by_scale = masked_branch * cotangent[at].astype(f32)
            unit = standard[cells, :]
            grad = active_grad[cells, 0:LANES]
            by_gain = grad * unit
            u = grad * gain[...]
            mean_u = jnp.mean(u, axis=-1, keepdims=True)
            mean_us = jnp.mean(u * unit, axis=-1, keepdims=True)
            out = (inv_std[cells, :] * (u - mean_u - unit * mean_us)).astype(bf16)
            conv_grad[at] = out
            grad_flat[pl.ds(pl.multiple_of(at * TILE, TILE), TILE), :] = out.astype(f32)
            for k in range(GROUPS):
                row_sums[0:8, :] += by_scale[8 * k : 8 * k + 8]
                row_sums[8:16, :] += by_gain[8 * k : 8 * k + 8]
            return 0

        lax.fori_loop(0, CHUNK, finish, 0, unroll=2)
        for b in range(KERNEL):
            totals = [tap_sums[a * KERNEL + b] for a in range(KERNEL)]
            for g in range(GROUPS):
                grads = [
                    grad_flat[pl.ds((first + row) * TILE + 8 * g, 8), :] for row in range(CHUNK)
                ]
                column = PAD + 8 * g + DILATION * b
                for i in range(CHUNK + 2 * HALO):
                    window = ext[first + i, pl.ds(column, 8), :]
                    for a in range(KERNEL):
                        row = i - DILATION * a
                        if 0 <= row < CHUNK:
                            totals[a] = totals[a] + grads[row] * window
            for a in range(KERNEL):
                tap_sums[a * KERNEL + b] = totals[a]
        return 0

    lax.fori_loop(0, TILE // CHUNK, chunk, 0)
    pack_strips(grad_flat, beside, where, top, bottom, to_before, to_after)

    quarters = up_sum.shape[1] // LANES
    for q in range(quarters):
        lanes = slice(q * LANES, (q + 1) * LANES)
        sums[q * LANES : (q + 1) * LANES, :] = up_sum[:, lanes]
        sums[(quarters + q) * LANES : (quarters + q + 1) * LANES, :] = down_sum[:, lanes]
    at = 2 * quarters * LANES
    sums[at:, :] = jnp.zeros((sums.shape[0] - at, LANES), f32)
    sums[at : at + TAPS, :] = jnp.sum(tap_sums[...], axis=1)
    sums[at + TAPS : at + TAPS + 1, :] = jnp.sum(row_sums[0:8, :], axis=0, keepdims=True)
    sums[at + TAPS + 1 : at + TAPS + 2, :] = jnp.sum(row_sums[8:16, :], axis=0, keepdims=True)
    for q in range(quarters):
        row = at + TAPS + 2 + q
        sums[row : row + 1, :] = bias_sum[0:1, q * LANES : (q + 1) * LANES]


def back_kernel(
    beside, where, conv_grad, cotangent, mask, s0, s1, s2, s3, s4, s5, weights, fields_grad, ext
):
    ext_flat = ext.reshape(EXT_ROWS * EXT_COLS, LANES)

    def centre(i, _):
        ext[HALO + i, pl.ds(8, TILE), :] = conv_grad[i].astype(f32)
        return 0

    lax.fori_loop(0, TILE, centre, 0, unroll=4)
    place_rims(ext, ext_flat, beside, where, (s0, s1, s2, s3, s4, s5))

    def chunk(step, _):
        first = pl.multiple_of(step * CHUNK, CHUNK)
        columns = [conv_group(ext, weights, first, g) for g in range(GROUPS)]
        for row in range(CHUNK):
            at = first + row
            whole = jnp.concatenate([columns[g][row] for g in range(GROUPS)], axis=0)
            out = cotangent[at].astype(f32) + mask[at].astype(f32) * whole
            fields_grad[at] = out.astype(bf16)
        return 0

    lax.fori_loop(0, TILE // CHUNK, chunk, 0)


def shape(dims, dtype=bf16):
    return jax.ShapeDtypeStruct(dims, dtype)


STRIP = (HALO, TILE, LANES)
WHOLE = (TILE, TILE, LANES)


def call(kernel, scalars, operands, outs, scratch, flops, limit):
    size = sum(math.prod(a.shape) * a.dtype.itemsize for a in (*operands, *outs))
    return pl.pallas_call(
        kernel,
        out_shape=outs,
        in_specs=[SMEM] * len(scalars) + [VMEM] * len(operands),
        out_specs=[VMEM] * len(outs),
        scratch_shapes=scratch,
        compiler_params=pltpu.CompilerParams(vmem_limit_bytes=limit * 2**20),
        cost_estimate=pl.CostEstimate(flops=flops, bytes_accessed=size, transcendentals=0),
    )(*scalars, *operands)


def shifted(value, step):
    count = lax.axis_size("space")
    first, last = (max(0, -step), min(count, count - step))
    return lax.ppermute(value, "space", [(source, source + step) for source in range(first, last)])


def exchange(top, bottom, to_before, to_after):
    sent = {3: bottom, 2: bottom, 1: to_after, -1: to_before, -2: top, -3: top}
    return [shifted(sent[-step], -step) for step in STEPS]


def summed_everywhere(flat, factor):
    rows, lanes = flat.shape
    dp, space = lax.axis_size("dp"), lax.axis_size("space")
    part = lax.all_to_all(flat.reshape(dp, rows // dp, lanes), "dp", 0, 0, tiled=True)
    part = jnp.sum(part, axis=0).reshape(space, -1)
    part = jnp.sum(lax.all_to_all(part, "space", 0, 0, tiled=True), axis=0) * factor
    part = jnp.broadcast_to(part, (space,) + part.shape)
    part = lax.all_to_all(part, "space", 0, 0, tiled=True).reshape(rows // dp, lanes)
    part = jnp.broadcast_to(part, (dp,) + part.shape)
    return lax.all_to_all(part, "dp", 0, 0, tiled=True).reshape(rows, lanes)


def local(
    fields,
    cotangent,
    land_mask,
    neighbours,
    conv_kernel,
    norm_gain,
    up_weight,
    up_bias,
    down_weight,
    layer_scale,
):
    beside = neighbours[0]
    where = lax.axis_index("space").astype(jnp.int32)[None]
    tile, upstream = fields[0, 0], cotangent[0, 0]
    mask = jnp.broadcast_to(land_mask[0].astype(bf16)[..., None], WHOLE)
    taps = conv_kernel.reshape(TAPS, LANES)
    units = up_weight.shape[1]
    quarters = units // LANES
    sum_rows = -(-(2 * units + TAPS + 2 + quarters) // 64) * 64

    rims = call(
        pack_kernel,
        (beside, where),
        (tile, mask),
        [shape(STRIP)] * 4,
        [pltpu.VMEM((TILE * TILE, LANES), f32)],
        TILE * TILE * LANES,
        32,
    )
    strips = exchange(*rims)
    block_out, conv_grad, *rims, sums = call(
        block_kernel,
        (beside, where),
        (
            tile,
            upstream,
            mask,
            *strips,
            taps,
            norm_gain[None],
            up_weight,
            up_bias[None],
            down_weight,
            layer_scale[None],
        ),
        [shape(WHOLE), shape(WHOLE)] + [shape(STRIP)] * 4 + [shape((sum_rows, LANES), f32)],
        [
            pltpu.VMEM((EXT_ROWS, EXT_COLS, LANES), f32),
            pltpu.VMEM((TILE * TILE, LANES), f32),
            pltpu.VMEM((CELLS_IN_CHUNK, LANES), f32),
            pltpu.VMEM((CELLS_IN_CHUNK, LANES), f32),
            pltpu.VMEM((CELLS_IN_CHUNK, LANES), bf16),
            pltpu.VMEM((CELLS_IN_CHUNK, LANES), bf16),
            pltpu.VMEM((CELLS_IN_CHUNK, units), f32),
            pltpu.VMEM((CELLS_IN_CHUNK, units), f32),
            pltpu.VMEM((CELLS_IN_CHUNK, units), bf16),
            pltpu.VMEM((CELLS_IN_CHUNK, units), bf16),
            pltpu.VMEM((LANES, units), f32),
            pltpu.VMEM((LANES, units), f32),
            pltpu.VMEM((8, units), f32),
            pltpu.VMEM((TAPS, 8, LANES), f32),
            pltpu.VMEM((16, LANES), f32),
        ],
        12 * TILE * TILE * LANES * units,
        40,
    )
    strips = exchange(*rims)
    cells = TILE * TILE * lax.axis_size("dp") * lax.axis_size("space")
    total = summed_everywhere(sums, 1.0 / math.sqrt(cells))
    (fields_grad,) = call(
        back_kernel,
        (beside, where),
        (conv_grad, upstream, mask, *strips, taps[::-1]),
        [shape(WHOLE)],
        [pltpu.VMEM((EXT_ROWS, EXT_COLS, LANES), f32)],
        2 * TAPS * TILE * TILE * LANES,
        32,
    )
    up_grad = total[:units].reshape(quarters, LANES, LANES).transpose(1, 0, 2).reshape(LANES, units)
    down_grad = total[units : 2 * units].reshape(quarters, LANES, LANES).transpose(0, 2, 1)
    at = 2 * units
    return (
        block_out[None, None],
        fields_grad[None, None],
        total[at : at + TAPS].reshape(KERNEL, KERNEL, LANES),
        total[at + TAPS + 1],
        up_grad,
        total[at + TAPS + 2 : at + TAPS + 2 + quarters].reshape(units),
        down_grad.reshape(units, LANES),
        total[at + TAPS],
    )


def solution(mesh):
    tiles = P("dp", "space", None, None, None)
    return jax.shard_map(
        local,
        mesh=mesh,
        in_specs=(
            tiles,
            tiles,
            P("space", None, None),
            P("space", None),
            P(),
            P(),
            P(),
            P(),
            P(),
            P(),
        ),
        out_specs=(tiles, tiles, P(), P(), P(), P(), P(), P()),
        check_vma=False,
    )
```

time: 787 us -> 169 us (0.21)
  the two profiles are of different devices: /device:TPU:1 before, /device:TPU:6 now
where the time goes in v2:
time: 169 us; the launch traced here: 168 us
  blocking collectives  62.2 us (37%)
  Pallas kernels  39.6 us (23%)
  starting transfers between devices  37.5 us (22%)
  local copies, waits for them, and re-layouts  15 us (9%)
  waiting for transfers between devices  11.8 us (7%)
    pallas_call x3, Pallas kernels, call(): pl.pallas_call(kernel, out_shape=outs, in_specs=[SMEM] * len(scalars) + [...  39.6 us
    ppermute x12, starting transfers between devices, shifted(): lax.ppermute(value, 'space', [(source, source + step) for source in range...  31.2 us
    all_to_all x1, blocking collectives, summed_everywhere(): lax.all_to_all(part, 'space', 0, 0, tiled=True)  28.2 us
    all_to_all x1, blocking collectives, summed_everywhere(): lax.all_to_all(flat.reshape(dp, rows // dp, lanes), 'dp', 0, 0, tiled=True)  17.5 us
    all_to_all x1, blocking collectives, summed_everywhere(): lax.all_to_all(part, 'space', 0, 0, tiled=True).reshape(rows // dp, lanes)  16.4 us
    ppermute x12, waiting for transfers between devices, shifted(): lax.ppermute(value, 'space', [(source, source + step) for source in range...  11.8 us
    unnamed x42, local copies, waits for them, and re-layouts  10.1 us
    all_to_all x1, starting transfers between devices, summed_everywhere(): return lax.all_to_all(part, 'dp', 0, 0, tiled=True).reshape(rows, lanes)  6.33 us
  transfers between devices with their start and end apart: 13, of which 4 were waited for; matrix products, arithmetic and copies ran while one was open for 0% of the time, Pallas kernels for 5%

profile of v2, /device:TPU:6, one launch (start us, length us, event | category | flops | bytes accessed | tf_op | source)
XLA Modules:
  0.0 167.9 jit_solution(3965276442220110961)
XLA Ops:
  0.6 0.0 copy-start.1
  0.6 0.8 convert_bitcast_fusion
  1.5 0.4 broadcast_in_dim.31.mask
  1.8 0.0 copy-done.1
  1.8 0.3 copy-done.2
  2.2 0.8 shard_map.161
  3.0 4.0 %collective-permute-start.2 = (bf16[6,48,128]{2,1,0:T(8,128)(2,1)S(1)}, bf16[6,48,128]{2,1,0:T(8,128)(2,1)S(1)}, u32[]{:S(2)}, u32[]{:S(2)}) collective-permute-start(bf16[6,48,128]{2,1,0:T(8,128)(2,1)S(1)} %get-tuple-element.20), channel_id=1, source_target_pairs={{0,1},{1,2},{2,3},{3,4},{4,5},{5,6},{6,7},{7,8},{8,9},{9,10},{10,1... | collective-permute-start | bytes 221192 | tf_op jit(solution)/shard_map/ppermute | solution.py:370
  7.0 3.9 %collective-permute-start.1 = (bf16[6,48,128]{2,1,0:T(8,128)(2,1)S(1)}, bf16[6,48,128]{2,1,0:T(8,128)(2,1)S(1)}, u32[]{:S(2)}, u32[]{:S(2)}) collective-permute-start(bf16[6,48,128]{2,1,0:T(8,128)(2,1)S(1)} %get-tuple-element.19), channel_id=1, source_target_pairs={{0,2},{1,3},{2,4},{3,5},{4,6},{5,7},{6,8},{7,9},{8,10},{9,11},{10,... | collective-permute-start | bytes 221192 | tf_op jit(solution)/shard_map/ppermute | solution.py:370
  10.9 4.5 %collective-permute-start = (bf16[6,48,128]{2,1,0:T(8,128)(2,1)S(1)}, bf16[6,48,128]{2,1,0:T(8,128)(2,1)S(1)}, u32[]{:S(2)}, u32[]{:S(2)}) collective-permute-start(bf16[6,48,128]{2,1,0:T(8,128)(2,1)S(1)} %get-tuple-element.19), channel_id=1, source_target_pairs={{0,3},{1,4},{2,5},{3,6},{4,7},{5,8},{6,9},{7,10},{8,11},{9,12},{10... | collective-permute-start | bytes 221192 | tf_op jit(solution)/shard_map/ppermute | solution.py:370
  15.4 2.7 %collective-permute-start.3 = (bf16[6,48,128]{2,1,0:T(8,128)(2,1)S(1)}, bf16[6,48,128]{2,1,0:T(8,128)(2,1)S(1)}, u32[]{:S(2)}, u32[]{:S(2)}) collective-permute-start(bf16[6,48,128]{2,1,0:T(8,128)(2,1)S(1)} %get-tuple-element.21), channel_id=1, source_target_pairs={{1,0},{2,1},{3,2},{4,3},{5,4},{6,5},{7,6},{8,7},{9,8},{10,9},{11,1... | collective-permute-start | bytes 221192 | tf_op jit(solution)/shard_map/ppermute | solution.py:370
  18.1 1.3 collective-permute-start.5
  19.4 0.0 collective-permute-done.2.s2
  19.4 0.0 copy-start.5
  19.4 0.6 copy-done.5
  20.0 1.3 collective-permute-start.4
  21.3 0.0 copy-done.20
  21.3 1.7 collective-permute-done.3.s3
  23.0 0.6 copy-done.11
  23.6 0.0 collective-permute-done.1.s1
  23.6 0.6 copy-done.7
  24.3 0.0 collective-permute-done.s0
  24.3 0.6 copy-done.9
  24.9 3.1 %collective-permute-done.5.s5 = bf16[6,48,128]{2,1,0:T(8,128)(2,1)S(1)} collective-permute-done((bf16[6,48,128]{2,1,0:T(8,128)(2,1)S(1)}, bf16[6,48,128]{2,1,0:T(8,128)(2,1)S(1)}, u32[]{:S(2)}, u32[]{:S(2)}) %collective-permute-start.5) | collective-permute-done | bytes 73760 | tf_op jit(solution)/shard_map/ppermute | solution.py:370
  28.0 0.6 copy-done.13
  28.6 0.0 collective-permute-done.4.s4
  28.6 0.6 copy-done.15
  29.3 0.0 copy-done
  29.3 0.0 copy-done.3
  29.3 0.7 copy-done.17
  30.0 0.9 copy-done.6
  30.8 0.9 copy-done.8
  31.7 0.9 copy-done.10
  32.6 0.9 copy-done.12
  33.5 0.9 copy-done.14
  34.4 0.9 copy-done.16
  35.3 30.5 %shard_map.162 = (bf16[48,48,128]{2,1,0:T(8,128)(2,1)}, bf16[48,48,128]{2,1,0:T(8,128)(2,1)S(1)}, bf16[6,48,128]{2,1,0:T(8,128)(2,1)S(1)}, bf16[6,48,128]{2,1,0:...) custom-call(s32[8]{0:T(128)S(1)} %bitcast.33, ...), custom_call_target="tpu_custom_call" | custom-call | flops 1811939328 | bytes 4533760 | tf_op jit(solution)/shard_map/pallas_call | solution.py:356
  65.8 17.5 %all_to_all.25 = f32[16,68,128]{2,1,0:T(8,128)S(1)} all-to-all(f32[16,68,128]{2,1,0:T(8,128)S(1)} %reshape.62), channel_id=1, replica_groups=mesh['dp'=16,'space'=32] {'dp'}, dimensions={0} | all-to-all | bytes 1114112 | tf_op jit(solution)/shard_map/all_to_all | solution.py:381
  83.4 0.1 all_to_all.17
  83.5 28.2 %all_to_all.26 = f32[32,1,272]{2,1,0:T(1,128)S(1)} all-to-all(f32[32,1,272]{2,1,0:T(1,128)S(1)} %all_to_all.17), channel_id=1, replica_groups=mesh['dp'=16,'space'=32] {'space'}, dimensions={0} | all-to-all | bytes 69632 | tf_op jit(solution)/shard_map/all_to_all | solution.py:383
  111.8 0.1 reduce_sum.19
  111.9 16.4 %all_to_all.27 = f32[32,1,272]{2,1,0:T(1,128)S(1)} all-to-all(f32[32,1,272]{2,1,0:T(1,128)S(1)} %broadcast_in_dim.37), channel_id=1, replica_groups=mesh['dp'=16,'space'=32] {'space'}, dimensions={0} | all-to-all | bytes 69632 | tf_op jit(solution)/shard_map/all_to_all | solution.py:385
  128.3 0.1 reduce.1
  128.4 0.1 reshape.63
  128.5 0.9 broadcast_in_dim.38
  129.4 6.3 %all-to-all-start.3 = ((f32[16,68,128]{2,1,0:T(8,128)}), f32[16,68,128]{2,1,0:T(8,128)S(1)}, u32[]{:S(2)}, u32[]{:S(2)}) async-start(f32[16,68,128]{2,1,0:T(8,128)} %broadcast_in_dim.38), calls=%async_computation.3 | async-start | bytes 1179648 | tf_op jit(solution)/shard_map/all_to_all | solution.py:387
  135.7 2.3 %collective-permute-start.8 = (bf16[6,48,128]{2,1,0:T(8,128)(2,1)S(1)}, bf16[6,48,128]{2,1,0:T(8,128)(2,1)S(1)}, u32[]{:S(2)}, u32[]{:S(2)}) collective-permute-start(bf16[6,48,128]{2,1,0:T(8,128)(2,1)S(1)} %get-tuple-element.26), channel_id=1, source_target_pairs={{0,1},{1,2},{2,3},{3,4},{4,5},{5,6},{6,7},{7,8},{8,9},{9,10},{10,1... | collective-permute-start | bytes 221192 | tf_op jit(solution)/shard_map/ppermute | solution.py:370
  138.1 2.3 %collective-permute-start.7 = (bf16[6,48,128]{2,1,0:T(8,128)(2,1)S(1)}, bf16[6,48,128]{2,1,0:T(8,128)(2,1)S(1)}, u32[]{:S(2)}, u32[]{:S(2)}) collective-permute-start(bf16[6,48,128]{2,1,0:T(8,128)(2,1)S(1)} %get-tuple-element.25), channel_id=1, source_target_pairs={{0,2},{1,3},{2,4},{3,5},{4,6},{5,7},{6,8},{7,9},{8,10},{9,11},{10,... | collective-permute-start | bytes 221192 | tf_op jit(solution)/shard_map/ppermute | solution.py:370
  140.4 3.7 %collective-permute-start.6 = (bf16[6,48,128]{2,1,0:T(8,128)(2,1)S(1)}, bf16[6,48,128]{2,1,0:T(8,128)(2,1)S(1)}, u32[]{:S(2)}, u32[]{:S(2)}) collective-permute-start(bf16[6,48,128]{2,1,0:T(8,128)(2,1)S(1)} %get-tuple-element.25), channel_id=1, source_target_pairs={{0,3},{1,4},{2,5},{3,6},{4,7},{5,8},{6,9},{7,10},{8,11},{9,12},{10... | collective-permute-start | bytes 221192 | tf_op jit(solution)/shard_map/ppermute | solution.py:370
  144.1 2.6 %collective-permute-start.9 = (bf16[6,48,128]{2,1,0:T(8,128)(2,1)S(1)}, bf16[6,48,128]{2,1,0:T(8,128)(2,1)S(1)}, u32[]{:S(2)}, u32[]{:S(2)}) collective-permute-start(bf16[6,48,128]{2,1,0:T(8,128)(2,1)S(1)} %get-tuple-element.27), channel_id=1, source_target_pairs={{1,0},{2,1},{3,2},{4,3},{5,4},{6,5},{7,6},{8,7},{9,8},{10,9},{11,1... | collective-permute-start | bytes 221192 | tf_op jit(solution)/shard_map/ppermute | solution.py:370
  146.7 1.3 collective-permute-start.11
  148.0 0.0 collective-permute-done.8.s2
  148.0 1.3 collective-permute-start.10
  149.4 1.9 %collective-permute-done.9.s3 = bf16[6,48,128]{2,1,0:T(8,128)(2,1)S(1)} collective-permute-done((bf16[6,48,128]{2,1,0:T(8,128)(2,1)S(1)}, bf16[6,48,128]{2,1,0:T(8,128)(2,1)S(1)}, u32[]{:S(2)}, u32[]{:S(2)}) %collective-permute-start.9) | collective-permute-done | bytes 73760 | tf_op jit(solution)/shard_map/ppermute | solution.py:370
  151.3 0.0 collective-permute-done.7.s1
  151.3 0.0 collective-permute-done.6.s0
  151.3 5.1 %collective-permute-done.11.s5 = bf16[6,48,128]{2,1,0:T(8,128)(2,1)S(1)} collective-permute-done((bf16[6,48,128]{2,1,0:T(8,128)(2,1)S(1)}, bf16[6,48,128]{2,1,0:T(8,128)(2,1)S(1)}, u32[]{:S(2)}, u32[]{:S(2)}) %collective-permute-start.11) | collective-permute-done | bytes 73760 | tf_op jit(solution)/shard_map/ppermute | solution.py:370
  156.3 0.0 collective-permute-done.10.s4
  156.4 8.2 %shard_map.163 = bf16[48,48,128]{2,1,0:T(8,128)(2,1)} custom-call(s32[8]{0:T(128)S(1)} %bitcast.34, s32[1]{0:T(128)} %bitcast.1.where, bf16[48,48,128]{2,1,0:T(8,128)(2,1)S(1)} %get-tuple-element.24.conv_grad, bf16[48,48,128]{2,1,0:T(8,128)(2,1)S(1)} %bitcast.29, bf16[48,48,128]{2,1,0:T(8,128)(2,1)S(1)} %broadcast_in_dim.31.mask, ...), custom_call_target="tpu_custom_call" | custom-call | flops 28901376 | bytes 2826752 | tf_op jit(solution)/shard_map/pallas_call | solution.py:356
  164.6 0.0 all-to-all-done.3
  164.6 0.5 slice_bitcast_fusion.1
  165.1 0.6 slice_bitcast_fusion
  165.8 0.8 copy.23
  166.6 0.7 copy.26
  167.3 0.6 reshape.65
  (31 shorter events, 0.2 us)
Async XLA Ops:
  0.6 1.2 copy-start.1
  1.4 0.7 copy-start.2
  2.1 19.2 %copy-start.20 = (f32[7,7,128]{2,1,0:T(8,128)S(1)}, f32[7,7,128]{2,1,0:T(8,128)}, u32[]{:S(2)}) copy-start(f32[7,7,128]{2,1,0:T(8,128)} %param.14) | copy-start | bytes 75268
  2.2 27.1 %copy-start = (bf16[1,1,48,48,128]{4,3,2,1,0:T(8,128)(2,1)S(1)}, bf16[1,1,48,48,128]{4,3,2,1,0:T(8,128)(2,1)}, u32[]{:S(2)}) copy-start(bf16[1,1,48,48,128]{4,3,2,1,0:T(8,128)(2,1)} %param.11) | copy-start | bytes 1769476
  2.2 27.1 %copy-start.3 = (bf16[128,512]{1,0:T(8,128)(2,1)S(1)}, bf16[128,512]{1,0:T(8,128)(2,1)}, u32[]{:S(2)}) copy-start(bf16[128,512]{1,0:T(8,128)(2,1)} %up_weight.1) | copy-start | bytes 393220
  2.2 27.1 %copy-start.4 = (bf16[512,128]{1,0:T(8,128)(2,1)S(1)}, bf16[512,128]{1,0:T(8,128)(2,1)}, u32[]{:S(2)}) copy-start(bf16[512,128]{1,0:T(8,128)(2,1)} %down_weight.1) | copy-start | bytes 393220
  3.0 16.4 %collective-permute-start.2 = (bf16[6,48,128]{2,1,0:T(8,128)(2,1)S(1)}, bf16[6,48,128]{2,1,0:T(8,128)(2,1)S(1)}, u32[]{:S(2)}, u32[]{:S(2)}) collective-permute-start(bf16[6,48,128]{2,1,0:T(8,128)(2,1)S(1)} %get-tuple-element.20), channel_id=1, source_target_pairs={{0,1},{1,2},{2,3},{3,4},{4,5},{5,6},{6,7},{7,8},{8,9},{9,10},{10,1... | collective-permute-start | bytes 221192 | tf_op jit(solution)/shard_map/ppermute | solution.py:370
  7.0 16.6 %collective-permute-start.1 = (bf16[6,48,128]{2,1,0:T(8,128)(2,1)S(1)}, bf16[6,48,128]{2,1,0:T(8,128)(2,1)S(1)}, u32[]{:S(2)}, u32[]{:S(2)}) collective-permute-start(bf16[6,48,128]{2,1,0:T(8,128)(2,1)S(1)} %get-tuple-element.19), channel_id=1, source_target_pairs={{0,2},{1,3},{2,4},{3,5},{4,6},{5,7},{6,8},{7,9},{8,10},{9,11},{10,... | collective-permute-start | bytes 221192 | tf_op jit(solution)/shard_map/ppermute | solution.py:370
  10.9 13.4 %collective-permute-start = (bf16[6,48,128]{2,1,0:T(8,128)(2,1)S(1)}, bf16[6,48,128]{2,1,0:T(8,128)(2,1)S(1)}, u32[]{:S(2)}, u32[]{:S(2)}) collective-permute-start(bf16[6,48,128]{2,1,0:T(8,128)(2,1)S(1)} %get-tuple-element.19), channel_id=1, source_target_pairs={{0,3},{1,4},{2,5},{3,6},{4,7},{5,8},{6,9},{7,10},{8,11},{9,12},{10... | collective-permute-start | bytes 221192 | tf_op jit(solution)/shard_map/ppermute | solution.py:370
  15.4 7.6 %collective-permute-start.3 = (bf16[6,48,128]{2,1,0:T(8,128)(2,1)S(1)}, bf16[6,48,128]{2,1,0:T(8,128)(2,1)S(1)}, u32[]{:S(2)}, u32[]{:S(2)}) collective-permute-start(bf16[6,48,128]{2,1,0:T(8,128)(2,1)S(1)} %get-tuple-element.21), channel_id=1, source_target_pairs={{1,0},{2,1},{3,2},{4,3},{5,4},{6,5},{7,6},{8,7},{9,8},{10,9},{11,1... | collective-permute-start | bytes 221192 | tf_op jit(solution)/shard_map/ppermute | solution.py:370
  18.1 9.9 %collective-permute-start.5 = (bf16[6,48,128]{2,1,0:T(8,128)(2,1)S(1)}, bf16[6,48,128]{2,1,0:T(8,128)(2,1)S(1)}, u32[]{:S(2)}, u32[]{:S(2)}) collective-permute-start(bf16[6,48,128]{2,1,0:T(8,128)(2,1)S(1)} %get-tuple-element.22), channel_id=1, source_target_pairs={{3,0},{4,1},{5,2},{6,3},{7,4},{8,5},{9,6},{10,7},{11,8},{12,9},{13... | collective-permute-start | bytes 221192 | tf_op jit(solution)/shard_map/ppermute | solution.py:370
  19.4 0.6 copy-start.5
  20.0 8.6 %collective-permute-start.4 = (bf16[6,48,128]{2,1,0:T(8,128)(2,1)S(1)}, bf16[6,48,128]{2,1,0:T(8,128)(2,1)S(1)}, u32[]{:S(2)}, u32[]{:S(2)}) collective-permute-start(bf16[6,48,128]{2,1,0:T(8,128)(2,1)S(1)} %get-tuple-element.22), channel_id=1, source_target_pairs={{2,0},{3,1},{4,2},{5,3},{6,4},{7,5},{8,6},{9,7},{10,8},{11,9},{12,... | collective-permute-start | bytes 221192 | tf_op jit(solution)/shard_map/ppermute | solution.py:370
  23.0 0.6 copy-start.11
  23.6 0.6 copy-start.7
  24.3 0.6 copy-start.9
  28.0 0.6 copy-start.13
  28.6 0.6 copy-start.15
  29.3 0.7 copy-start.17
  29.3 0.7 copy-start.18
  29.3 0.7 copy-start.19
  30.0 0.9 copy-start.6
  30.8 0.9 copy-start.8
  31.7 0.9 copy-start.10
  32.6 0.9 copy-start.12
  33.5 0.9 copy-start.14
  34.4 0.9 copy-start.16
  129.4 35.2 %all-to-all-start.3 = ((f32[16,68,128]{2,1,0:T(8,128)}), f32[16,68,128]{2,1,0:T(8,128)S(1)}, u32[]{:S(2)}, u32[]{:S(2)}) async-start(f32[16,68,128]{2,1,0:T(8,128)} %broadcast_in_dim.38), calls=%async_computation.3 | async-start | bytes 1179648 | tf_op jit(solution)/shard_map/all_to_all | solution.py:387
  135.7 12.3 %collective-permute-start.8 = (bf16[6,48,128]{2,1,0:T(8,128)(2,1)S(1)}, bf16[6,48,128]{2,1,0:T(8,128)(2,1)S(1)}, u32[]{:S(2)}, u32[]{:S(2)}) collective-permute-start(bf16[6,48,128]{2,1,0:T(8,128)(2,1)S(1)} %get-tuple-element.26), channel_id=1, source_target_pairs={{0,1},{1,2},{2,3},{3,4},{4,5},{5,6},{6,7},{7,8},{8,9},{9,10},{10,1... | collective-permute-start | bytes 221192 | tf_op jit(solution)/shard_map/ppermute | solution.py:370
  138.1 13.2 %collective-permute-start.7 = (bf16[6,48,128]{2,1,0:T(8,128)(2,1)S(1)}, bf16[6,48,128]{2,1,0:T(8,128)(2,1)S(1)}, u32[]{:S(2)}, u32[]{:S(2)}) collective-permute-start(bf16[6,48,128]{2,1,0:T(8,128)(2,1)S(1)} %get-tuple-element.25), channel_id=1, source_target_pairs={{0,2},{1,3},{2,4},{3,5},{4,6},{5,7},{6,8},{7,9},{8,10},{9,11},{10,... | collective-permute-start | bytes 221192 | tf_op jit(solution)/shard_map/ppermute | solution.py:370
  140.4 10.8 %collective-permute-start.6 = (bf16[6,48,128]{2,1,0:T(8,128)(2,1)S(1)}, bf16[6,48,128]{2,1,0:T(8,128)(2,1)S(1)}, u32[]{:S(2)}, u32[]{:S(2)}) collective-permute-start(bf16[6,48,128]{2,1,0:T(8,128)(2,1)S(1)} %get-tuple-element.25), channel_id=1, source_target_pairs={{0,3},{1,4},{2,5},{3,6},{4,7},{5,8},{6,9},{7,10},{8,11},{9,12},{10... | collective-permute-start | bytes 221192 | tf_op jit(solution)/shard_map/ppermute | solution.py:370
  144.1 7.1 %collective-permute-start.9 = (bf16[6,48,128]{2,1,0:T(8,128)(2,1)S(1)}, bf16[6,48,128]{2,1,0:T(8,128)(2,1)S(1)}, u32[]{:S(2)}, u32[]{:S(2)}) collective-permute-start(bf16[6,48,128]{2,1,0:T(8,128)(2,1)S(1)} %get-tuple-element.27), channel_id=1, source_target_pairs={{1,0},{2,1},{3,2},{4,3},{5,4},{6,5},{7,6},{8,7},{9,8},{10,9},{11,1... | collective-permute-start | bytes 221192 | tf_op jit(solution)/shard_map/ppermute | solution.py:370
  146.7 9.6 %collective-permute-start.11 = (bf16[6,48,128]{2,1,0:T(8,128)(2,1)S(1)}, bf16[6,48,128]{2,1,0:T(8,128)(2,1)S(1)}, u32[]{:S(2)}, u32[]{:S(2)}) collective-permute-start(bf16[6,48,128]{2,1,0:T(8,128)(2,1)S(1)} %get-tuple-element.28), channel_id=1, source_target_pairs={{3,0},{4,1},{5,2},{6,3},{7,4},{8,5},{9,6},{10,7},{11,8},{12,9},{13... | collective-permute-start | bytes 221192 | tf_op jit(solution)/shard_map/ppermute | solution.py:370
  148.0 8.3 %collective-permute-start.10 = (bf16[6,48,128]{2,1,0:T(8,128)(2,1)S(1)}, bf16[6,48,128]{2,1,0:T(8,128)(2,1)S(1)}, u32[]{:S(2)}, u32[]{:S(2)}) collective-permute-start(bf16[6,48,128]{2,1,0:T(8,128)(2,1)S(1)} %get-tuple-element.28), channel_id=1, source_target_pairs={{2,0},{3,1},{4,2},{5,3},{6,4},{7,5},{8,6},{9,7},{10,8},{11,9},{12,... | collective-permute-start | bytes 221192 | tf_op jit(solution)/shard_map/ppermute | solution.py:370

commit v3 on v2

--- a/solution.py
+++ b/solution.py
@@ -20,6 +20,10 @@
 CELLS_IN_CHUNK = CHUNK * TILE
 GROUPS = TILE // 8
 STEPS = (-3, -2, -1, 1, 2, 3)
+VMEM_LIMIT = 32 * 2**20
+DP = ("x_hi", "y", "core")
+SPACE = ("z", "x_lo")
+PLANE = ("x_hi", "y", "core", "x_lo")
 
 norm_eps = 1e-06
 inv_sqrt_two_pi = 0.3989422804014327
@@ -307,7 +311,7 @@
     for q in range(quarters):
         lanes = slice(q * LANES, (q + 1) * LANES)
         sums[q * LANES : (q + 1) * LANES, :] = up_sum[:, lanes]
-        sums[(quarters + q) * LANES : (quarters + q + 1) * LANES, :] = down_sum[:, lanes]
+        sums[(quarters + q) * LANES : (quarters + q + 1) * LANES, :] = down_sum[:, lanes].T
     at = 2 * quarters * LANES
     sums[at:, :] = jnp.zeros((sums.shape[0] - at, LANES), f32)
     sums[at : at + TAPS, :] = jnp.sum(tap_sums[...], axis=1)
@@ -343,6 +347,23 @@
     lax.fori_loop(0, TILE // CHUNK, chunk, 0)
 
 
+def unpack_kernel(total, kernel_grad, gain_grad, up_grad, bias_grad, down_grad, scale_grad):
+    quarters = up_grad.shape[1] // LANES
+    units = quarters * LANES
+    for q in range(quarters):
+        lanes = slice(q * LANES, (q + 1) * LANES)
+        up_grad[:, lanes] = total[q * LANES : (q + 1) * LANES, :].astype(f32)
+        down_grad[lanes, :] = total[units + q * LANES : units + (q + 1) * LANES, :].astype(f32)
+    at = 2 * units
+    rest = total[at:, :].astype(f32)
+    kernel_grad[...] = rest[0:TAPS]
+    scale_grad[...] = rest[TAPS : TAPS + 1]
+    gain_grad[...] = rest[TAPS + 1 : TAPS + 2]
+    for q in range(quarters):
+        row = TAPS + 2 + q
+        bias_grad[:, q * LANES : (q + 1) * LANES] = rest[row : row + 1]
+
+
 def shape(dims, dtype=bf16):
     return jax.ShapeDtypeStruct(dims, dtype)
 
@@ -351,7 +372,7 @@
 WHOLE = (TILE, TILE, LANES)
 
 
-def call(kernel, scalars, operands, outs, scratch, flops, limit):
+def call(kernel, scalars, operands, outs, scratch, flops):
     size = sum(math.prod(a.shape) * a.dtype.itemsize for a in (*operands, *outs))
     return pl.pallas_call(
         kernel,
@@ -359,15 +380,15 @@
         in_specs=[SMEM] * len(scalars) + [VMEM] * len(operands),
         out_specs=[VMEM] * len(outs),
         scratch_shapes=scratch,
-        compiler_params=pltpu.CompilerParams(vmem_limit_bytes=limit * 2**20),
+        compiler_params=pltpu.CompilerParams(vmem_limit_bytes=VMEM_LIMIT),
         cost_estimate=pl.CostEstimate(flops=flops, bytes_accessed=size, transcendentals=0),
     )(*scalars, *operands)
 
 
 def shifted(value, step):
-    count = lax.axis_size("space")
+    count = lax.axis_size(SPACE)
     first, last = (max(0, -step), min(count, count - step))
-    return lax.ppermute(value, "space", [(source, source + step) for source in range(first, last)])
+    return lax.ppermute(value, SPACE, [(source, source + step) for source in range(first, last)])
 
 
 def exchange(top, bottom, to_before, to_after):
@@ -375,16 +396,9 @@
     return [shifted(sent[-step], -step) for step in STEPS]
 
 
-def summed_everywhere(flat, factor):
-    rows, lanes = flat.shape
-    dp, space = lax.axis_size("dp"), lax.axis_size("space")
-    part = lax.all_to_all(flat.reshape(dp, rows // dp, lanes), "dp", 0, 0, tiled=True)
-    part = jnp.sum(part, axis=0).reshape(space, -1)
-    part = jnp.sum(lax.all_to_all(part, "space", 0, 0, tiled=True), axis=0) * factor
-    part = jnp.broadcast_to(part, (space,) + part.shape)
-    part = lax.all_to_all(part, "space", 0, 0, tiled=True).reshape(rows // dp, lanes)
-    part = jnp.broadcast_to(part, (dp,) + part.shape)
-    return lax.all_to_all(part, "dp", 0, 0, tiled=True).reshape(rows, lanes)
+def spread(value, axes):
+    copies = jnp.broadcast_to(value, (lax.axis_size(axes),) + value.shape)
+    return lax.all_to_all(copies, axes, 0, 0, tiled=True)
 
 
 def local(
@@ -400,7 +414,7 @@
     layer_scale,
 ):
     beside = neighbours[0]
-    where = lax.axis_index("space").astype(jnp.int32)[None]
+    where = lax.axis_index(SPACE).astype(jnp.int32)[None]
     tile, upstream = fields[0, 0], cotangent[0, 0]
     mask = jnp.broadcast_to(land_mask[0].astype(bf16)[..., None], WHOLE)
     taps = conv_kernel.reshape(TAPS, LANES)
@@ -415,7 +429,6 @@
         [shape(STRIP)] * 4,
         [pltpu.VMEM((TILE * TILE, LANES), f32)],
         TILE * TILE * LANES,
-        32,
     )
     strips = exchange(*rims)
     block_out, conv_grad, *rims, sums = call(
@@ -452,11 +465,14 @@
             pltpu.VMEM((16, LANES), f32),
         ],
         12 * TILE * TILE * LANES * units,
-        40,
     )
     strips = exchange(*rims)
-    cells = TILE * TILE * lax.axis_size("dp") * lax.axis_size("space")
-    total = summed_everywhere(sums, 1.0 / math.sqrt(cells))
+    cells = TILE * TILE * lax.axis_size(DP) * lax.axis_size(SPACE)
+    part = sums.reshape(lax.axis_size(PLANE), -1, LANES)
+    part = jnp.sum(lax.all_to_all(part, PLANE, 0, 0, tiled=True), axis=0)
+    part, strips = lax.optimization_barrier((part, strips))
+    part = jnp.sum(spread(part, "z"), axis=0) * (1.0 / math.sqrt(cells))
+    total = spread(part.astype(bf16), PLANE).reshape(sum_rows, LANES)
     (fields_grad,) = call(
         back_kernel,
         (beside, where),
@@ -464,33 +480,45 @@
         [shape(WHOLE)],
         [pltpu.VMEM((EXT_ROWS, EXT_COLS, LANES), f32)],
         2 * TAPS * TILE * TILE * LANES,
-        32,
     )
-    up_grad = total[:units].reshape(quarters, LANES, LANES).transpose(1, 0, 2).reshape(LANES, units)
-    down_grad = total[units : 2 * units].reshape(quarters, LANES, LANES).transpose(0, 2, 1)
-    at = 2 * units
+    kernel_grad, gain_grad, up_grad, bias_grad, down_grad, scale_grad = call(
+        unpack_kernel,
+        (),
+        (total,),
+        [
+            shape((TAPS, LANES), f32),
+            shape((1, LANES), f32),
+            shape((LANES, units), f32),
+            shape((1, units), f32),
+            shape((units, LANES), f32),
+            shape((1, LANES), f32),
+        ],
+        [],
+        sum_rows * LANES,
+    )
     return (
         block_out[None, None],
         fields_grad[None, None],
-        total[at : at + TAPS].reshape(KERNEL, KERNEL, LANES),
-        total[at + TAPS + 1],
+        kernel_grad.reshape(KERNEL, KERNEL, LANES),
+        gain_grad[0],
         up_grad,
-        total[at + TAPS + 2 : at + TAPS + 2 + quarters].reshape(units),
-        down_grad.reshape(units, LANES),
-        total[at + TAPS],
+        bias_grad[0],
+        down_grad,
+        scale_grad[0],
     )
 
 
 def solution(mesh):
-    tiles = P("dp", "space", None, None, None)
+    fine = jax.sharding.Mesh(mesh.devices.reshape(2, 4, 2, 16, 2), DP + SPACE)
+    tiles = P(DP, SPACE, None, None, None)
     return jax.shard_map(
         local,
-        mesh=mesh,
+        mesh=fine,
         in_specs=(
             tiles,
             tiles,
-            P("space", None, None),
-            P("space", None),
+            P(SPACE, None, None),
+            P(SPACE, None),
             P(),
             P(),
             P(),

time: 169 us -> 159 us (0.941)
  the two profiles are of different devices: /device:TPU:6 before, /device:TPU:1 now
where the time goes in v3:
time: 159 us; the launch traced here: 158 us
  starting transfers between devices  58.9 us (37%)
  Pallas kernels  37.5 us (24%)
  blocking collectives  25.5 us (16%)
  waiting for transfers between devices  21.1 us (13%)
  local copies, waits for them, and re-layouts  12.8 us (8%)
    pallas_call x4, Pallas kernels, call(): pl.pallas_call(kernel, out_shape=outs, in_specs=[SMEM] * len(scalars) + [...  37.5 us
    ppermute x12, starting transfers between devices, shifted(): lax.ppermute(value, SPACE, [(source, source + step) for source in range(f...  32.9 us
    all_to_all x1, blocking collectives, spread(): return lax.all_to_all(copies, axes, 0, 0, tiled=True)  25.5 us
    all_to_all x1, starting transfers between devices, spread(): return lax.all_to_all(copies, axes, 0, 0, tiled=True)  15.4 us
    ppermute x12, waiting for transfers between devices, shifted(): lax.ppermute(value, SPACE, [(source, source + step) for source in range(f...  12 us
    all_to_all x1, starting transfers between devices, local(): part = jnp.sum(lax.all_to_all(part, PLANE, 0, 0, tiled=True), axis=0)  10.6 us
    unnamed x42, local copies, waits for them, and re-layouts  10.1 us
    all_to_all x1, waiting for transfers between devices, spread(): return lax.all_to_all(copies, axes, 0, 0, tiled=True)  9.07 us
  transfers between devices with their start and end apart: 14, of which 6 were waited for; matrix products, arithmetic and copies ran while one was open for 0% of the time, Pallas kernels for 0%

profile of v3, /device:TPU:1, one launch (start us, length us, event | category | flops | bytes accessed | tf_op | source)
XLA Modules:
  0.0 157.6 jit_solution(9043792603693750177)
XLA Ops:
  0.6 0.0 copy-start.1
  0.6 0.8 convert_bitcast_fusion
  1.5 0.4 broadcast_in_dim.31.mask
  1.8 0.0 copy-done.1
  1.8 0.3 copy-done.2
  2.2 0.8 shard_map.161
  3.0 5.3 %collective-permute-start = (bf16[6,48,128]{2,1,0:T(8,128)(2,1)S(1)}, bf16[6,48,128]{2,1,0:T(8,128)(2,1)S(1)}, u32[]{:S(2)}, u32[]{:S(2)}) collective-permute-start(bf16[6,48,128]{2,1,0:T(8,128)(2,1)S(1)} %get-tuple-element.32), channel_id=1, source_target_pairs={{0,3},{1,4},{2,5},{3,6},{4,7},{5,8},{6,9},{7,10},{8,11},{9,12},{10... | collective-permute-start | bytes 221192 | tf_op jit(solution)/shard_map/ppermute | solution.py:391
  8.3 3.5 %collective-permute-start.1 = (bf16[6,48,128]{2,1,0:T(8,128)(2,1)S(1)}, bf16[6,48,128]{2,1,0:T(8,128)(2,1)S(1)}, u32[]{:S(2)}, u32[]{:S(2)}) collective-permute-start(bf16[6,48,128]{2,1,0:T(8,128)(2,1)S(1)} %get-tuple-element.32), channel_id=1, source_target_pairs={{0,2},{1,3},{2,4},{3,5},{4,6},{5,7},{6,8},{7,9},{8,10},{9,11},{10,... | collective-permute-start | bytes 221192 | tf_op jit(solution)/shard_map/ppermute | solution.py:391
  11.8 3.5 %collective-permute-start.2 = (bf16[6,48,128]{2,1,0:T(8,128)(2,1)S(1)}, bf16[6,48,128]{2,1,0:T(8,128)(2,1)S(1)}, u32[]{:S(2)}, u32[]{:S(2)}) collective-permute-start(bf16[6,48,128]{2,1,0:T(8,128)(2,1)S(1)} %get-tuple-element.33), channel_id=1, source_target_pairs={{0,1},{1,2},{2,3},{3,4},{4,5},{5,6},{6,7},{7,8},{8,9},{9,10},{10,1... | collective-permute-start | bytes 221192 | tf_op jit(solution)/shard_map/ppermute | solution.py:391
  15.4 1.3 collective-permute-start.3
  16.7 1.3 collective-permute-start.4
  18.0 0.0 collective-permute-done.s0
  18.0 0.0 copy-start.5
  18.0 0.6 copy-done.5
  18.6 1.3 collective-permute-start.5
  19.9 0.0 copy-done.20
  19.9 0.0 collective-permute-done.1.s1
  19.9 0.0 copy-start.7
  19.9 0.6 copy-done.7
  20.6 0.0 collective-permute-done.2.s2
  20.6 0.6 copy-done.9
  21.2 0.0 collective-permute-done.3.s3
  21.2 0.6 copy-done.11
  21.8 2.5 %collective-permute-done.4.s4 = bf16[6,48,128]{2,1,0:T(8,128)(2,1)S(1)} collective-permute-done((bf16[6,48,128]{2,1,0:T(8,128)(2,1)S(1)}, bf16[6,48,128]{2,1,0:T(8,128)(2,1)S(1)}, u32[]{:S(2)}, u32[]{:S(2)}) %collective-permute-start.4) | collective-permute-done | bytes 73760 | tf_op jit(solution)/shard_map/ppermute | solution.py:391
  24.3 0.6 copy-done.13
  24.9 2.8 %collective-permute-done.5.s5 = bf16[6,48,128]{2,1,0:T(8,128)(2,1)S(1)} collective-permute-done((bf16[6,48,128]{2,1,0:T(8,128)(2,1)S(1)}, bf16[6,48,128]{2,1,0:T(8,128)(2,1)S(1)}, u32[]{:S(2)}, u32[]{:S(2)}) %collective-permute-start.5) | collective-permute-done | bytes 73760 | tf_op jit(solution)/shard_map/ppermute | solution.py:391
  27.7 0.6 copy-done.15
  28.3 0.0 copy-done
  28.3 0.0 copy-done.3
  28.3 0.0 copy-done.4
  28.3 0.7 copy-done.17
  29.0 0.0 copy-done.18
  29.0 0.0 copy-done.19
  29.0 0.9 copy-done.6
  29.9 0.9 copy-done.8
  30.8 0.9 copy-done.10
  31.6 0.9 copy-done.12
  32.5 0.9 copy-done.14
  33.4 0.9 copy-done.16
  34.3 28.8 %shard_map.162 = (bf16[48,48,128]{2,1,0:T(8,128)(2,1)}, bf16[48,48,128]{2,1,0:T(8,128)(2,1)S(1)}, bf16[6,48,128]{2,1,0:T(8,128)(2,1)S(1)}, bf16[6,48,128]{2,1,0:...) custom-call(s32[8]{0:T(128)S(1)} %bitcast.19, ...), custom_call_target="tpu_custom_call" | custom-call | flops 1811939328 | bytes 4533760 | tf_op jit(solution)/shard_map/pallas_call | solution.py:377
  63.1 0.9 reshape.35
  64.0 10.6 %all-to-all-start = ((f32[32,34,128]{2,1,0:T(8,128)}), f32[32,34,128]{2,1,0:T(8,128)S(1)}, u32[]{:S(2)}, u32[]{:S(2)}) async-start(f32[32,34,128]{2,1,0:T(8,128)} %reshape.35), calls=%async_computation | async-start | bytes 1310720 | tf_op jit(solution)/shard_map/all_to_all | solution.py:472
  74.6 5.3 %collective-permute-start.6 = (bf16[6,48,128]{2,1,0:T(8,128)(2,1)S(1)}, bf16[6,48,128]{2,1,0:T(8,128)(2,1)S(1)}, u32[]{:S(2)}, u32[]{:S(2)}) collective-permute-start(bf16[6,48,128]{2,1,0:T(8,128)(2,1)S(1)} %get-tuple-element.39), channel_id=1, source_target_pairs={{0,3},{1,4},{2,5},{3,6},{4,7},{5,8},{6,9},{7,10},{8,11},{9,12},{10... | collective-permute-start | bytes 221192 | tf_op jit(solution)/shard_map/ppermute | solution.py:391
  80.0 4.1 %collective-permute-start.7 = (bf16[6,48,128]{2,1,0:T(8,128)(2,1)S(1)}, bf16[6,48,128]{2,1,0:T(8,128)(2,1)S(1)}, u32[]{:S(2)}, u32[]{:S(2)}) collective-permute-start(bf16[6,48,128]{2,1,0:T(8,128)(2,1)S(1)} %get-tuple-element.39), channel_id=1, source_target_pairs={{0,2},{1,3},{2,4},{3,5},{4,6},{5,7},{6,8},{7,9},{8,10},{9,11},{10,... | collective-permute-start | bytes 221192 | tf_op jit(solution)/shard_map/ppermute | solution.py:391
  84.1 3.3 %collective-permute-start.8 = (bf16[6,48,128]{2,1,0:T(8,128)(2,1)S(1)}, bf16[6,48,128]{2,1,0:T(8,128)(2,1)S(1)}, u32[]{:S(2)}, u32[]{:S(2)}) collective-permute-start(bf16[6,48,128]{2,1,0:T(8,128)(2,1)S(1)} %get-tuple-element.40), channel_id=1, source_target_pairs={{0,1},{1,2},{2,3},{3,4},{4,5},{5,6},{6,7},{7,8},{8,9},{9,10},{10,1... | collective-permute-start | bytes 221192 | tf_op jit(solution)/shard_map/ppermute | solution.py:391
  87.4 1.3 collective-permute-start.9
  88.7 1.3 collective-permute-start.10
  90.0 0.0 collective-permute-done.6.s0
  90.0 1.3 collective-permute-start.11
  91.3 0.0 all-to-all-done
  91.3 0.1 reduce_sum.18
  91.4 0.0 collective-permute-done.7.s1
  91.4 0.0 collective-permute-done.8.s2
  91.4 1.1 collective-permute-done.9.s3
  92.5 3.6 %collective-permute-done.10.s4 = bf16[6,48,128]{2,1,0:T(8,128)(2,1)S(1)} collective-permute-done((bf16[6,48,128]{2,1,0:T(8,128)(2,1)S(1)}, bf16[6,48,128]{2,1,0:T(8,128)(2,1)S(1)}, u32[]{:S(2)}, u32[]{:S(2)}) %collective-permute-start.10) | collective-permute-done | bytes 73760 | tf_op jit(solution)/shard_map/ppermute | solution.py:391
  96.0 2.2 %collective-permute-done.11.s5 = bf16[6,48,128]{2,1,0:T(8,128)(2,1)S(1)} collective-permute-done((bf16[6,48,128]{2,1,0:T(8,128)(2,1)S(1)}, bf16[6,48,128]{2,1,0:T(8,128)(2,1)S(1)}, u32[]{:S(2)}, u32[]{:S(2)}) %collective-permute-start.11) | collective-permute-done | bytes 73760 | tf_op jit(solution)/shard_map/ppermute | solution.py:391
  98.2 25.5 %all_to_all.15 = f32[16,34,128]{2,1,0:T(8,128)S(1)} all-to-all(f32[16,34,128]{2,1,0:T(8,128)S(1)} %broadcast_in_dim.37), channel_id=1, replica_groups=mesh['x_hi'=2,'y'=4,'core'=2,'z'=16,'x_lo'=2] {'z'}, dimensions={0} | all-to-all | bytes 557056 | tf_op jit(solution)/shard_map/all_to_all | solution.py:401
  123.8 0.8 broadcast_in_dim.38
  124.6 15.4 %all-to-all-start.2 = ((bf16[32,34,128]{2,1,0:T(8,128)(2,1)}), bf16[32,34,128]{2,1,0:T(8,128)(2,1)S(1)}, u32[]{:S(2)}, u32[]{:S(2)}) async-start(bf16[32,34,128]{2,1,0:T(8,128)(2,1)} %broadcast_in_dim.38), calls=%async_computation.2 | async-start | bytes 655360 | tf_op jit(solution)/shard_map/all_to_all | solution.py:401
  139.9 9.1 %all-to-all-done.2 = bf16[32,34,128]{2,1,0:T(8,128)(2,1)S(1)} async-done(((bf16[32,34,128]{2,1,0:T(8,128)(2,1)}), bf16[32,34,128]{2,1,0:T(8,128)(2,1)S(1)}, u32[]{:S(2)}, u32[]{:S(2)}) %all-to-all-start.2) | async-done | bytes 278560 | tf_op jit(solution)/shard_map/all_to_all | solution.py:401
  149.0 0.1 reshape.36.total
  149.1 7.0 %shard_map.163 = bf16[48,48,128]{2,1,0:T(8,128)(2,1)} custom-call(s32[8]{0:T(128)S(1)} %bitcast.20, s32[1]{0:T(128)} %bitcast.1.where, bf16[48,48,128]{2,1,0:T(8,128)(2,1)S(1)} %get-tuple-element.37.conv_grad, bf16[48,48,128]{2,1,0:T(8,128)(2,1)S(1)} %bitcast.15, bf16[48,48,128]{2,1,0:T(8,128)(2,1)S(1)} %broadcast_in_dim.31.mask, ...), custom_call_target="tpu_custom_call" | custom-call | flops 28901376 | bytes 2826752 | tf_op jit(solution)/shard_map/pallas_call | solution.py:377
  156.1 0.8 shard_map.164
  157.0 0.6 reshape.37
  (23 shorter events, 0.1 us)
Async XLA Ops:
  0.6 1.2 copy-start.1
  1.5 0.7 copy-start.2
  2.2 17.7 %copy-start.20 = (f32[7,7,128]{2,1,0:T(8,128)S(1)}, f32[7,7,128]{2,1,0:T(8,128)}, u32[]{:S(2)}) copy-start(f32[7,7,128]{2,1,0:T(8,128)} %param.14) | copy-start | bytes 75268
  2.2 26.2 %copy-start = (bf16[1,1,48,48,128]{4,3,2,1,0:T(8,128)(2,1)S(1)}, bf16[1,1,48,48,128]{4,3,2,1,0:T(8,128)(2,1)}, u32[]{:S(2)}) copy-start(bf16[1,1,48,48,128]{4,3,2,1,0:T(8,128)(2,1)} %param.11) | copy-start | bytes 1769476
  2.2 26.2 %copy-start.3 = (bf16[128,512]{1,0:T(8,128)(2,1)S(1)}, bf16[128,512]{1,0:T(8,128)(2,1)}, u32[]{:S(2)}) copy-start(bf16[128,512]{1,0:T(8,128)(2,1)} %up_weight.1) | copy-start | bytes 393220
  2.2 26.2 %copy-start.4 = (bf16[512,128]{1,0:T(8,128)(2,1)S(1)}, bf16[512,128]{1,0:T(8,128)(2,1)}, u32[]{:S(2)}) copy-start(bf16[512,128]{1,0:T(8,128)(2,1)} %down_weight.1) | copy-start | bytes 393220
  3.0 15.0 %collective-permute-start = (bf16[6,48,128]{2,1,0:T(8,128)(2,1)S(1)}, bf16[6,48,128]{2,1,0:T(8,128)(2,1)S(1)}, u32[]{:S(2)}, u32[]{:S(2)}) collective-permute-start(bf16[6,48,128]{2,1,0:T(8,128)(2,1)S(1)} %get-tuple-element.32), channel_id=1, source_target_pairs={{0,3},{1,4},{2,5},{3,6},{4,7},{5,8},{6,9},{7,10},{8,11},{9,12},{10... | collective-permute-start | bytes 221192 | tf_op jit(solution)/shard_map/ppermute | solution.py:391
  8.3 11.6 %collective-permute-start.1 = (bf16[6,48,128]{2,1,0:T(8,128)(2,1)S(1)}, bf16[6,48,128]{2,1,0:T(8,128)(2,1)S(1)}, u32[]{:S(2)}, u32[]{:S(2)}) collective-permute-start(bf16[6,48,128]{2,1,0:T(8,128)(2,1)S(1)} %get-tuple-element.32), channel_id=1, source_target_pairs={{0,2},{1,3},{2,4},{3,5},{4,6},{5,7},{6,8},{7,9},{8,10},{9,11},{10,... | collective-permute-start | bytes 221192 | tf_op jit(solution)/shard_map/ppermute | solution.py:391
  11.8 8.7 %collective-permute-start.2 = (bf16[6,48,128]{2,1,0:T(8,128)(2,1)S(1)}, bf16[6,48,128]{2,1,0:T(8,128)(2,1)S(1)}, u32[]{:S(2)}, u32[]{:S(2)}) collective-permute-start(bf16[6,48,128]{2,1,0:T(8,128)(2,1)S(1)} %get-tuple-element.33), channel_id=1, source_target_pairs={{0,1},{1,2},{2,3},{3,4},{4,5},{5,6},{6,7},{7,8},{8,9},{9,10},{10,1... | collective-permute-start | bytes 221192 | tf_op jit(solution)/shard_map/ppermute | solution.py:391
  15.4 5.8 %collective-permute-start.3 = (bf16[6,48,128]{2,1,0:T(8,128)(2,1)S(1)}, bf16[6,48,128]{2,1,0:T(8,128)(2,1)S(1)}, u32[]{:S(2)}, u32[]{:S(2)}) collective-permute-start(bf16[6,48,128]{2,1,0:T(8,128)(2,1)S(1)} %get-tuple-element.34), channel_id=1, source_target_pairs={{1,0},{2,1},{3,2},{4,3},{5,4},{6,5},{7,6},{8,7},{9,8},{10,9},{11,1... | collective-permute-start | bytes 221192 | tf_op jit(solution)/shard_map/ppermute | solution.py:391
  16.7 7.6 %collective-permute-start.4 = (bf16[6,48,128]{2,1,0:T(8,128)(2,1)S(1)}, bf16[6,48,128]{2,1,0:T(8,128)(2,1)S(1)}, u32[]{:S(2)}, u32[]{:S(2)}) collective-permute-start(bf16[6,48,128]{2,1,0:T(8,128)(2,1)S(1)} %get-tuple-element.35), channel_id=1, source_target_pairs={{2,0},{3,1},{4,2},{5,3},{6,4},{7,5},{8,6},{9,7},{10,8},{11,9},{12,... | collective-permute-start | bytes 221192 | tf_op jit(solution)/shard_map/ppermute | solution.py:391
  18.0 0.6 copy-start.5
  18.6 9.1 %collective-permute-start.5 = (bf16[6,48,128]{2,1,0:T(8,128)(2,1)S(1)}, bf16[6,48,128]{2,1,0:T(8,128)(2,1)S(1)}, u32[]{:S(2)}, u32[]{:S(2)}) collective-permute-start(bf16[6,48,128]{2,1,0:T(8,128)(2,1)S(1)} %get-tuple-element.35), channel_id=1, source_target_pairs={{3,0},{4,1},{5,2},{6,3},{7,4},{8,5},{9,6},{10,7},{11,8},{12,9},{13... | collective-permute-start | bytes 221192 | tf_op jit(solution)/shard_map/ppermute | solution.py:391
  19.9 0.6 copy-start.7
  20.6 0.6 copy-start.9
  21.2 0.6 copy-start.11
  24.3 0.6 copy-start.13
  27.7 0.6 copy-start.15
  28.3 0.7 copy-start.17
  28.3 0.7 copy-start.18
  28.3 0.7 copy-start.19
  29.0 0.9 copy-start.6
  29.9 0.9 copy-start.8
  30.8 0.9 copy-start.10
  31.6 0.9 copy-start.12
  32.5 0.9 copy-start.14
  33.4 0.9 copy-start.16
  64.0 27.3 %all-to-all-start = ((f32[32,34,128]{2,1,0:T(8,128)}), f32[32,34,128]{2,1,0:T(8,128)S(1)}, u32[]{:S(2)}, u32[]{:S(2)}) async-start(f32[32,34,128]{2,1,0:T(8,128)} %reshape.35), calls=%async_computation | async-start | bytes 1310720 | tf_op jit(solution)/shard_map/all_to_all | solution.py:472
  74.6 15.4 %collective-permute-start.6 = (bf16[6,48,128]{2,1,0:T(8,128)(2,1)S(1)}, bf16[6,48,128]{2,1,0:T(8,128)(2,1)S(1)}, u32[]{:S(2)}, u32[]{:S(2)}) collective-permute-start(bf16[6,48,128]{2,1,0:T(8,128)(2,1)S(1)} %get-tuple-element.39), channel_id=1, source_target_pairs={{0,3},{1,4},{2,5},{3,6},{4,7},{5,8},{6,9},{7,10},{8,11},{9,12},{10... | collective-permute-start | bytes 221192 | tf_op jit(solution)/shard_map/ppermute | solution.py:391
  80.0 11.4 %collective-permute-start.7 = (bf16[6,48,128]{2,1,0:T(8,128)(2,1)S(1)}, bf16[6,48,128]{2,1,0:T(8,128)(2,1)S(1)}, u32[]{:S(2)}, u32[]{:S(2)}) collective-permute-start(bf16[6,48,128]{2,1,0:T(8,128)(2,1)S(1)} %get-tuple-element.39), channel_id=1, source_target_pairs={{0,2},{1,3},{2,4},{3,5},{4,6},{5,7},{6,8},{7,9},{8,10},{9,11},{10,... | collective-permute-start | bytes 221192 | tf_op jit(solution)/shard_map/ppermute | solution.py:391
  84.1 7.3 %collective-permute-start.8 = (bf16[6,48,128]{2,1,0:T(8,128)(2,1)S(1)}, bf16[6,48,128]{2,1,0:T(8,128)(2,1)S(1)}, u32[]{:S(2)}, u32[]{:S(2)}) collective-permute-start(bf16[6,48,128]{2,1,0:T(8,128)(2,1)S(1)} %get-tuple-element.40), channel_id=1, source_target_pairs={{0,1},{1,2},{2,3},{3,4},{4,5},{5,6},{6,7},{7,8},{8,9},{9,10},{10,1... | collective-permute-start | bytes 221192 | tf_op jit(solution)/shard_map/ppermute | solution.py:391
  87.4 5.1 %collective-permute-start.9 = (bf16[6,48,128]{2,1,0:T(8,128)(2,1)S(1)}, bf16[6,48,128]{2,1,0:T(8,128)(2,1)S(1)}, u32[]{:S(2)}, u32[]{:S(2)}) collective-permute-start(bf16[6,48,128]{2,1,0:T(8,128)(2,1)S(1)} %get-tuple-element.41), channel_id=1, source_target_pairs={{1,0},{2,1},{3,2},{4,3},{5,4},{6,5},{7,6},{8,7},{9,8},{10,9},{11,1... | collective-permute-start | bytes 221192 | tf_op jit(solution)/shard_map/ppermute | solution.py:391
  88.7 7.3 %collective-permute-start.10 = (bf16[6,48,128]{2,1,0:T(8,128)(2,1)S(1)}, bf16[6,48,128]{2,1,0:T(8,128)(2,1)S(1)}, u32[]{:S(2)}, u32[]{:S(2)}) collective-permute-start(bf16[6,48,128]{2,1,0:T(8,128)(2,1)S(1)} %get-tuple-element.42), channel_id=1, source_target_pairs={{2,0},{3,1},{4,2},{5,3},{6,4},{7,5},{8,6},{9,7},{10,8},{11,9},{12,... | collective-permute-start | bytes 221192 | tf_op jit(solution)/shard_map/ppermute | solution.py:391
  90.0 8.2 %collective-permute-start.11 = (bf16[6,48,128]{2,1,0:T(8,128)(2,1)S(1)}, bf16[6,48,128]{2,1,0:T(8,128)(2,1)S(1)}, u32[]{:S(2)}, u32[]{:S(2)}) collective-permute-start(bf16[6,48,128]{2,1,0:T(8,128)(2,1)S(1)} %get-tuple-element.42), channel_id=1, source_target_pairs={{3,0},{4,1},{5,2},{6,3},{7,4},{8,5},{9,6},{10,7},{11,8},{12,9},{13... | collective-permute-start | bytes 221192 | tf_op jit(solution)/shard_map/ppermute | solution.py:391
  124.6 24.5 %all-to-all-start.2 = ((bf16[32,34,128]{2,1,0:T(8,128)(2,1)}), bf16[32,34,128]{2,1,0:T(8,128)(2,1)S(1)}, u32[]{:S(2)}, u32[]{:S(2)}) async-start(bf16[32,34,128]{2,1,0:T(8,128)(2,1)} %broadcast_in_dim.38), calls=%async_computation.2 | async-start | bytes 655360 | tf_op jit(solution)/shard_map/all_to_all | solution.py:401

commit v4 on v3

--- a/solution.py
+++ b/solution.py
@@ -16,11 +16,11 @@
 PAD = 2
 EXT_ROWS = TILE + 2 * HALO
 EXT_COLS = 64
-CHUNK = 8
+CHUNK = 16
 CELLS_IN_CHUNK = CHUNK * TILE
 GROUPS = TILE // 8
 STEPS = (-3, -2, -1, 1, 2, 3)
-VMEM_LIMIT = 32 * 2**20
+LARGE, SMALL = 60 * 2**20, 16 * 2**20
 DP = ("x_hi", "y", "core")
 SPACE = ("z", "x_lo")
 PLANE = ("x_hi", "y", "core", "x_lo")
@@ -41,6 +41,7 @@
 bf16 = jnp.bfloat16
 VMEM = pl.BlockSpec(memory_space=pltpu.VMEM)
 SMEM = pl.BlockSpec(memory_space=pltpu.SMEM)
+HBM = pl.BlockSpec(memory_space=pltpu.HBM)
 
 
 def pack_strips(flat, beside, where, top, bottom, to_before, to_after):
@@ -152,23 +153,33 @@
     pack_strips(flat, beside, where, top, bottom, to_before, to_after)
 
 
+def start_copies(sources, targets, done):
+    copies = [
+        pltpu.make_async_copy(source, target, done.at[i])
+        for i, (source, target) in enumerate(zip(sources, targets))
+    ]
+    for copy in copies:
+        copy.start()
+    return copies
+
+
 def block_kernel(
     beside,
     where,
-    fields,
-    cotangent,
-    mask,
+    fields_hbm,
+    mask_hbm,
     s0,
     s1,
     s2,
     s3,
     s4,
     s5,
-    weights,
+    weights_hbm,
+    cotangent_hbm,
+    up_weight_hbm,
+    down_weight_hbm,
     gain,
-    up_weight,
     up_bias,
-    down_weight,
     scale,
     block_out,
     conv_grad,
@@ -192,20 +203,39 @@
     bias_sum,
     tap_sums,
     row_sums,
+    fields,
+    mask,
+    strips,
+    weights,
+    cotangent,
+    up_weight,
+    down_weight,
+    done,
 ):
     ext_flat = ext.reshape(EXT_ROWS * EXT_COLS, LANES)
-
-    def centre(i, _):
-        ext[HALO + i, pl.ds(8, TILE), :] = fields[i].astype(f32) * mask[i].astype(f32)
-        return 0
-
-    lax.fori_loop(0, TILE, centre, 0, unroll=4)
-    place_rims(ext, ext_flat, beside, where, (s0, s1, s2, s3, s4, s5))
+    rims = [strips.at[i] for i in range(len(STEPS))]
+    copies = start_copies(
+        (fields_hbm, mask_hbm, s0, s1, s2, s3, s4, s5)
+        + (weights_hbm, cotangent_hbm, up_weight_hbm, down_weight_hbm),
+        [fields, mask, *rims, weights, cotangent, up_weight, down_weight],
+        done,
+    )
     up_sum[...] = jnp.zeros_like(up_sum)
     down_sum[...] = jnp.zeros_like(down_sum)
     bias_sum[...] = jnp.zeros_like(bias_sum)
     tap_sums[...] = jnp.zeros_like(tap_sums)
     row_sums[...] = jnp.zeros_like(row_sums)
+    for copy in copies[:2]:
+        copy.wait()
+
+    def centre(i, _):
+        ext[HALO + i, pl.ds(8, TILE), :] = fields[i].astype(f32) * mask[i].astype(f32)
+        return 0
+
+    lax.fori_loop(0, TILE, centre, 0, unroll=4)
+    for copy in copies[2:]:
+        copy.wait()
+    place_rims(ext, ext_flat, beside, where, rims)
     ones = jnp.ones((8, CELLS_IN_CHUNK), bf16)
 
     def chunk(step, _):
@@ -228,7 +258,7 @@
             branch_grad[cells, :] = (weighted * cotangent[first + row].astype(f32)).astype(bf16)
             return 0
 
-        lax.fori_loop(0, CHUNK, normalise, 0, unroll=2)
+        lax.fori_loop(0, CHUNK, normalise, 0, unroll=CHUNK)
         hidden[...] = jnp.dot(normed[...], up_weight[...], preferred_element_type=f32)
         active_grad[...] = lax.dot_general(
             branch_grad[...],
@@ -252,7 +282,7 @@
             hidden_grad[cells, :] = (active_grad[cells, :] * slope).astype(bf16)
             return 0
 
-        lax.fori_loop(0, CELLS_IN_CHUNK // 16, activate, 0, unroll=2)
+        lax.fori_loop(0, CELLS_IN_CHUNK // 16, activate, 0, unroll=CELLS_IN_CHUNK // 16)
         hidden[:, 0:LANES] = jnp.dot(active[...], down_weight[...], preferred_element_type=f32)
         active_grad[:, 0:LANES] = lax.dot_general(
             hidden_grad[...], up_weight[...], (((1,), (1,)), ((), ())), preferred_element_type=f32
@@ -286,7 +316,7 @@
                 row_sums[8:16, :] += by_gain[8 * k : 8 * k + 8]
             return 0
 
-        lax.fori_loop(0, CHUNK, finish, 0, unroll=2)
+        lax.fori_loop(0, CHUNK, finish, 0, unroll=CHUNK)
         for b in range(KERNEL):
             totals = [tap_sums[a * KERNEL + b] for a in range(KERNEL)]
             for g in range(GROUPS):
@@ -323,16 +353,44 @@
 
 
 def back_kernel(
-    beside, where, conv_grad, cotangent, mask, s0, s1, s2, s3, s4, s5, weights, fields_grad, ext
+    beside,
+    where,
+    conv_grad_hbm,
+    s0,
+    s1,
+    s2,
+    s3,
+    s4,
+    s5,
+    weights_hbm,
+    mask_hbm,
+    cotangent_hbm,
+    fields_grad,
+    ext,
+    conv_grad,
+    strips,
+    weights,
+    mask,
+    cotangent,
+    done,
 ):
     ext_flat = ext.reshape(EXT_ROWS * EXT_COLS, LANES)
+    rims = [strips.at[i] for i in range(len(STEPS))]
+    copies = start_copies(
+        (conv_grad_hbm, s0, s1, s2, s3, s4, s5, weights_hbm, mask_hbm, cotangent_hbm),
+        [conv_grad, *rims, weights, mask, cotangent],
+        done,
+    )
+    copies[0].wait()
 
     def centre(i, _):
         ext[HALO + i, pl.ds(8, TILE), :] = conv_grad[i].astype(f32)
         return 0
 
     lax.fori_loop(0, TILE, centre, 0, unroll=4)
-    place_rims(ext, ext_flat, beside, where, (s0, s1, s2, s3, s4, s5))
+    for copy in copies[1:]:
+        copy.wait()
+    place_rims(ext, ext_flat, beside, where, rims)
 
     def chunk(step, _):
         first = pl.multiple_of(step * CHUNK, CHUNK)
@@ -372,15 +430,15 @@
 WHOLE = (TILE, TILE, LANES)
 
 
-def call(kernel, scalars, operands, outs, scratch, flops):
+def call(kernel, scalars, operands, outs, scratch, flops, limit, spaces=VMEM):
     size = sum(math.prod(a.shape) * a.dtype.itemsize for a in (*operands, *outs))
     return pl.pallas_call(
         kernel,
         out_shape=outs,
-        in_specs=[SMEM] * len(scalars) + [VMEM] * len(operands),
+        in_specs=[SMEM] * len(scalars) + (spaces if spaces is not VMEM else [VMEM] * len(operands)),
         out_specs=[VMEM] * len(outs),
         scratch_shapes=scratch,
-        compiler_params=pltpu.CompilerParams(vmem_limit_bytes=VMEM_LIMIT),
+        compiler_params=pltpu.CompilerParams(vmem_limit_bytes=limit),
         cost_estimate=pl.CostEstimate(flops=flops, bytes_accessed=size, transcendentals=0),
     )(*scalars, *operands)
 
@@ -399,6 +457,46 @@
 def spread(value, axes):
     copies = jnp.broadcast_to(value, (lax.axis_size(axes),) + value.shape)
     return lax.all_to_all(copies, axes, 0, 0, tiled=True)
+
+
+def block_call(beside, where, *operands):
+    units = operands[10].shape[1]
+    quarters = units // LANES
+    sum_rows = -(-(2 * units + TAPS + 2 + quarters) // 64) * 64
+    return call(
+        block_kernel,
+        (beside, where),
+        operands,
+        [shape(WHOLE), shape(WHOLE)] + [shape(STRIP)] * 4 + [shape((sum_rows, LANES), f32)],
+        [
+            pltpu.VMEM((EXT_ROWS, EXT_COLS, LANES), f32),
+            pltpu.VMEM((TILE * TILE, LANES), f32),
+            pltpu.VMEM((CELLS_IN_CHUNK, LANES), f32),
+            pltpu.VMEM((CELLS_IN_CHUNK, LANES), f32),
+            pltpu.VMEM((CELLS_IN_CHUNK, LANES), bf16),
+            pltpu.VMEM((CELLS_IN_CHUNK, LANES), bf16),
+            pltpu.VMEM((CELLS_IN_CHUNK, units), f32),
+            pltpu.VMEM((CELLS_IN_CHUNK, units), f32),
+            pltpu.VMEM((CELLS_IN_CHUNK, units), bf16),
+            pltpu.VMEM((CELLS_IN_CHUNK, units), bf16),
+            pltpu.VMEM((LANES, units), f32),
+            pltpu.VMEM((LANES, units), f32),
+            pltpu.VMEM((8, units), f32),
+            pltpu.VMEM((TAPS, 8, LANES), f32),
+            pltpu.VMEM((16, LANES), f32),
+            pltpu.VMEM(WHOLE, bf16),
+            pltpu.VMEM(WHOLE, bf16),
+            pltpu.VMEM((len(STEPS), *STRIP), bf16),
+            pltpu.VMEM((TAPS, LANES), f32),
+            pltpu.VMEM(WHOLE, bf16),
+            pltpu.VMEM((LANES, units), bf16),
+            pltpu.VMEM((units, LANES), bf16),
+            pltpu.SemaphoreType.DMA((12,)),
+        ],
+        12 * TILE * TILE * LANES * units,
+        LARGE,
+        [HBM] * 12 + [VMEM] * 3,
+    )
 
 
 def local(
@@ -419,8 +517,6 @@
     mask = jnp.broadcast_to(land_mask[0].astype(bf16)[..., None], WHOLE)
     taps = conv_kernel.reshape(TAPS, LANES)
     units = up_weight.shape[1]
-    quarters = units // LANES
-    sum_rows = -(-(2 * units + TAPS + 2 + quarters) // 64) * 64
 
     rims = call(
         pack_kernel,
@@ -429,58 +525,51 @@
         [shape(STRIP)] * 4,
         [pltpu.VMEM((TILE * TILE, LANES), f32)],
         TILE * TILE * LANES,
+        SMALL,
     )
     strips = exchange(*rims)
-    block_out, conv_grad, *rims, sums = call(
-        block_kernel,
-        (beside, where),
-        (
-            tile,
-            upstream,
-            mask,
-            *strips,
-            taps,
-            norm_gain[None],
-            up_weight,
-            up_bias[None],
-            down_weight,
-            layer_scale[None],
-        ),
-        [shape(WHOLE), shape(WHOLE)] + [shape(STRIP)] * 4 + [shape((sum_rows, LANES), f32)],
-        [
-            pltpu.VMEM((EXT_ROWS, EXT_COLS, LANES), f32),
-            pltpu.VMEM((TILE * TILE, LANES), f32),
-            pltpu.VMEM((CELLS_IN_CHUNK, LANES), f32),
-            pltpu.VMEM((CELLS_IN_CHUNK, LANES), f32),
-            pltpu.VMEM((CELLS_IN_CHUNK, LANES), bf16),
-            pltpu.VMEM((CELLS_IN_CHUNK, LANES), bf16),
-            pltpu.VMEM((CELLS_IN_CHUNK, units), f32),
-            pltpu.VMEM((CELLS_IN_CHUNK, units), f32),
-            pltpu.VMEM((CELLS_IN_CHUNK, units), bf16),
-            pltpu.VMEM((CELLS_IN_CHUNK, units), bf16),
-            pltpu.VMEM((LANES, units), f32),
-            pltpu.VMEM((LANES, units), f32),
-            pltpu.VMEM((8, units), f32),
-            pltpu.VMEM((TAPS, 8, LANES), f32),
-            pltpu.VMEM((16, LANES), f32),
-        ],
-        12 * TILE * TILE * LANES * units,
-    )
-    strips = exchange(*rims)
+    block_out, conv_grad, *rims, sums = block_call(
+        beside,
+        where,
+        tile,
+        mask,
+        *strips,
+        taps,
+        upstream,
+        up_weight,
+        down_weight,
+        norm_gain[None],
+        up_bias[None],
+        layer_scale[None],
+    )
+    sum_rows = sums.shape[0]
     cells = TILE * TILE * lax.axis_size(DP) * lax.axis_size(SPACE)
     part = sums.reshape(lax.axis_size(PLANE), -1, LANES)
     part = jnp.sum(lax.all_to_all(part, PLANE, 0, 0, tiled=True), axis=0)
+    part, rims = lax.optimization_barrier((part, rims))
+    strips = exchange(*rims)
+    part = jnp.sum(spread(part, "z"), axis=0) * (1.0 / math.sqrt(cells))
     part, strips = lax.optimization_barrier((part, strips))
-    part = jnp.sum(spread(part, "z"), axis=0) * (1.0 / math.sqrt(cells))
     total = spread(part.astype(bf16), PLANE).reshape(sum_rows, LANES)
     (fields_grad,) = call(
         back_kernel,
         (beside, where),
-        (conv_grad, upstream, mask, *strips, taps[::-1]),
+        (conv_grad, *strips, taps[::-1], mask, upstream),
         [shape(WHOLE)],
-        [pltpu.VMEM((EXT_ROWS, EXT_COLS, LANES), f32)],
+        [
+            pltpu.VMEM((EXT_ROWS, EXT_COLS, LANES), f32),
+            pltpu.VMEM(WHOLE, bf16),
+            pltpu.VMEM((len(STEPS), *STRIP), bf16),
+            pltpu.VMEM((TAPS, LANES), f32),
+            pltpu.VMEM(WHOLE, bf16),
+            pltpu.VMEM(WHOLE, bf16),
+            pltpu.SemaphoreType.DMA((10,)),
+        ],
         2 * TAPS * TILE * TILE * LANES,
-    )
+        LARGE,
+        [HBM] * 10,
+    )
+    total, fields_grad = lax.optimization_barrier((total, fields_grad))
     kernel_grad, gain_grad, up_grad, bias_grad, down_grad, scale_grad = call(
         unpack_kernel,
         (),
@@ -495,6 +584,7 @@
         ],
         [],
         sum_rows * LANES,
+        SMALL,
     )
     return (
         block_out[None, None],

time: 159 us -> 136 us (0.86)
  waiting for transfers between devices: 21.1 us -> 10.2 us
  local copies, waits for them, and re-layouts: 12.8 us -> 5.95 us
  Pallas kernels: 37.5 us -> 33.2 us
  blocking collectives: 25.5 us -> 23.6 us
  starting transfers between devices: 58.9 us -> 60.7 us
    all_to_all x1 -> x2, starting transfers between devices: 15.4 us -> 30.1 us  [spread(): return lax.all_to_all(copies, axes, 0, 0, tiled=True)]
    all_to_all x1 -> x0, starting transfers between devices: 10.6 us -> none  [local(): part = jnp.sum(lax.all_to_all(part, PLANE, 0, 0, tiled=True), axis=0)]
    unnamed x42, local copies, waits for them, and re-layouts: 10.1 us -> 1.01 us
    all_to_all x1 -> x2, waiting for transfers between devices: 9.07 us -> 0.93 us  [spread(): return lax.all_to_all(copies, axes, 0, 0, tiled=True)]
    pallas_call x4, Pallas kernels: 37.5 us -> 33.2 us  [call(): pl.pallas_call(kernel, out_shape=outs, in_specs=[SMEM] * len(scalars) + (...]
    ppermute x12, waiting for transfers between devices: 12 us -> 9.3 us  [shifted(): lax.ppermute(value, SPACE, [(source, source + step) for source in range(f...]
    ppermute x12, starting transfers between devices: 32.9 us -> 30.6 us  [shifted(): lax.ppermute(value, SPACE, [(source, source + step) for source in range(f...]
    all_to_all x1, blocking collectives: 25.5 us -> 23.6 us  [local(): part = jnp.sum(lax.all_to_all(part, PLANE, 0, 0, tiled=True), axis=0)]
  transfers between devices with their start and end apart: 14 -> 14, of which waited for: 6 -> 6; matrix products, arithmetic and copies ran while one was open for 0% -> 1% of each run, Pallas kernels for 0% -> 6%
where the time goes in v4:
time: 136 us
  starting transfers between devices  60.7 us (45%)
  Pallas kernels  33.2 us (24%)
  blocking collectives  23.6 us (17%)
  waiting for transfers between devices  10.2 us (7%)
  local copies, waits for them, and re-layouts  5.95 us (4%)
    pallas_call x4, Pallas kernels, call(): pl.pallas_call(kernel, out_shape=outs, in_specs=[SMEM] * len(scalars) + (...  33.2 us
    ppermute x12, starting transfers between devices, shifted(): lax.ppermute(value, SPACE, [(source, source + step) for source in range(f...  30.6 us
    all_to_all x2, starting transfers between devices, spread(): return lax.all_to_all(copies, axes, 0, 0, tiled=True)  30.1 us
    all_to_all x1, blocking collectives, local(): part = jnp.sum(lax.all_to_all(part, PLANE, 0, 0, tiled=True), axis=0)  23.6 us
    ppermute x12, waiting for transfers between devices, shifted(): lax.ppermute(value, SPACE, [(source, source + step) for source in range(f...  9.3 us
  transfers between devices with their start and end apart: 14, of which 6 were waited for; matrix products, arithmetic and copies ran while one was open for 1% of the time, Pallas kernels for 6%

profile of v4, /device:TPU:1, one launch (start us, length us, event | category | flops | bytes accessed | tf_op | source)
XLA Modules:
  0.0 135.6 jit_solution(10404738272566173207)
XLA Ops:
  0.6 0.0 copy-start.1
  0.6 0.8 convert_bitcast_fusion
  1.5 0.4 broadcast_in_dim.31.mask.mask_hbm
  1.8 0.0 copy-done.1
  1.8 0.3 copy-done.2
  2.2 0.8 shard_map.161
  3.0 0.0 copy-done
  3.0 4.0 %collective-permute-start.2 = (bf16[6,48,128]{2,1,0:T(8,128)(2,1)S(1)}, bf16[6,48,128]{2,1,0:T(8,128)(2,1)S(1)}, u32[]{:S(2)}, u32[]{:S(2)}) collective-permute-start(bf16[6,48,128]{2,1,0:T(8,128)(2,1)S(1)} %get-tuple-element.40), channel_id=1, source_target_pairs={{0,1},{1,2},{2,3},{3,4},{4,5},{5,6},{6,7},{7,8},{8,9},{9,10},{10,1... | collective-permute-start | bytes 221192 | tf_op jit(solution)/shard_map/ppermute | solution.py:449
  6.9 3.5 %collective-permute-start.1 = (bf16[6,48,128]{2,1,0:T(8,128)(2,1)S(1)}, bf16[6,48,128]{2,1,0:T(8,128)(2,1)S(1)}, u32[]{:S(2)}, u32[]{:S(2)}) collective-permute-start(bf16[6,48,128]{2,1,0:T(8,128)(2,1)S(1)} %get-tuple-element.39), channel_id=1, source_target_pairs={{0,2},{1,3},{2,4},{3,5},{4,6},{5,7},{6,8},{7,9},{8,10},{9,11},{10,... | collective-permute-start | bytes 221192 | tf_op jit(solution)/shard_map/ppermute | solution.py:449
  10.5 4.9 %collective-permute-start = (bf16[6,48,128]{2,1,0:T(8,128)(2,1)S(1)}, bf16[6,48,128]{2,1,0:T(8,128)(2,1)S(1)}, u32[]{:S(2)}, u32[]{:S(2)}) collective-permute-start(bf16[6,48,128]{2,1,0:T(8,128)(2,1)S(1)} %get-tuple-element.39), channel_id=1, source_target_pairs={{0,3},{1,4},{2,5},{3,6},{4,7},{5,8},{6,9},{7,10},{8,11},{9,12},{10... | collective-permute-start | bytes 221192 | tf_op jit(solution)/shard_map/ppermute | solution.py:449
  15.3 1.3 collective-permute-start.3
  16.6 1.3 collective-permute-start.5
  17.9 0.0 collective-permute-done.2.s2
  18.0 0.0 copy-start.15
  18.0 1.3 collective-permute-start.4
  19.3 0.0 copy-done.10
  19.3 0.6 reshape.34.weights_hbm
  19.9 0.6 collective-permute-done.3.s3
  20.4 0.0 collective-permute-done.1.s1
  20.5 0.0 collective-permute-done.s0
  20.5 0.0 copy-start.17
  20.5 4.5 %collective-permute-done.5.s5 = bf16[6,48,128]{2,1,0:T(8,128)(2,1)S(1)} collective-permute-done((bf16[6,48,128]{2,1,0:T(8,128)(2,1)S(1)}, bf16[6,48,128]{2,1,0:T(8,128)(2,1)S(1)}, u32[]{:S(2)}, u32[]{:S(2)}) %collective-permute-start.5) | collective-permute-done | bytes 73760 | tf_op jit(solution)/shard_map/ppermute | solution.py:449
  25.0 0.2 collective-permute-done.4.s4
  25.1 0.0 copy-done.15
  25.1 0.0 copy-done.18
  25.1 0.5 copy-done.19
  25.6 0.2 copy-done.20
  25.7 23.3 %shard_map.162 = (bf16[48,48,128]{2,1,0:T(8,128)(2,1)}, bf16[48,48,128]{2,1,0:T(8,128)(2,1)}, bf16[6,48,128]{2,1,0:T(8,128)(2,1)}, bf16[6,48,128]{2,1,0:T(8,128)...) custom-call(s32[8]{0:T(128)} %bitcast.16, s32[1]{0:T(128)} %bitcast.1.where, ...), custom_call_target="tpu_custom_call" | custom-call | flops 1811939328 | bytes 4533760 | tf_op jit(solution)/shard_map/pallas_call | solution.py:435
  49.0 1.1 reshape.35
  50.1 23.6 %all_to_all.15 = f32[32,34,128]{2,1,0:T(8,128)S(1)} all-to-all(f32[32,34,128]{2,1,0:T(8,128)S(1)} %reshape.35), channel_id=1, replica_groups=mesh['x_hi'=2,'y'=4,'core'=2,'z'=16,'x_lo'=2] {'x_hi','y','core','x_lo'}, dimensions={0} | all-to-all | bytes 1114112 | tf_op jit(solution)/shard_map/all_to_all | solution.py:548
  73.7 0.1 reduce_sum.18
  73.8 0.7 broadcast_in_dim.36
  74.6 13.7 %all-to-all-start.1 = ((f32[16,34,128]{2,1,0:T(8,128)}), f32[16,34,128]{2,1,0:T(8,128)S(1)}, u32[]{:S(2)}, u32[]{:S(2)}) async-start(f32[16,34,128]{2,1,0:T(8,128)} %broadcast_in_dim.36), calls=%async_computation.1 | async-start | bytes 655360 | tf_op jit(solution)/shard_map/all_to_all | solution.py:459
  88.2 0.0 copy-done.14
  88.2 0.0 copy-start.13
  88.2 1.9 %collective-permute-start.8 = (bf16[6,48,128]{2,1,0:T(8,128)(2,1)S(1)}, bf16[6,48,128]{2,1,0:T(8,128)(2,1)S(1)}, u32[]{:S(2)}, u32[]{:S(2)}) collective-permute-start(bf16[6,48,128]{2,1,0:T(8,128)(2,1)S(1)} %copy-done.14), channel_id=1, source_target_pairs={{0,1},{1,2},{2,3},{3,4},{4,5},{5,6},{6,7},{7,8},{8,9},{9,10},{10,1... | collective-permute-start | bytes 221192 | tf_op jit(solution)/shard_map/ppermute | solution.py:449
  90.2 3.4 %collective-permute-start.7 = (bf16[6,48,128]{2,1,0:T(8,128)(2,1)S(1)}, bf16[6,48,128]{2,1,0:T(8,128)(2,1)S(1)}, u32[]{:S(2)}, u32[]{:S(2)}) collective-permute-start(bf16[6,48,128]{2,1,0:T(8,128)(2,1)S(1)} %copy-done.12), channel_id=1, source_target_pairs={{0,2},{1,3},{2,4},{3,5},{4,6},{5,7},{6,8},{7,9},{8,10},{9,11},{10,... | collective-permute-start | bytes 221192 | tf_op jit(solution)/shard_map/ppermute | solution.py:449
  93.6 5.2 %collective-permute-start.6 = (bf16[6,48,128]{2,1,0:T(8,128)(2,1)S(1)}, bf16[6,48,128]{2,1,0:T(8,128)(2,1)S(1)}, u32[]{:S(2)}, u32[]{:S(2)}) collective-permute-start(bf16[6,48,128]{2,1,0:T(8,128)(2,1)S(1)} %copy-done.12), channel_id=1, source_target_pairs={{0,3},{1,4},{2,5},{3,6},{4,7},{5,8},{6,9},{7,10},{8,11},{9,12},{10... | collective-permute-start | bytes 221192 | tf_op jit(solution)/shard_map/ppermute | solution.py:449
  98.8 0.0 copy-done.11
  98.8 1.3 collective-permute-start.11
  100.1 1.3 collective-permute-start.10
  101.4 0.8 all-to-all-done.1
  102.2 0.0 collective-permute-done.8.s2
  102.2 0.0 copy-done.13
  102.2 0.0 copy-start.4
  102.2 1.3 collective-permute-start.9
  103.5 4.1 %collective-permute-done.9.s3 = bf16[6,48,128]{2,1,0:T(8,128)(2,1)S(1)} collective-permute-done((bf16[6,48,128]{2,1,0:T(8,128)(2,1)S(1)}, bf16[6,48,128]{2,1,0:T(8,128)(2,1)S(1)}, u32[]{:S(2)}, u32[]{:S(2)}) %collective-permute-start.9) | collective-permute-done | bytes 73760 | tf_op jit(solution)/shard_map/ppermute | solution.py:449
  107.6 0.0 collective-permute-done.7.s1
  107.6 0.0 collective-permute-done.6.s0
  107.6 0.0 copy-start.6
  107.6 0.0 collective-permute-done.11.s5
  107.7 0.0 collective-permute-done.10.s4
  107.7 0.8 broadcast_in_dim.37
  108.5 0.0 copy-done.7
  108.5 0.0 copy-done.8
  108.5 0.0 copy-start.3
  108.5 16.4 %all-to-all-start.2 = ((bf16[32,34,128]{2,1,0:T(8,128)(2,1)}), bf16[32,34,128]{2,1,0:T(8,128)(2,1)S(1)}, u32[]{:S(2)}, u32[]{:S(2)}) async-start(bf16[32,34,128]{2,1,0:T(8,128)(2,1)} %broadcast_in_dim.37), calls=%async_computation.2 | async-start | bytes 655360 | tf_op jit(solution)/shard_map/all_to_all | solution.py:459
  124.9 0.0 copy-done.3
  125.0 0.6 rev.3.weights_hbm
  125.6 8.3 %shard_map.163 = bf16[48,48,128]{2,1,0:T(8,128)(2,1)} custom-call(s32[8]{0:T(128)} %bitcast.17, s32[1]{0:T(128)} %bitcast.1.where, bf16[48,48,128]{2,1,0:T(8,128)(2,1)} %get-tuple-element.55.conv_grad_hbm, bf16[6,48,128]{2,1,0:T(8,128)(2,1)} %copy-done.6, bf16[6,48,128]{2,1,0:T(8,128)(2,1)} %copy-done.5, bf16[6,48,128]{2,1,0:T(8,128)(2,1)} %copy-done.4, ...), custom_call_target="tpu_custom_call" | custom-call | flops 28901376 | bytes 2826752 | tf_op jit(solution)/shard_map/pallas_call | solution.py:435
  133.9 0.1 all-to-all-done.2
  134.0 0.1 reshape.36.total
  134.1 0.8 shard_map.164
  135.0 0.6 reshape.37
  (23 shorter events, 0.1 us)
Async XLA Ops:
  0.6 1.2 copy-start.1
  1.5 0.7 copy-start.2
  2.2 0.8 copy-start
  2.2 17.1 %copy-start.10 = (f32[7,7,128]{2,1,0:T(8,128)S(1)}, f32[7,7,128]{2,1,0:T(8,128)}, u32[]{:S(2)}) copy-start(f32[7,7,128]{2,1,0:T(8,128)} %param.14) | copy-start | bytes 75268
  3.0 15.0 %collective-permute-start.2 = (bf16[6,48,128]{2,1,0:T(8,128)(2,1)S(1)}, bf16[6,48,128]{2,1,0:T(8,128)(2,1)S(1)}, u32[]{:S(2)}, u32[]{:S(2)}) collective-permute-start(bf16[6,48,128]{2,1,0:T(8,128)(2,1)S(1)} %get-tuple-element.40), channel_id=1, source_target_pairs={{0,1},{1,2},{2,3},{3,4},{4,5},{5,6},{6,7},{7,8},{8,9},{9,10},{10,1... | collective-permute-start | bytes 221192 | tf_op jit(solution)/shard_map/ppermute | solution.py:449
  6.9 13.5 %collective-permute-start.1 = (bf16[6,48,128]{2,1,0:T(8,128)(2,1)S(1)}, bf16[6,48,128]{2,1,0:T(8,128)(2,1)S(1)}, u32[]{:S(2)}, u32[]{:S(2)}) collective-permute-start(bf16[6,48,128]{2,1,0:T(8,128)(2,1)S(1)} %get-tuple-element.39), channel_id=1, source_target_pairs={{0,2},{1,3},{2,4},{3,5},{4,6},{5,7},{6,8},{7,9},{8,10},{9,11},{10,... | collective-permute-start | bytes 221192 | tf_op jit(solution)/shard_map/ppermute | solution.py:449
  10.5 10.0 %collective-permute-start = (bf16[6,48,128]{2,1,0:T(8,128)(2,1)S(1)}, bf16[6,48,128]{2,1,0:T(8,128)(2,1)S(1)}, u32[]{:S(2)}, u32[]{:S(2)}) collective-permute-start(bf16[6,48,128]{2,1,0:T(8,128)(2,1)S(1)} %get-tuple-element.39), channel_id=1, source_target_pairs={{0,3},{1,4},{2,5},{3,6},{4,7},{5,8},{6,9},{7,10},{8,11},{9,12},{10... | collective-permute-start | bytes 221192 | tf_op jit(solution)/shard_map/ppermute | solution.py:449
  15.3 5.1 %collective-permute-start.3 = (bf16[6,48,128]{2,1,0:T(8,128)(2,1)S(1)}, bf16[6,48,128]{2,1,0:T(8,128)(2,1)S(1)}, u32[]{:S(2)}, u32[]{:S(2)}) collective-permute-start(bf16[6,48,128]{2,1,0:T(8,128)(2,1)S(1)} %get-tuple-element.41), channel_id=1, source_target_pairs={{1,0},{2,1},{3,2},{4,3},{5,4},{6,5},{7,6},{8,7},{9,8},{10,9},{11,1... | collective-permute-start | bytes 221192 | tf_op jit(solution)/shard_map/ppermute | solution.py:449
  16.6 8.3 %collective-permute-start.5 = (bf16[6,48,128]{2,1,0:T(8,128)(2,1)S(1)}, bf16[6,48,128]{2,1,0:T(8,128)(2,1)S(1)}, u32[]{:S(2)}, u32[]{:S(2)}) collective-permute-start(bf16[6,48,128]{2,1,0:T(8,128)(2,1)S(1)} %get-tuple-element.42), channel_id=1, source_target_pairs={{3,0},{4,1},{5,2},{6,3},{7,4},{8,5},{9,6},{10,7},{11,8},{12,9},{13... | collective-permute-start | bytes 221192 | tf_op jit(solution)/shard_map/ppermute | solution.py:449
  18.0 7.2 %copy-start.15 = (bf16[6,48,128]{2,1,0:T(8,128)(2,1)}, bf16[6,48,128]{2,1,0:T(8,128)(2,1)S(1)}, u32[]{:S(2)}) copy-start(bf16[6,48,128]{2,1,0:T(8,128)(2,1)S(1)} %collective-permute-done.2.s2) | copy-start | bytes 221188
  18.0 7.2 %collective-permute-start.4 = (bf16[6,48,128]{2,1,0:T(8,128)(2,1)S(1)}, bf16[6,48,128]{2,1,0:T(8,128)(2,1)S(1)}, u32[]{:S(2)}, u32[]{:S(2)}) collective-permute-start(bf16[6,48,128]{2,1,0:T(8,128)(2,1)S(1)} %get-tuple-element.42), channel_id=1, source_target_pairs={{2,0},{3,1},{4,2},{5,3},{6,4},{7,5},{8,6},{9,7},{10,8},{11,9},{12,... | collective-permute-start | bytes 221192 | tf_op jit(solution)/shard_map/ppermute | solution.py:449
  20.4 4.7 %copy-start.18 = (bf16[6,48,128]{2,1,0:T(8,128)(2,1)}, bf16[6,48,128]{2,1,0:T(8,128)(2,1)S(1)}, u32[]{:S(2)}) copy-start(bf16[6,48,128]{2,1,0:T(8,128)(2,1)S(1)} %collective-permute-done.3.s3) | copy-start | bytes 221188
  20.4 4.7 %copy-start.16 = (bf16[6,48,128]{2,1,0:T(8,128)(2,1)}, bf16[6,48,128]{2,1,0:T(8,128)(2,1)S(1)}, u32[]{:S(2)}) copy-start(bf16[6,48,128]{2,1,0:T(8,128)(2,1)S(1)} %collective-permute-done.1.s1) | copy-start | bytes 221188
  20.5 4.7 %copy-start.17 = (bf16[6,48,128]{2,1,0:T(8,128)(2,1)}, bf16[6,48,128]{2,1,0:T(8,128)(2,1)S(1)}, u32[]{:S(2)}) copy-start(bf16[6,48,128]{2,1,0:T(8,128)(2,1)S(1)} %collective-permute-done.s0) | copy-start | bytes 221188
  25.0 0.6 copy-start.19
  25.1 0.6 copy-start.20
  74.5 13.7 %copy-start.14 = (bf16[6,48,128]{2,1,0:T(8,128)(2,1)S(1)}, bf16[6,48,128]{2,1,0:T(8,128)(2,1)}, u32[]{:S(2)}) copy-start(bf16[6,48,128]{2,1,0:T(8,128)(2,1)} %get-tuple-element.51) | copy-start | bytes 221188
  74.5 15.6 %copy-start.12 = (bf16[6,48,128]{2,1,0:T(8,128)(2,1)S(1)}, bf16[6,48,128]{2,1,0:T(8,128)(2,1)}, u32[]{:S(2)}) copy-start(bf16[6,48,128]{2,1,0:T(8,128)(2,1)} %get-tuple-element.50) | copy-start | bytes 221188
  74.5 24.2 %copy-start.11 = (bf16[6,48,128]{2,1,0:T(8,128)(2,1)S(1)}, bf16[6,48,128]{2,1,0:T(8,128)(2,1)}, u32[]{:S(2)}) copy-start(bf16[6,48,128]{2,1,0:T(8,128)(2,1)} %get-tuple-element.53) | copy-start | bytes 221188
  74.6 27.6 %all-to-all-start.1 = ((f32[16,34,128]{2,1,0:T(8,128)}), f32[16,34,128]{2,1,0:T(8,128)S(1)}, u32[]{:S(2)}, u32[]{:S(2)}) async-start(f32[16,34,128]{2,1,0:T(8,128)} %broadcast_in_dim.36), calls=%async_computation.1 | async-start | bytes 655360 | tf_op jit(solution)/shard_map/all_to_all | solution.py:459
  88.2 14.0 %copy-start.13 = (bf16[6,48,128]{2,1,0:T(8,128)(2,1)S(1)}, bf16[6,48,128]{2,1,0:T(8,128)(2,1)}, u32[]{:S(2)}) copy-start(bf16[6,48,128]{2,1,0:T(8,128)(2,1)} %get-tuple-element.52) | copy-start | bytes 221188
  88.2 14.0 %collective-permute-start.8 = (bf16[6,48,128]{2,1,0:T(8,128)(2,1)S(1)}, bf16[6,48,128]{2,1,0:T(8,128)(2,1)S(1)}, u32[]{:S(2)}, u32[]{:S(2)}) collective-permute-start(bf16[6,48,128]{2,1,0:T(8,128)(2,1)S(1)} %copy-done.14), channel_id=1, source_target_pairs={{0,1},{1,2},{2,3},{3,4},{4,5},{5,6},{6,7},{7,8},{8,9},{9,10},{10,1... | collective-permute-start | bytes 221192 | tf_op jit(solution)/shard_map/ppermute | solution.py:449
  90.2 17.4 %collective-permute-start.7 = (bf16[6,48,128]{2,1,0:T(8,128)(2,1)S(1)}, bf16[6,48,128]{2,1,0:T(8,128)(2,1)S(1)}, u32[]{:S(2)}, u32[]{:S(2)}) collective-permute-start(bf16[6,48,128]{2,1,0:T(8,128)(2,1)S(1)} %copy-done.12), channel_id=1, source_target_pairs={{0,2},{1,3},{2,4},{3,5},{4,6},{5,7},{6,8},{7,9},{8,10},{9,11},{10,... | collective-permute-start | bytes 221192 | tf_op jit(solution)/shard_map/ppermute | solution.py:449
  93.6 14.0 %collective-permute-start.6 = (bf16[6,48,128]{2,1,0:T(8,128)(2,1)S(1)}, bf16[6,48,128]{2,1,0:T(8,128)(2,1)S(1)}, u32[]{:S(2)}, u32[]{:S(2)}) collective-permute-start(bf16[6,48,128]{2,1,0:T(8,128)(2,1)S(1)} %copy-done.12), channel_id=1, source_target_pairs={{0,3},{1,4},{2,5},{3,6},{4,7},{5,8},{6,9},{7,10},{8,11},{9,12},{10... | collective-permute-start | bytes 221192 | tf_op jit(solution)/shard_map/ppermute | solution.py:449
  98.8 8.9 %collective-permute-start.11 = (bf16[6,48,128]{2,1,0:T(8,128)(2,1)S(1)}, bf16[6,48,128]{2,1,0:T(8,128)(2,1)S(1)}, u32[]{:S(2)}, u32[]{:S(2)}) collective-permute-start(bf16[6,48,128]{2,1,0:T(8,128)(2,1)S(1)} %copy-done.11), channel_id=1, source_target_pairs={{3,0},{4,1},{5,2},{6,3},{7,4},{8,5},{9,6},{10,7},{11,8},{12,9},{13... | collective-permute-start | bytes 221192 | tf_op jit(solution)/shard_map/ppermute | solution.py:449
  100.1 7.6 %collective-permute-start.10 = (bf16[6,48,128]{2,1,0:T(8,128)(2,1)S(1)}, bf16[6,48,128]{2,1,0:T(8,128)(2,1)S(1)}, u32[]{:S(2)}, u32[]{:S(2)}) collective-permute-start(bf16[6,48,128]{2,1,0:T(8,128)(2,1)S(1)} %copy-done.11), channel_id=1, source_target_pairs={{2,0},{3,1},{4,2},{5,3},{6,4},{7,5},{8,6},{9,7},{10,8},{11,9},{12,... | collective-permute-start | bytes 221192 | tf_op jit(solution)/shard_map/ppermute | solution.py:449
  102.2 6.3 %copy-start.4 = (bf16[6,48,128]{2,1,0:T(8,128)(2,1)}, bf16[6,48,128]{2,1,0:T(8,128)(2,1)S(1)}, u32[]{:S(2)}) copy-start(bf16[6,48,128]{2,1,0:T(8,128)(2,1)S(1)} %collective-permute-done.8.s2) | copy-start | bytes 221188
  102.2 5.4 %collective-permute-start.9 = (bf16[6,48,128]{2,1,0:T(8,128)(2,1)S(1)}, bf16[6,48,128]{2,1,0:T(8,128)(2,1)S(1)}, u32[]{:S(2)}, u32[]{:S(2)}) collective-permute-start(bf16[6,48,128]{2,1,0:T(8,128)(2,1)S(1)} %copy-done.13), channel_id=1, source_target_pairs={{1,0},{2,1},{3,2},{4,3},{5,4},{6,5},{7,6},{8,7},{9,8},{10,9},{11,1... | collective-permute-start | bytes 221192 | tf_op jit(solution)/shard_map/ppermute | solution.py:449
  107.6 0.9 copy-start.9
  107.6 0.9 copy-start.5
  107.6 0.9 copy-start.6
  107.7 0.8 copy-start.7
  107.7 0.8 copy-start.8
  108.5 16.4 %copy-start.3 = (f32[49,128]{1,0:T(8,128)S(1)}, f32[49,128]{1,0:T(8,128)}, u32[]{:S(2)}) copy-start(f32[49,128]{1,0:T(8,128)} %reshape.34.weights_hbm) | copy-start | bytes 75268
  108.5 25.5 %all-to-all-start.2 = ((bf16[32,34,128]{2,1,0:T(8,128)(2,1)}), bf16[32,34,128]{2,1,0:T(8,128)(2,1)S(1)}, u32[]{:S(2)}, u32[]{:S(2)}) async-start(bf16[32,34,128]{2,1,0:T(8,128)(2,1)} %broadcast_in_dim.37), calls=%async_computation.2 | async-start | bytes 655360 | tf_op jit(solution)/shard_map/all_to_all | solution.py:459

commit v5 on v4

--- a/solution.py
+++ b/solution.py
@@ -25,6 +25,8 @@
 SPACE = ("z", "x_lo")
 PLANE = ("x_hi", "y", "core", "x_lo")
 
+SHARES = 32 * 8
+
 norm_eps = 1e-06
 inv_sqrt_two_pi = 0.3989422804014327
 TAIL_RATE = 0.3889087296526013
@@ -62,7 +64,7 @@
 
     for out, step in ((to_before, -1), (to_after, 1)):
         for direction, first in ((2, 0), (3, TILE - HALO)):
-            source = beside[direction]
+            source = beside[0, direction]
 
             @pl.when((source >= 0) & (source - position == step))
             def _(out=out, first=first):
@@ -117,7 +119,7 @@
         (2, (-1, 1), put_columns(PAD)),
         (3, (-1, 1), put_columns(8 + TILE)),
     ):
-        source = beside[direction]
+        source = beside[0, direction]
         for step in steps:
 
             @pl.when((source >= 0) & (source - position == step))
@@ -125,11 +127,14 @@
                 put(strips[STEPS.index(step)][...])
 
 
-def conv_group(ext, weights, first_row, g):
+def conv_group(ext, weights, first_row, g, reverse=False):
+    def tap(a, b):
+        return (KERNEL - 1 - a, KERNEL - 1 - b) if reverse else (a, b)
+
     sums = [None] * CHUNK
     for b in range(KERNEL):
         taps = [
-            jnp.broadcast_to(weights[a * KERNEL + b : a * KERNEL + b + 1, :], (8, LANES))
+            jnp.broadcast_to(weights[tap(a, b)[0], pl.ds(tap(a, b)[1], 1), :], (8, LANES))
             for a in range(KERNEL)
         ]
         column = PAD + 8 * g + DILATION * b
@@ -143,13 +148,19 @@
     return sums
 
 
-def pack_kernel(beside, where, fields, mask, top, bottom, to_before, to_after, flat):
-    def rows(i, _):
-        cells = pl.ds(pl.multiple_of(i * TILE, TILE), TILE)
-        flat[cells, :] = fields[i].astype(f32) * mask[i].astype(f32)
-        return 0
-
-    lax.fori_loop(0, TILE, rows, 0, unroll=4)
+def pack_kernel(beside, where, land_mask, fields, mask, top, bottom, to_before, to_after, flat):
+    side = (TILE, TILE)
+    diagonal = lax.broadcasted_iota(jnp.int32, side, 0) == lax.broadcasted_iota(jnp.int32, side, 1)
+    by_column = lax.dot_general(
+        land_mask[0].astype(f32).astype(bf16),
+        jnp.where(diagonal, 1.0, 0.0).astype(bf16),
+        (((0,), (0,)), ((), ())),
+        preferred_element_type=f32,
+    )
+    for row in range(TILE):
+        wide = jnp.broadcast_to(by_column[:, row : row + 1], (TILE, LANES))
+        mask[row] = wide.astype(bf16)
+        flat[row * TILE : (row + 1) * TILE, :] = fields[0, 0, row].astype(f32) * wide
     pack_strips(flat, beside, where, top, bottom, to_before, to_after)
 
 
@@ -394,7 +405,7 @@
 
     def chunk(step, _):
         first = pl.multiple_of(step * CHUNK, CHUNK)
-        columns = [conv_group(ext, weights, first, g) for g in range(GROUPS)]
+        columns = [conv_group(ext, weights, first, g, True) for g in range(GROUPS)]
         for row in range(CHUNK):
             at = first + row
             whole = jnp.concatenate([columns[g][row] for g in range(GROUPS)], axis=0)
@@ -413,8 +424,9 @@
         up_grad[:, lanes] = total[q * LANES : (q + 1) * LANES, :].astype(f32)
         down_grad[lanes, :] = total[units + q * LANES : units + (q + 1) * LANES, :].astype(f32)
     at = 2 * units
-    rest = total[at:, :].astype(f32)
-    kernel_grad[...] = rest[0:TAPS]
+    rest = total[at : at + 64, :].astype(f32)
+    for a in range(KERNEL):
+        kernel_grad[a] = rest[a * KERNEL : (a + 1) * KERNEL]
     scale_grad[...] = rest[TAPS : TAPS + 1]
     gain_grad[...] = rest[TAPS + 1 : TAPS + 2]
     for q in range(quarters):
@@ -449,9 +461,9 @@
     return lax.ppermute(value, SPACE, [(source, source + step) for source in range(first, last)])
 
 
-def exchange(top, bottom, to_before, to_after):
+def exchange(top, bottom, to_before, to_after, steps=STEPS):
     sent = {3: bottom, 2: bottom, 1: to_after, -1: to_before, -2: top, -3: top}
-    return [shifted(sent[-step], -step) for step in STEPS]
+    return {step: shifted(sent[-step], -step) for step in steps}
 
 
 def spread(value, axes):
@@ -462,7 +474,7 @@
 def block_call(beside, where, *operands):
     units = operands[10].shape[1]
     quarters = units // LANES
-    sum_rows = -(-(2 * units + TAPS + 2 + quarters) // 64) * 64
+    sum_rows = -(-(2 * units + TAPS + 2 + quarters) // SHARES) * SHARES
     return call(
         block_kernel,
         (beside, where),
@@ -487,7 +499,7 @@
             pltpu.VMEM(WHOLE, bf16),
             pltpu.VMEM(WHOLE, bf16),
             pltpu.VMEM((len(STEPS), *STRIP), bf16),
-            pltpu.VMEM((TAPS, LANES), f32),
+            pltpu.VMEM((KERNEL, KERNEL, LANES), f32),
             pltpu.VMEM(WHOLE, bf16),
             pltpu.VMEM((LANES, units), bf16),
             pltpu.VMEM((units, LANES), bf16),
@@ -511,30 +523,28 @@
     down_weight,
     layer_scale,
 ):
-    beside = neighbours[0]
+    beside = neighbours
     where = lax.axis_index(SPACE).astype(jnp.int32)[None]
     tile, upstream = fields[0, 0], cotangent[0, 0]
-    mask = jnp.broadcast_to(land_mask[0].astype(bf16)[..., None], WHOLE)
-    taps = conv_kernel.reshape(TAPS, LANES)
     units = up_weight.shape[1]
-
-    rims = call(
+    mask, *rims = call(
         pack_kernel,
         (beside, where),
-        (tile, mask),
-        [shape(STRIP)] * 4,
+        (land_mask, fields),
+        [shape(WHOLE)] + [shape(STRIP)] * 4,
         [pltpu.VMEM((TILE * TILE, LANES), f32)],
         TILE * TILE * LANES,
-        SMALL,
+        LARGE,
     )
     strips = exchange(*rims)
+    strips = [strips[step] for step in STEPS]
     block_out, conv_grad, *rims, sums = block_call(
         beside,
         where,
         tile,
         mask,
         *strips,
-        taps,
+        conv_kernel,
         upstream,
         up_weight,
         down_weight,
@@ -546,21 +556,23 @@
     cells = TILE * TILE * lax.axis_size(DP) * lax.axis_size(SPACE)
     part = sums.reshape(lax.axis_size(PLANE), -1, LANES)
     part = jnp.sum(lax.all_to_all(part, PLANE, 0, 0, tiled=True), axis=0)
-    part, rims = lax.optimization_barrier((part, rims))
-    strips = exchange(*rims)
+    near = exchange(*rims, steps=(-1, 1))
+    part, rims, near = lax.optimization_barrier((part, rims, near))
+    far = exchange(*rims, steps=(-3, -2, 2, 3))
     part = jnp.sum(spread(part, "z"), axis=0) * (1.0 / math.sqrt(cells))
-    part, strips = lax.optimization_barrier((part, strips))
+    part, far = lax.optimization_barrier((part, far))
+    strips = [{**near, **far}[step] for step in STEPS]
     total = spread(part.astype(bf16), PLANE).reshape(sum_rows, LANES)
     (fields_grad,) = call(
         back_kernel,
         (beside, where),
-        (conv_grad, *strips, taps[::-1], mask, upstream),
+        (conv_grad, *strips, conv_kernel, mask, upstream),
         [shape(WHOLE)],
         [
             pltpu.VMEM((EXT_ROWS, EXT_COLS, LANES), f32),
             pltpu.VMEM(WHOLE, bf16),
             pltpu.VMEM((len(STEPS), *STRIP), bf16),
-            pltpu.VMEM((TAPS, LANES), f32),
+            pltpu.VMEM((KERNEL, KERNEL, LANES), f32),
             pltpu.VMEM(WHOLE, bf16),
             pltpu.VMEM(WHOLE, bf16),
             pltpu.SemaphoreType.DMA((10,)),
@@ -575,7 +587,7 @@
         (),
         (total,),
         [
-            shape((TAPS, LANES), f32),
+            shape((KERNEL, KERNEL, LANES), f32),
             shape((1, LANES), f32),
             shape((LANES, units), f32),
             shape((1, units), f32),
@@ -589,7 +601,7 @@
     return (
         block_out[None, None],
         fields_grad[None, None],
-        kernel_grad.reshape(KERNEL, KERNEL, LANES),
+        kernel_grad,
         gain_grad[0],
         up_grad,
         bias_grad[0],

time: 136 us -> 130 us (0.956)
  blocking collectives: 23.6 us -> 0 us
  waiting for transfers between devices: 10.2 us -> 24.9 us
  starting transfers between devices: 60.7 us -> 66.3 us
  local copies, waits for them, and re-layouts: 5.95 us -> 2.18 us
  Pallas kernels: 33.2 us -> 35.1 us
    all_to_all x1 -> x0, blocking collectives: 23.6 us -> none  [local(): part = jnp.sum(lax.all_to_all(part, PLANE, 0, 0, tiled=True), axis=0)]
    all_to_all x0 -> x1, starting transfers between devices: none -> 11.9 us  [local(): part = jnp.sum(lax.all_to_all(part, PLANE, 0, 0, tiled=True), axis=0)]
    all_to_all x0 -> x1, waiting for transfers between devices: none -> 8.31 us  [local(): part = jnp.sum(lax.all_to_all(part, PLANE, 0, 0, tiled=True), axis=0)]
    all_to_all x2, waiting for transfers between devices: 0.93 us -> 6.66 us  [spread(): return lax.all_to_all(copies, axes, 0, 0, tiled=True)]
    all_to_all x2, starting transfers between devices: 30.1 us -> 25.1 us  [spread(): return lax.all_to_all(copies, axes, 0, 0, tiled=True)]
    reshape x4 -> x0, local copies, waits for them, and re-layouts: 2.41 us -> none  [the longest x1 1.1 us: local(): part = sums.reshape(lax.axis_size(PLANE), -1, LANES)]
    pallas_call x4, Pallas kernels: 33.2 us -> 35.1 us  [call(): pl.pallas_call(kernel, out_shape=outs, in_specs=[SMEM] * len(scalars) + (...]
  transfers between devices with their start and end apart: 14 -> 15, of which waited for: 6 -> 9; matrix products, arithmetic and copies ran while one was open for 1% -> 0% of each run, Pallas kernels for 6% -> 6%
where the time goes in v5:
time: 130 us
  starting transfers between devices  66.3 us (51%)
  Pallas kernels  35.1 us (27%)
  waiting for transfers between devices  24.9 us (19%)
  local copies, waits for them, and re-layouts  2.18 us (2%)
    pallas_call x4, Pallas kernels, call(): pl.pallas_call(kernel, out_shape=outs, in_specs=[SMEM] * len(scalars) + (...  35.1 us
    ppermute x12, starting transfers between devices, shifted(): lax.ppermute(value, SPACE, [(source, source + step) for source in range(f...  29.3 us
    all_to_all x2, starting transfers between devices, spread(): return lax.all_to_all(copies, axes, 0, 0, tiled=True)  25.1 us
    all_to_all x1, starting transfers between devices, local(): part = jnp.sum(lax.all_to_all(part, PLANE, 0, 0, tiled=True), axis=0)  11.9 us
    ppermute x12, waiting for transfers between devices, shifted(): lax.ppermute(value, SPACE, [(source, source + step) for source in range(f...  9.97 us
    all_to_all x1, waiting for transfers between devices, local(): part = jnp.sum(lax.all_to_all(part, PLANE, 0, 0, tiled=True), axis=0)  8.31 us
    all_to_all x2, waiting for transfers between devices, spread(): return lax.all_to_all(copies, axes, 0, 0, tiled=True)  6.66 us
  transfers between devices with their start and end apart: 15, of which 9 were waited for; matrix products, arithmetic and copies ran while one was open for 0% of the time, Pallas kernels for 6%

profile of v5, /device:TPU:1, one launch (start us, length us, event | category | flops | bytes accessed | tf_op | source)
XLA Modules:
  0.0 129.6 jit_solution(9581672230595466339)
XLA Ops:
  0.6 2.7 %shard_map.161 = (bf16[48,48,128]{2,1,0:T(8,128)(2,1)}, bf16[6,48,128]{2,1,0:T(8,128)(2,1)}, bf16[6,48,128]{2,1,0:T(8,128)(2,1)}, bf16[6,48,128]{2,1,0:T(8,128)(2,1)}, bf16[6,48,128]{2,1,0:T(8,128)(2,1)}) custom-call(s32[1,8]{1,0:T(1,128)} %beside.5, s32[1]{0:T(128)} %bitcast.where, s32[1,48,48]{2,1,0:T(8,128)} %land_mask.1, bf16[1,1,48,48,128]{4,3,2,1,0:T(8,128)(2,1)} %fields.1), custom_call_target="tpu_custom_call" | custom-call | flops 294912 | bytes 1483776 | tf_op jit(solution)/shard_map/pallas_call | solution.py:447
  3.4 3.9 %collective-permute-start.2 = (bf16[6,48,128]{2,1,0:T(8,128)(2,1)}, bf16[6,48,128]{2,1,0:T(8,128)(2,1)S(1)}, u32[]{:S(2)}, u32[]{:S(2)}) collective-permute-start(bf16[6,48,128]{2,1,0:T(8,128)(2,1)} %get-tuple-element.40), channel_id=1, source_target_pairs={{0,1},{1,2},{2,3},{3,4},{4,5},{5,6},{6,7},{7,8},{8,9},{9,10},{10,1... | collective-permute-start | bytes 221192 | tf_op jit(solution)/shard_map/ppermute | solution.py:461
  7.3 3.5 %collective-permute-start.1 = (bf16[6,48,128]{2,1,0:T(8,128)(2,1)}, bf16[6,48,128]{2,1,0:T(8,128)(2,1)S(1)}, u32[]{:S(2)}, u32[]{:S(2)}) collective-permute-start(bf16[6,48,128]{2,1,0:T(8,128)(2,1)} %get-tuple-element.39), channel_id=1, source_target_pairs={{0,2},{1,3},{2,4},{3,5},{4,6},{5,7},{6,8},{7,9},{8,10},{9,11},{10,... | collective-permute-start | bytes 221192 | tf_op jit(solution)/shard_map/ppermute | solution.py:461
  10.8 4.9 %collective-permute-start = (bf16[6,48,128]{2,1,0:T(8,128)(2,1)}, bf16[6,48,128]{2,1,0:T(8,128)(2,1)S(1)}, u32[]{:S(2)}, u32[]{:S(2)}) collective-permute-start(bf16[6,48,128]{2,1,0:T(8,128)(2,1)} %get-tuple-element.39), channel_id=1, source_target_pairs={{0,3},{1,4},{2,5},{3,6},{4,7},{5,8},{6,9},{7,10},{8,11},{9,12},{10... | collective-permute-start | bytes 221192 | tf_op jit(solution)/shard_map/ppermute | solution.py:461
  15.7 1.3 collective-permute-start.3
  17.0 1.3 collective-permute-start.5
  18.3 0.0 collective-permute-done.2.s2
  18.3 0.0 copy-start.8
  18.3 1.3 collective-permute-start.4
  19.6 1.4 %collective-permute-done.3.s3 = bf16[6,48,128]{2,1,0:T(8,128)(2,1)S(1)} collective-permute-done((bf16[6,48,128]{2,1,0:T(8,128)(2,1)}, bf16[6,48,128]{2,1,0:T(8,128)(2,1)S(1)}, u32[]{:S(2)}, u32[]{:S(2)}) %collective-permute-start.3) | collective-permute-done | bytes 73760 | tf_op jit(solution)/shard_map/ppermute | solution.py:461
  21.0 0.0 copy-start.11
  21.0 0.0 collective-permute-done.1.s1
  21.0 0.0 copy-start.9
  21.0 0.0 collective-permute-done.s0
  21.0 0.0 copy-start.10
  21.0 4.5 %collective-permute-done.5.s5 = bf16[6,48,128]{2,1,0:T(8,128)(2,1)S(1)} collective-permute-done((bf16[6,48,128]{2,1,0:T(8,128)(2,1)}, bf16[6,48,128]{2,1,0:T(8,128)(2,1)S(1)}, u32[]{:S(2)}, u32[]{:S(2)}) %collective-permute-start.5) | collective-permute-done | bytes 73760 | tf_op jit(solution)/shard_map/ppermute | solution.py:461
  25.5 0.0 copy-start.12
  25.5 0.2 collective-permute-done.4.s4
  25.7 0.0 copy-start.14
  25.7 0.0 copy-done.8
  25.7 0.0 copy-done.11
  25.7 0.0 copy-done.9
  25.7 0.0 copy-done.10
  25.7 0.4 copy-done.12
  26.2 0.2 copy-done.14
  26.3 23.2 %shard_map.162 = (bf16[48,48,128]{2,1,0:T(8,128)(2,1)}, bf16[48,48,128]{2,1,0:T(8,128)(2,1)}, bf16[6,48,128]{2,1,0:T(8,128)(2,1)}, bf16[6,48,128]{2,1,0:T(8,128)...) custom-call(s32[1,8]{1,0:T(1,128)} %beside.5, s32[1]{0:T(128)} %bitcast.where, ...), custom_call_target="tpu_custom_call" | custom-call | flops 1811939328 | bytes 4632064 | tf_op jit(solution)/shard_map/pallas_call | solution.py:447
  49.6 0.0 copy-start.15
  49.6 0.0 copy-start.13
  49.6 11.9 %all-to-all-start = ((f32[32,40,128]{2,1,0:T(8,128)}), f32[32,40,128]{2,1,0:T(8,128)S(1)}, u32[]{:S(2)}, u32[]{:S(2)}) async-start(f32[32,40,128]{2,1,0:T(8,128)} %bitcast.14), calls=%async_computation | async-start | bytes 1310720 | tf_op jit(solution)/shard_map/all_to_all | solution.py:558
  61.5 0.0 copy-done.15
  61.5 1.3 collective-permute-start.7
  62.8 0.0 copy-done.13
  62.8 4.0 %collective-permute-start.6 = (bf16[6,48,128]{2,1,0:T(8,128)(2,1)S(1)}, bf16[6,48,128]{2,1,0:T(8,128)(2,1)S(1)}, u32[]{:S(2)}, u32[]{:S(2)}) collective-permute-start(bf16[6,48,128]{2,1,0:T(8,128)(2,1)S(1)} %copy-done.13), channel_id=1, source_target_pairs={{0,1},{1,2},{2,3},{3,4},{4,5},{5,6},{6,7},{7,8},{8,9},{9,10},{10,1... | collective-permute-start | bytes 221192 | tf_op jit(solution)/shard_map/ppermute | solution.py:461
  66.8 8.3 %all-to-all-done = f32[32,40,128]{2,1,0:T(8,128)S(1)} async-done(((f32[32,40,128]{2,1,0:T(8,128)}), f32[32,40,128]{2,1,0:T(8,128)S(1)}, u32[]{:S(2)}, u32[]{:S(2)}) %all-to-all-start) | async-done | bytes 655392 | tf_op jit(solution)/shard_map/all_to_all | solution.py:558
  75.1 0.1 reduce_sum.18
  75.2 0.0 collective-permute-done.7.s3
  75.2 0.0 copy-start
  75.2 0.0 collective-permute-done.6.s2
  75.2 0.0 copy-start.1
  75.2 0.7 broadcast_in_dim.29
  76.0 0.0 copy-done
  76.0 0.0 copy-done.1
  76.0 13.7 %all-to-all-start.1 = ((f32[16,40,128]{2,1,0:T(8,128)}), f32[16,40,128]{2,1,0:T(8,128)S(1)}, u32[]{:S(2)}, u32[]{:S(2)}) async-start(f32[16,40,128]{2,1,0:T(8,128)} %broadcast_in_dim.29), calls=%async_computation.1 | async-start | bytes 655360 | tf_op jit(solution)/shard_map/all_to_all | solution.py:471
  89.7 0.0 copy-done.7
  89.7 3.3 %collective-permute-start.9 = (bf16[6,48,128]{2,1,0:T(8,128)(2,1)S(1)}, bf16[6,48,128]{2,1,0:T(8,128)(2,1)S(1)}, u32[]{:S(2)}, u32[]{:S(2)}) collective-permute-start(bf16[6,48,128]{2,1,0:T(8,128)(2,1)S(1)} %copy-done.7), channel_id=1, source_target_pairs={{0,2},{1,3},{2,4},{3,5},{4,6},{5,7},{6,8},{7,9},{8,10},{9,11},{10,... | collective-permute-start | bytes 221192 | tf_op jit(solution)/shard_map/ppermute | solution.py:461
  92.9 2.0 %collective-permute-start.8 = (bf16[6,48,128]{2,1,0:T(8,128)(2,1)S(1)}, bf16[6,48,128]{2,1,0:T(8,128)(2,1)S(1)}, u32[]{:S(2)}, u32[]{:S(2)}) collective-permute-start(bf16[6,48,128]{2,1,0:T(8,128)(2,1)S(1)} %copy-done.7), channel_id=1, source_target_pairs={{0,3},{1,4},{2,5},{3,6},{4,7},{5,8},{6,9},{7,10},{8,11},{9,12},{10... | collective-permute-start | bytes 221192 | tf_op jit(solution)/shard_map/ppermute | solution.py:461
  94.9 0.0 copy-done.6
  95.0 1.3 collective-permute-start.11
  96.3 1.3 collective-permute-start.10
  97.6 5.9 %all-to-all-done.1 = f32[16,40,128]{2,1,0:T(8,128)S(1)} async-done(((f32[16,40,128]{2,1,0:T(8,128)}), f32[16,40,128]{2,1,0:T(8,128)S(1)}, u32[]{:S(2)}, u32[]{:S(2)}) %all-to-all-start.1) | async-done | bytes 327712 | tf_op jit(solution)/shard_map/all_to_all | solution.py:471
  103.5 0.0 collective-permute-done.9.s1
  103.5 0.0 copy-start.2
  103.5 1.6 %collective-permute-done.8.s0 = bf16[6,48,128]{2,1,0:T(8,128)(2,1)S(1)} collective-permute-done((bf16[6,48,128]{2,1,0:T(8,128)(2,1)S(1)}, bf16[6,48,128]{2,1,0:T(8,128)(2,1)S(1)}, u32[]{:S(2)}, u32[]{:S(2)}) %collective-permute-start.8) | collective-permute-done | bytes 73760 | tf_op jit(solution)/shard_map/ppermute | solution.py:461
  105.1 0.6 collective-permute-done.11.s5
  105.7 1.7 %collective-permute-done.10.s4 = bf16[6,48,128]{2,1,0:T(8,128)(2,1)S(1)} collective-permute-done((bf16[6,48,128]{2,1,0:T(8,128)(2,1)S(1)}, bf16[6,48,128]{2,1,0:T(8,128)(2,1)S(1)}, u32[]{:S(2)}, u32[]{:S(2)}) %collective-permute-start.10) | collective-permute-done | bytes 73760 | tf_op jit(solution)/shard_map/ppermute | solution.py:461
  107.4 0.8 broadcast_in_dim.30
  108.2 0.0 copy-done.2
  108.2 0.0 copy-done.3
  108.2 0.0 copy-done.4
  108.2 0.0 copy-done.5
  108.2 11.4 %all-to-all-start.2 = ((bf16[32,40,128]{2,1,0:T(8,128)(2,1)}), bf16[32,40,128]{2,1,0:T(8,128)(2,1)S(1)}, u32[]{:S(2)}, u32[]{:S(2)}) async-start(bf16[32,40,128]{2,1,0:T(8,128)(2,1)} %broadcast_in_dim.30), calls=%async_computation.2 | async-start | bytes 655360 | tf_op jit(solution)/shard_map/all_to_all | solution.py:471
  119.6 8.3 %shard_map.163 = bf16[48,48,128]{2,1,0:T(8,128)(2,1)} custom-call(s32[1,8]{1,0:T(1,128)} %beside.5, s32[1]{0:T(128)} %bitcast.where, bf16[48,48,128]{2,1,0:T(8,128)(2,1)} %get-tuple-element.53.conv_grad_hbm, bf16[6,48,128]{2,1,0:T(8,128)(2,1)} %copy-done.3, bf16[6,48,128]{2,1,0:T(8,128)(2,1)} %copy-done.2, bf16[6,48,128]{2,1,0:T(8,128)(2,1)} %copy-done.1, ...), custom_call_target="tpu_custom_call" | custom-call | flops 28901376 | bytes 2826752 | tf_op jit(solution)/shard_map/pallas_call | solution.py:447
  127.9 0.8 all-to-all-done.2
  128.7 0.8 shard_map.164
  (7 shorter events, 0.0 us)
Async XLA Ops:
  3.4 14.9 %collective-permute-start.2 = (bf16[6,48,128]{2,1,0:T(8,128)(2,1)}, bf16[6,48,128]{2,1,0:T(8,128)(2,1)S(1)}, u32[]{:S(2)}, u32[]{:S(2)}) collective-permute-start(bf16[6,48,128]{2,1,0:T(8,128)(2,1)} %get-tuple-element.40), channel_id=1, source_target_pairs={{0,1},{1,2},{2,3},{3,4},{4,5},{5,6},{6,7},{7,8},{8,9},{9,10},{10,1... | collective-permute-start | bytes 221192 | tf_op jit(solution)/shard_map/ppermute | solution.py:461
  7.3 13.7 %collective-permute-start.1 = (bf16[6,48,128]{2,1,0:T(8,128)(2,1)}, bf16[6,48,128]{2,1,0:T(8,128)(2,1)S(1)}, u32[]{:S(2)}, u32[]{:S(2)}) collective-permute-start(bf16[6,48,128]{2,1,0:T(8,128)(2,1)} %get-tuple-element.39), channel_id=1, source_target_pairs={{0,2},{1,3},{2,4},{3,5},{4,6},{5,7},{6,8},{7,9},{8,10},{9,11},{10,... | collective-permute-start | bytes 221192 | tf_op jit(solution)/shard_map/ppermute | solution.py:461
  10.8 10.2 %collective-permute-start = (bf16[6,48,128]{2,1,0:T(8,128)(2,1)}, bf16[6,48,128]{2,1,0:T(8,128)(2,1)S(1)}, u32[]{:S(2)}, u32[]{:S(2)}) collective-permute-start(bf16[6,48,128]{2,1,0:T(8,128)(2,1)} %get-tuple-element.39), channel_id=1, source_target_pairs={{0,3},{1,4},{2,5},{3,6},{4,7},{5,8},{6,9},{7,10},{8,11},{9,12},{10... | collective-permute-start | bytes 221192 | tf_op jit(solution)/shard_map/ppermute | solution.py:461
  15.7 5.3 %collective-permute-start.3 = (bf16[6,48,128]{2,1,0:T(8,128)(2,1)}, bf16[6,48,128]{2,1,0:T(8,128)(2,1)S(1)}, u32[]{:S(2)}, u32[]{:S(2)}) collective-permute-start(bf16[6,48,128]{2,1,0:T(8,128)(2,1)} %get-tuple-element.41), channel_id=1, source_target_pairs={{1,0},{2,1},{3,2},{4,3},{5,4},{6,5},{7,6},{8,7},{9,8},{10,9},{11,1... | collective-permute-start | bytes 221192 | tf_op jit(solution)/shard_map/ppermute | solution.py:461
  17.0 8.5 %collective-permute-start.5 = (bf16[6,48,128]{2,1,0:T(8,128)(2,1)}, bf16[6,48,128]{2,1,0:T(8,128)(2,1)S(1)}, u32[]{:S(2)}, u32[]{:S(2)}) collective-permute-start(bf16[6,48,128]{2,1,0:T(8,128)(2,1)} %get-tuple-element.42), channel_id=1, source_target_pairs={{3,0},{4,1},{5,2},{6,3},{7,4},{8,5},{9,6},{10,7},{11,8},{12,9},{13... | collective-permute-start | bytes 221192 | tf_op jit(solution)/shard_map/ppermute | solution.py:461
  18.3 7.4 %copy-start.8 = (bf16[6,48,128]{2,1,0:T(8,128)(2,1)}, bf16[6,48,128]{2,1,0:T(8,128)(2,1)S(1)}, u32[]{:S(2)}) copy-start(bf16[6,48,128]{2,1,0:T(8,128)(2,1)S(1)} %collective-permute-done.2.s2) | copy-start | bytes 221188
  18.3 7.4 %collective-permute-start.4 = (bf16[6,48,128]{2,1,0:T(8,128)(2,1)}, bf16[6,48,128]{2,1,0:T(8,128)(2,1)S(1)}, u32[]{:S(2)}, u32[]{:S(2)}) collective-permute-start(bf16[6,48,128]{2,1,0:T(8,128)(2,1)} %get-tuple-element.42), channel_id=1, source_target_pairs={{2,0},{3,1},{4,2},{5,3},{6,4},{7,5},{8,6},{9,7},{10,8},{11,9},{12,... | collective-permute-start | bytes 221192 | tf_op jit(solution)/shard_map/ppermute | solution.py:461
  21.0 4.7 %copy-start.11 = (bf16[6,48,128]{2,1,0:T(8,128)(2,1)}, bf16[6,48,128]{2,1,0:T(8,128)(2,1)S(1)}, u32[]{:S(2)}) copy-start(bf16[6,48,128]{2,1,0:T(8,128)(2,1)S(1)} %collective-permute-done.3.s3) | copy-start | bytes 221188
  21.0 4.7 %copy-start.9 = (bf16[6,48,128]{2,1,0:T(8,128)(2,1)}, bf16[6,48,128]{2,1,0:T(8,128)(2,1)S(1)}, u32[]{:S(2)}) copy-start(bf16[6,48,128]{2,1,0:T(8,128)(2,1)S(1)} %collective-permute-done.1.s1) | copy-start | bytes 221188
  21.0 4.7 %copy-start.10 = (bf16[6,48,128]{2,1,0:T(8,128)(2,1)}, bf16[6,48,128]{2,1,0:T(8,128)(2,1)S(1)}, u32[]{:S(2)}) copy-start(bf16[6,48,128]{2,1,0:T(8,128)(2,1)S(1)} %collective-permute-done.s0) | copy-start | bytes 221188
  25.5 0.6 copy-start.12
  25.7 0.6 copy-start.14
  49.6 11.9 %copy-start.15 = (bf16[6,48,128]{2,1,0:T(8,128)(2,1)S(1)}, bf16[6,48,128]{2,1,0:T(8,128)(2,1)}, u32[]{:S(2)}) copy-start(bf16[6,48,128]{2,1,0:T(8,128)(2,1)} %get-tuple-element.47) | copy-start | bytes 221188
  49.6 13.2 %copy-start.13 = (bf16[6,48,128]{2,1,0:T(8,128)(2,1)S(1)}, bf16[6,48,128]{2,1,0:T(8,128)(2,1)}, u32[]{:S(2)}) copy-start(bf16[6,48,128]{2,1,0:T(8,128)(2,1)} %get-tuple-element.48) | copy-start | bytes 221188
  49.6 25.5 %all-to-all-start = ((f32[32,40,128]{2,1,0:T(8,128)}), f32[32,40,128]{2,1,0:T(8,128)S(1)}, u32[]{:S(2)}, u32[]{:S(2)}) async-start(f32[32,40,128]{2,1,0:T(8,128)} %bitcast.14), calls=%async_computation | async-start | bytes 1310720 | tf_op jit(solution)/shard_map/all_to_all | solution.py:558
  61.5 13.7 %collective-permute-start.7 = (bf16[6,48,128]{2,1,0:T(8,128)(2,1)S(1)}, bf16[6,48,128]{2,1,0:T(8,128)(2,1)S(1)}, u32[]{:S(2)}, u32[]{:S(2)}) collective-permute-start(bf16[6,48,128]{2,1,0:T(8,128)(2,1)S(1)} %copy-done.15), channel_id=1, source_target_pairs={{1,0},{2,1},{3,2},{4,3},{5,4},{6,5},{7,6},{8,7},{9,8},{10,9},{11,1... | collective-permute-start | bytes 221192 | tf_op jit(solution)/shard_map/ppermute | solution.py:461
  62.8 12.4 %collective-permute-start.6 = (bf16[6,48,128]{2,1,0:T(8,128)(2,1)S(1)}, bf16[6,48,128]{2,1,0:T(8,128)(2,1)S(1)}, u32[]{:S(2)}, u32[]{:S(2)}) collective-permute-start(bf16[6,48,128]{2,1,0:T(8,128)(2,1)S(1)} %copy-done.13), channel_id=1, source_target_pairs={{0,1},{1,2},{2,3},{3,4},{4,5},{5,6},{6,7},{7,8},{8,9},{9,10},{10,1... | collective-permute-start | bytes 221192 | tf_op jit(solution)/shard_map/ppermute | solution.py:461
  75.2 0.8 copy-start
  75.2 0.8 copy-start.1
  76.0 13.7 %copy-start.7 = (bf16[6,48,128]{2,1,0:T(8,128)(2,1)S(1)}, bf16[6,48,128]{2,1,0:T(8,128)(2,1)}, u32[]{:S(2)}) copy-start(bf16[6,48,128]{2,1,0:T(8,128)(2,1)} %get-tuple-element.50) | copy-start | bytes 221188
  76.0 19.0 %copy-start.6 = (bf16[6,48,128]{2,1,0:T(8,128)(2,1)S(1)}, bf16[6,48,128]{2,1,0:T(8,128)(2,1)}, u32[]{:S(2)}) copy-start(bf16[6,48,128]{2,1,0:T(8,128)(2,1)} %get-tuple-element.51) | copy-start | bytes 221188
  76.0 27.5 %all-to-all-start.1 = ((f32[16,40,128]{2,1,0:T(8,128)}), f32[16,40,128]{2,1,0:T(8,128)S(1)}, u32[]{:S(2)}, u32[]{:S(2)}) async-start(f32[16,40,128]{2,1,0:T(8,128)} %broadcast_in_dim.29), calls=%async_computation.1 | async-start | bytes 655360 | tf_op jit(solution)/shard_map/all_to_all | solution.py:471
  89.7 13.8 %collective-permute-start.9 = (bf16[6,48,128]{2,1,0:T(8,128)(2,1)S(1)}, bf16[6,48,128]{2,1,0:T(8,128)(2,1)S(1)}, u32[]{:S(2)}, u32[]{:S(2)}) collective-permute-start(bf16[6,48,128]{2,1,0:T(8,128)(2,1)S(1)} %copy-done.7), channel_id=1, source_target_pairs={{0,2},{1,3},{2,4},{3,5},{4,6},{5,7},{6,8},{7,9},{8,10},{9,11},{10,... | collective-permute-start | bytes 221192 | tf_op jit(solution)/shard_map/ppermute | solution.py:461
  92.9 12.1 %collective-permute-start.8 = (bf16[6,48,128]{2,1,0:T(8,128)(2,1)S(1)}, bf16[6,48,128]{2,1,0:T(8,128)(2,1)S(1)}, u32[]{:S(2)}, u32[]{:S(2)}) collective-permute-start(bf16[6,48,128]{2,1,0:T(8,128)(2,1)S(1)} %copy-done.7), channel_id=1, source_target_pairs={{0,3},{1,4},{2,5},{3,6},{4,7},{5,8},{6,9},{7,10},{8,11},{9,12},{10... | collective-permute-start | bytes 221192 | tf_op jit(solution)/shard_map/ppermute | solution.py:461
  95.0 10.7 %collective-permute-start.11 = (bf16[6,48,128]{2,1,0:T(8,128)(2,1)S(1)}, bf16[6,48,128]{2,1,0:T(8,128)(2,1)S(1)}, u32[]{:S(2)}, u32[]{:S(2)}) collective-permute-start(bf16[6,48,128]{2,1,0:T(8,128)(2,1)S(1)} %copy-done.6), channel_id=1, source_target_pairs={{3,0},{4,1},{5,2},{6,3},{7,4},{8,5},{9,6},{10,7},{11,8},{12,9},{13... | collective-permute-start | bytes 221192 | tf_op jit(solution)/shard_map/ppermute | solution.py:461
  96.3 11.1 %collective-permute-start.10 = (bf16[6,48,128]{2,1,0:T(8,128)(2,1)S(1)}, bf16[6,48,128]{2,1,0:T(8,128)(2,1)S(1)}, u32[]{:S(2)}, u32[]{:S(2)}) collective-permute-start(bf16[6,48,128]{2,1,0:T(8,128)(2,1)S(1)} %copy-done.6), channel_id=1, source_target_pairs={{2,0},{3,1},{4,2},{5,3},{6,4},{7,5},{8,6},{9,7},{10,8},{11,9},{12,... | collective-permute-start | bytes 221192 | tf_op jit(solution)/shard_map/ppermute | solution.py:461
  103.5 4.7 %copy-start.2 = (bf16[6,48,128]{2,1,0:T(8,128)(2,1)}, bf16[6,48,128]{2,1,0:T(8,128)(2,1)S(1)}, u32[]{:S(2)}) copy-start(bf16[6,48,128]{2,1,0:T(8,128)(2,1)S(1)} %collective-permute-done.9.s1) | copy-start | bytes 221188
  105.1 3.1 %copy-start.3 = (bf16[6,48,128]{2,1,0:T(8,128)(2,1)}, bf16[6,48,128]{2,1,0:T(8,128)(2,1)S(1)}, u32[]{:S(2)}) copy-start(bf16[6,48,128]{2,1,0:T(8,128)(2,1)S(1)} %collective-permute-done.8.s0) | copy-start | bytes 221188
  105.7 2.5 %copy-start.4 = (bf16[6,48,128]{2,1,0:T(8,128)(2,1)}, bf16[6,48,128]{2,1,0:T(8,128)(2,1)S(1)}, u32[]{:S(2)}) copy-start(bf16[6,48,128]{2,1,0:T(8,128)(2,1)S(1)} %collective-permute-done.11.s5) | copy-start | bytes 221188
  107.4 0.8 copy-start.5
  108.2 20.5 %all-to-all-start.2 = ((bf16[32,40,128]{2,1,0:T(8,128)(2,1)}), bf16[32,40,128]{2,1,0:T(8,128)(2,1)S(1)}, u32[]{:S(2)}, u32[]{:S(2)}) async-start(bf16[32,40,128]{2,1,0:T(8,128)(2,1)} %broadcast_in_dim.30), calls=%async_computation.2 | async-start | bytes 655360 | tf_op jit(solution)/shard_map/all_to_all | solution.py:471

commit v6 on v5

--- a/solution.py
+++ b/solution.py
@@ -556,10 +556,10 @@
     cells = TILE * TILE * lax.axis_size(DP) * lax.axis_size(SPACE)
     part = sums.reshape(lax.axis_size(PLANE), -1, LANES)
     part = jnp.sum(lax.all_to_all(part, PLANE, 0, 0, tiled=True), axis=0)
-    near = exchange(*rims, steps=(-1, 1))
+    near = exchange(*rims, steps=(-2, -1, 1))
     part, rims, near = lax.optimization_barrier((part, rims, near))
-    far = exchange(*rims, steps=(-3, -2, 2, 3))
-    part = jnp.sum(spread(part, "z"), axis=0) * (1.0 / math.sqrt(cells))
+    far = exchange(*rims, steps=(-3, 2, 3))
+    part = jnp.sum(spread(part.astype(bf16), "z").astype(f32), axis=0) * (1.0 / math.sqrt(cells))
     part, far = lax.optimization_barrier((part, far))
     strips = [{**near, **far}[step] for step in STEPS]
     total = spread(part.astype(bf16), PLANE).reshape(sum_rows, LANES)

time: 130 us -> 126 us (0.969)
  waiting for transfers between devices: 24.9 us -> 13.9 us
  starting transfers between devices: 66.3 us -> 73 us
    all_to_all x1, waiting for transfers between devices: 8.31 us -> 3.06 us  [local(): part = jnp.sum(lax.all_to_all(part, PLANE, 0, 0, tiled=True), axis=0)]
    ppermute x12, starting transfers between devices: 29.3 us -> 33.3 us  [shifted(): lax.ppermute(value, SPACE, [(source, source + step) for source in range(f...]
    ppermute x12, waiting for transfers between devices: 9.97 us -> 6.04 us  [shifted(): lax.ppermute(value, SPACE, [(source, source + step) for source in range(f...]
    all_to_all x2, starting transfers between devices: 25.1 us -> 27.9 us  [spread(): return lax.all_to_all(copies, axes, 0, 0, tiled=True)]
    all_to_all x2, waiting for transfers between devices: 6.66 us -> 4.8 us  [spread(): return lax.all_to_all(copies, axes, 0, 0, tiled=True)]
  transfers between devices with their start and end apart: 15 -> 15, of which waited for: 9 -> 6; matrix products, arithmetic and copies ran while one was open for 0% -> 0% of each run, Pallas kernels for 6% -> 7%
where the time goes in v6:
time: 126 us; the launch traced here: 125 us
  starting transfers between devices  73 us (58%)
  Pallas kernels  35.1 us (28%)
  waiting for transfers between devices  13.9 us (11%)
  local copies, waits for them, and re-layouts  2.17 us (2%)
    pallas_call x4, Pallas kernels, call(): pl.pallas_call(kernel, out_shape=outs, in_specs=[SMEM] * len(scalars) + (...  35.1 us
    ppermute x12, starting transfers between devices, shifted(): lax.ppermute(value, SPACE, [(source, source + step) for source in range(f...  33.3 us
    all_to_all x2, starting transfers between devices, spread(): return lax.all_to_all(copies, axes, 0, 0, tiled=True)  27.9 us
    all_to_all x1, starting transfers between devices, local(): part = jnp.sum(lax.all_to_all(part, PLANE, 0, 0, tiled=True), axis=0)  11.9 us
    ppermute x12, waiting for transfers between devices, shifted(): lax.ppermute(value, SPACE, [(source, source + step) for source in range(f...  6.04 us
    all_to_all x2, waiting for transfers between devices, spread(): return lax.all_to_all(copies, axes, 0, 0, tiled=True)  4.8 us
    all_to_all x1, waiting for transfers between devices, local(): part = jnp.sum(lax.all_to_all(part, PLANE, 0, 0, tiled=True), axis=0)  3.06 us
  transfers between devices with their start and end apart: 15, of which 6 were waited for; matrix products, arithmetic and copies ran while one was open for 0% of the time, Pallas kernels for 7%

profile of v6, /device:TPU:1, one launch (start us, length us, event | category | flops | bytes accessed | tf_op | source)
XLA Modules:
  0.0 125.2 jit_solution(10534895197546788821)
XLA Ops:
  0.6 2.7 %shard_map.161 = (bf16[48,48,128]{2,1,0:T(8,128)(2,1)}, bf16[6,48,128]{2,1,0:T(8,128)(2,1)}, bf16[6,48,128]{2,1,0:T(8,128)(2,1)}, bf16[6,48,128]{2,1,0:T(8,128)(2,1)}, bf16[6,48,128]{2,1,0:T(8,128)(2,1)}) custom-call(s32[1,8]{1,0:T(1,128)} %beside.5, s32[1]{0:T(128)} %bitcast.where, s32[1,48,48]{2,1,0:T(8,128)} %land_mask.1, bf16[1,1,48,48,128]{4,3,2,1,0:T(8,128)(2,1)} %fields.1), custom_call_target="tpu_custom_call" | custom-call | flops 294912 | bytes 1483776 | tf_op jit(solution)/shard_map/pallas_call | solution.py:447
  3.4 3.9 %collective-permute-start.2 = (bf16[6,48,128]{2,1,0:T(8,128)(2,1)}, bf16[6,48,128]{2,1,0:T(8,128)(2,1)S(1)}, u32[]{:S(2)}, u32[]{:S(2)}) collective-permute-start(bf16[6,48,128]{2,1,0:T(8,128)(2,1)} %get-tuple-element.40), channel_id=1, source_target_pairs={{0,1},{1,2},{2,3},{3,4},{4,5},{5,6},{6,7},{7,8},{8,9},{9,10},{10,1... | collective-permute-start | bytes 221192 | tf_op jit(solution)/shard_map/ppermute | solution.py:461
  7.3 3.5 %collective-permute-start.1 = (bf16[6,48,128]{2,1,0:T(8,128)(2,1)}, bf16[6,48,128]{2,1,0:T(8,128)(2,1)S(1)}, u32[]{:S(2)}, u32[]{:S(2)}) collective-permute-start(bf16[6,48,128]{2,1,0:T(8,128)(2,1)} %get-tuple-element.39), channel_id=1, source_target_pairs={{0,2},{1,3},{2,4},{3,5},{4,6},{5,7},{6,8},{7,9},{8,10},{9,11},{10,... | collective-permute-start | bytes 221192 | tf_op jit(solution)/shard_map/ppermute | solution.py:461
  10.8 4.9 %collective-permute-start = (bf16[6,48,128]{2,1,0:T(8,128)(2,1)}, bf16[6,48,128]{2,1,0:T(8,128)(2,1)S(1)}, u32[]{:S(2)}, u32[]{:S(2)}) collective-permute-start(bf16[6,48,128]{2,1,0:T(8,128)(2,1)} %get-tuple-element.39), channel_id=1, source_target_pairs={{0,3},{1,4},{2,5},{3,6},{4,7},{5,8},{6,9},{7,10},{8,11},{9,12},{10... | collective-permute-start | bytes 221192 | tf_op jit(solution)/shard_map/ppermute | solution.py:461
  15.7 1.3 %collective-permute-start.3 = (bf16[6,48,128]{2,1,0:T(8,128)(2,1)}, bf16[6,48,128]{2,1,0:T(8,128)(2,1)S(1)}, u32[]{:S(2)}, u32[]{:S(2)}) collective-permute-start(bf16[6,48,128]{2,1,0:T(8,128)(2,1)} %get-tuple-element.41), channel_id=1, source_target_pairs={{1,0},{2,1},{3,2},{4,3},{5,4},{6,5},{7,6},{8,7},{9,8},{10,9},{11,1... | collective-permute-start | bytes 221192 | tf_op jit(solution)/shard_map/ppermute | solution.py:461
  17.0 1.3 %collective-permute-start.5 = (bf16[6,48,128]{2,1,0:T(8,128)(2,1)}, bf16[6,48,128]{2,1,0:T(8,128)(2,1)S(1)}, u32[]{:S(2)}, u32[]{:S(2)}) collective-permute-start(bf16[6,48,128]{2,1,0:T(8,128)(2,1)} %get-tuple-element.42), channel_id=1, source_target_pairs={{3,0},{4,1},{5,2},{6,3},{7,4},{8,5},{9,6},{10,7},{11,8},{12,9},{13... | collective-permute-start | bytes 221192 | tf_op jit(solution)/shard_map/ppermute | solution.py:461
  18.3 0.0 collective-permute-done.2.s2
  18.3 0.0 copy-start.8
  18.3 1.3 %collective-permute-start.4 = (bf16[6,48,128]{2,1,0:T(8,128)(2,1)}, bf16[6,48,128]{2,1,0:T(8,128)(2,1)S(1)}, u32[]{:S(2)}, u32[]{:S(2)}) collective-permute-start(bf16[6,48,128]{2,1,0:T(8,128)(2,1)} %get-tuple-element.42), channel_id=1, source_target_pairs={{2,0},{3,1},{4,2},{5,3},{6,4},{7,5},{8,6},{9,7},{10,8},{11,9},{12,... | collective-permute-start | bytes 221192 | tf_op jit(solution)/shard_map/ppermute | solution.py:461
  19.6 1.4 %collective-permute-done.3.s3 = bf16[6,48,128]{2,1,0:T(8,128)(2,1)S(1)} collective-permute-done((bf16[6,48,128]{2,1,0:T(8,128)(2,1)}, bf16[6,48,128]{2,1,0:T(8,128)(2,1)S(1)}, u32[]{:S(2)}, u32[]{:S(2)}) %collective-permute-start.3) | collective-permute-done | bytes 73760 | tf_op jit(solution)/shard_map/ppermute | solution.py:461
  21.0 0.0 collective-permute-done.1.s1
  21.0 0.0 collective-permute-done.s0
  21.0 0.0 copy-start.10
  21.1 4.5 %collective-permute-done.5.s5 = bf16[6,48,128]{2,1,0:T(8,128)(2,1)S(1)} collective-permute-done((bf16[6,48,128]{2,1,0:T(8,128)(2,1)}, bf16[6,48,128]{2,1,0:T(8,128)(2,1)S(1)}, u32[]{:S(2)}, u32[]{:S(2)}) %collective-permute-start.5) | collective-permute-done | bytes 73760 | tf_op jit(solution)/shard_map/ppermute | solution.py:461
  25.5 0.2 collective-permute-done.4.s4
  25.7 0.0 copy-done.8
  25.7 0.0 copy-done.12
  25.7 0.0 copy-done.9
  25.7 0.0 copy-done.10
  25.7 0.4 copy-done.14
  26.1 0.2 copy-done.15
  26.3 23.2 %shard_map.162 = (bf16[48,48,128]{2,1,0:T(8,128)(2,1)}, bf16[48,48,128]{2,1,0:T(8,128)(2,1)}, bf16[6,48,128]{2,1,0:T(8,128)(2,1)}, bf16[6,48,128]{2,1,0:T(8,128)...) custom-call(s32[1,8]{1,0:T(1,128)} %beside.5, s32[1]{0:T(128)} %bitcast.where, ...), custom_call_target="tpu_custom_call" | custom-call | flops 1811939328 | bytes 4632064 | tf_op jit(solution)/shard_map/pallas_call | solution.py:447
  49.6 0.0 copy-start.7
  49.6 0.0 copy-start.13
  49.6 0.0 copy-start.11
  49.6 11.9 %all-to-all-start = ((f32[32,40,128]{2,1,0:T(8,128)}), f32[32,40,128]{2,1,0:T(8,128)S(1)}, u32[]{:S(2)}, u32[]{:S(2)}) async-start(f32[32,40,128]{2,1,0:T(8,128)} %bitcast.14), calls=%async_computation | async-start | bytes 1310720 | tf_op jit(solution)/shard_map/all_to_all | solution.py:558
  61.5 0.0 copy-done.7
  61.5 3.7 %collective-permute-start.6 = (bf16[6,48,128]{2,1,0:T(8,128)(2,1)S(1)}, bf16[6,48,128]{2,1,0:T(8,128)(2,1)S(1)}, u32[]{:S(2)}, u32[]{:S(2)}) collective-permute-start(bf16[6,48,128]{2,1,0:T(8,128)(2,1)S(1)} %copy-done.7), channel_id=1, source_target_pairs={{0,2},{1,3},{2,4},{3,5},{4,6},{5,7},{6,8},{7,9},{8,10},{9,11},{10,... | collective-permute-start | bytes 221192 | tf_op jit(solution)/shard_map/ppermute | solution.py:461
  65.1 0.0 copy-done.13
  65.2 1.3 %collective-permute-start.8 = (bf16[6,48,128]{2,1,0:T(8,128)(2,1)S(1)}, bf16[6,48,128]{2,1,0:T(8,128)(2,1)S(1)}, u32[]{:S(2)}, u32[]{:S(2)}) collective-permute-start(bf16[6,48,128]{2,1,0:T(8,128)(2,1)S(1)} %copy-done.13), channel_id=1, source_target_pairs={{1,0},{2,1},{3,2},{4,3},{5,4},{6,5},{7,6},{8,7},{9,8},{10,9},{11,1... | collective-permute-start | bytes 221192 | tf_op jit(solution)/shard_map/ppermute | solution.py:461
  66.5 0.0 copy-done.11
  66.5 4.0 %collective-permute-start.7 = (bf16[6,48,128]{2,1,0:T(8,128)(2,1)S(1)}, bf16[6,48,128]{2,1,0:T(8,128)(2,1)S(1)}, u32[]{:S(2)}, u32[]{:S(2)}) collective-permute-start(bf16[6,48,128]{2,1,0:T(8,128)(2,1)S(1)} %copy-done.11), channel_id=1, source_target_pairs={{0,1},{1,2},{2,3},{3,4},{4,5},{5,6},{6,7},{7,8},{8,9},{9,10},{10,1... | collective-permute-start | bytes 221192 | tf_op jit(solution)/shard_map/ppermute | solution.py:461
  70.5 3.1 %all-to-all-done = f32[32,40,128]{2,1,0:T(8,128)S(1)} async-done(((f32[32,40,128]{2,1,0:T(8,128)}), f32[32,40,128]{2,1,0:T(8,128)S(1)}, u32[]{:S(2)}, u32[]{:S(2)}) %all-to-all-start) | async-done | bytes 655392 | tf_op jit(solution)/shard_map/all_to_all | solution.py:558
  73.5 0.1 reduce_sum.18
  73.6 0.0 collective-permute-done.6.s1
  73.6 0.0 copy-start
  73.6 0.0 collective-permute-done.8.s3
  73.6 0.0 copy-start.1
  73.6 0.0 collective-permute-done.7.s2
  73.6 0.0 copy-start.2
  73.6 0.7 broadcast_in_dim.29
  74.4 0.0 copy-done
  74.4 0.0 copy-done.1
  74.4 0.0 copy-done.2
  74.4 16.4 %all-to-all-start.1 = ((bf16[16,40,128]{2,1,0:T(8,128)(2,1)}), bf16[16,40,128]{2,1,0:T(8,128)(2,1)S(1)}, u32[]{:S(2)}, u32[]{:S(2)}) async-start(bf16[16,40,128]{2,1,0:T(8,128)(2,1)} %broadcast_in_dim.29), calls=%async_computation.1 | async-start | bytes 327680 | tf_op jit(solution)/shard_map/all_to_all | solution.py:471
  90.7 0.0 copy-done.6
  90.8 1.3 %collective-permute-start.11 = (bf16[6,48,128]{2,1,0:T(8,128)(2,1)S(1)}, bf16[6,48,128]{2,1,0:T(8,128)(2,1)S(1)}, u32[]{:S(2)}, u32[]{:S(2)}) collective-permute-start(bf16[6,48,128]{2,1,0:T(8,128)(2,1)S(1)} %copy-done.6), channel_id=1, source_target_pairs={{3,0},{4,1},{5,2},{6,3},{7,4},{8,5},{9,6},{10,7},{11,8},{12,9},{13... | collective-permute-start | bytes 221192 | tf_op jit(solution)/shard_map/ppermute | solution.py:461
  92.1 1.3 %collective-permute-start.10 = (bf16[6,48,128]{2,1,0:T(8,128)(2,1)S(1)}, bf16[6,48,128]{2,1,0:T(8,128)(2,1)S(1)}, u32[]{:S(2)}, u32[]{:S(2)}) collective-permute-start(bf16[6,48,128]{2,1,0:T(8,128)(2,1)S(1)} %copy-done.6), channel_id=1, source_target_pairs={{2,0},{3,1},{4,2},{5,3},{6,4},{7,5},{8,6},{9,7},{10,8},{11,9},{12,... | collective-permute-start | bytes 221192 | tf_op jit(solution)/shard_map/ppermute | solution.py:461
  93.4 5.5 %collective-permute-start.9 = (bf16[6,48,128]{2,1,0:T(8,128)(2,1)S(1)}, bf16[6,48,128]{2,1,0:T(8,128)(2,1)S(1)}, u32[]{:S(2)}, u32[]{:S(2)}) collective-permute-start(bf16[6,48,128]{2,1,0:T(8,128)(2,1)S(1)} %copy-done.7), channel_id=1, source_target_pairs={{0,3},{1,4},{2,5},{3,6},{4,7},{5,8},{6,9},{7,10},{8,11},{9,12},{10... | collective-permute-start | bytes 221192 | tf_op jit(solution)/shard_map/ppermute | solution.py:461
  98.9 4.0 %all-to-all-done.1 = bf16[16,40,128]{2,1,0:T(8,128)(2,1)S(1)} async-done(((bf16[16,40,128]{2,1,0:T(8,128)(2,1)}), bf16[16,40,128]{2,1,0:T(8,128)(2,1)S(1)}, u32[]{:S(2)}, u32[]{:S(2)}) %all-to-all-start.1) | async-done | bytes 163872 | tf_op jit(solution)/shard_map/all_to_all | solution.py:471
  102.9 0.0 collective-permute-done.9.s0
  102.9 0.0 copy-start.5
  103.0 0.0 collective-permute-done.11.s5
  103.0 0.0 copy-start.3
  103.0 0.0 collective-permute-done.10.s4
  103.0 0.0 copy-start.4
  103.0 0.8 broadcast_in_dim.30
  103.8 0.0 copy-done.5
  103.8 0.0 copy-done.3
  103.8 0.0 copy-done.4
  103.8 11.5 %all-to-all-start.2 = ((bf16[32,40,128]{2,1,0:T(8,128)(2,1)}), bf16[32,40,128]{2,1,0:T(8,128)(2,1)S(1)}, u32[]{:S(2)}, u32[]{:S(2)}) async-start(bf16[32,40,128]{2,1,0:T(8,128)(2,1)} %broadcast_in_dim.30), calls=%async_computation.2 | async-start | bytes 655360 | tf_op jit(solution)/shard_map/all_to_all | solution.py:471
  115.3 8.3 %shard_map.163 = bf16[48,48,128]{2,1,0:T(8,128)(2,1)} custom-call(s32[1,8]{1,0:T(1,128)} %beside.5, s32[1]{0:T(128)} %bitcast.where, bf16[48,48,128]{2,1,0:T(8,128)(2,1)} %get-tuple-element.53.conv_grad_hbm, bf16[6,48,128]{2,1,0:T(8,128)(2,1)} %copy-done.5, bf16[6,48,128]{2,1,0:T(8,128)(2,1)} %copy-done, bf16[6,48,128]{2,1,0:T(8,128)(2,1)} %copy-done.2, ...), custom_call_target="tpu_custom_call" | custom-call | flops 28901376 | bytes 2826752 | tf_op jit(solution)/shard_map/pallas_call | solution.py:447
  123.6 0.8 all-to-all-done.2
  124.4 0.8 shard_map.164
  (7 shorter events, 0.0 us)
Async XLA Ops:
  3.4 15.0 %collective-permute-start.2 = (bf16[6,48,128]{2,1,0:T(8,128)(2,1)}, bf16[6,48,128]{2,1,0:T(8,128)(2,1)S(1)}, u32[]{:S(2)}, u32[]{:S(2)}) collective-permute-start(bf16[6,48,128]{2,1,0:T(8,128)(2,1)} %get-tuple-element.40), channel_id=1, source_target_pairs={{0,1},{1,2},{2,3},{3,4},{4,5},{5,6},{6,7},{7,8},{8,9},{9,10},{10,1... | collective-permute-start | bytes 221192 | tf_op jit(solution)/shard_map/ppermute | solution.py:461
  7.3 13.7 %collective-permute-start.1 = (bf16[6,48,128]{2,1,0:T(8,128)(2,1)}, bf16[6,48,128]{2,1,0:T(8,128)(2,1)S(1)}, u32[]{:S(2)}, u32[]{:S(2)}) collective-permute-start(bf16[6,48,128]{2,1,0:T(8,128)(2,1)} %get-tuple-element.39), channel_id=1, source_target_pairs={{0,2},{1,3},{2,4},{3,5},{4,6},{5,7},{6,8},{7,9},{8,10},{9,11},{10,... | collective-permute-start | bytes 221192 | tf_op jit(solution)/shard_map/ppermute | solution.py:461
  10.8 10.2 %collective-permute-start = (bf16[6,48,128]{2,1,0:T(8,128)(2,1)}, bf16[6,48,128]{2,1,0:T(8,128)(2,1)S(1)}, u32[]{:S(2)}, u32[]{:S(2)}) collective-permute-start(bf16[6,48,128]{2,1,0:T(8,128)(2,1)} %get-tuple-element.39), channel_id=1, source_target_pairs={{0,3},{1,4},{2,5},{3,6},{4,7},{5,8},{6,9},{7,10},{8,11},{9,12},{10... | collective-permute-start | bytes 221192 | tf_op jit(solution)/shard_map/ppermute | solution.py:461
  15.7 5.3 %collective-permute-start.3 = (bf16[6,48,128]{2,1,0:T(8,128)(2,1)}, bf16[6,48,128]{2,1,0:T(8,128)(2,1)S(1)}, u32[]{:S(2)}, u32[]{:S(2)}) collective-permute-start(bf16[6,48,128]{2,1,0:T(8,128)(2,1)} %get-tuple-element.41), channel_id=1, source_target_pairs={{1,0},{2,1},{3,2},{4,3},{5,4},{6,5},{7,6},{8,7},{9,8},{10,9},{11,1... | collective-permute-start | bytes 221192 | tf_op jit(solution)/shard_map/ppermute | solution.py:461
  17.0 8.5 %collective-permute-start.5 = (bf16[6,48,128]{2,1,0:T(8,128)(2,1)}, bf16[6,48,128]{2,1,0:T(8,128)(2,1)S(1)}, u32[]{:S(2)}, u32[]{:S(2)}) collective-permute-start(bf16[6,48,128]{2,1,0:T(8,128)(2,1)} %get-tuple-element.42), channel_id=1, source_target_pairs={{3,0},{4,1},{5,2},{6,3},{7,4},{8,5},{9,6},{10,7},{11,8},{12,9},{13... | collective-permute-start | bytes 221192 | tf_op jit(solution)/shard_map/ppermute | solution.py:461
  18.3 7.4 %copy-start.8 = (bf16[6,48,128]{2,1,0:T(8,128)(2,1)}, bf16[6,48,128]{2,1,0:T(8,128)(2,1)S(1)}, u32[]{:S(2)}) copy-start(bf16[6,48,128]{2,1,0:T(8,128)(2,1)S(1)} %collective-permute-done.2.s2) | copy-start | bytes 221188
  18.3 7.3 %collective-permute-start.4 = (bf16[6,48,128]{2,1,0:T(8,128)(2,1)}, bf16[6,48,128]{2,1,0:T(8,128)(2,1)S(1)}, u32[]{:S(2)}, u32[]{:S(2)}) collective-permute-start(bf16[6,48,128]{2,1,0:T(8,128)(2,1)} %get-tuple-element.42), channel_id=1, source_target_pairs={{2,0},{3,1},{4,2},{5,3},{6,4},{7,5},{8,6},{9,7},{10,8},{11,9},{12,... | collective-permute-start | bytes 221192 | tf_op jit(solution)/shard_map/ppermute | solution.py:461
  21.0 4.7 %copy-start.12 = (bf16[6,48,128]{2,1,0:T(8,128)(2,1)}, bf16[6,48,128]{2,1,0:T(8,128)(2,1)S(1)}, u32[]{:S(2)}) copy-start(bf16[6,48,128]{2,1,0:T(8,128)(2,1)S(1)} %collective-permute-done.3.s3) | copy-start | bytes 221188
  21.0 4.7 %copy-start.9 = (bf16[6,48,128]{2,1,0:T(8,128)(2,1)}, bf16[6,48,128]{2,1,0:T(8,128)(2,1)S(1)}, u32[]{:S(2)}) copy-start(bf16[6,48,128]{2,1,0:T(8,128)(2,1)S(1)} %collective-permute-done.1.s1) | copy-start | bytes 221188
  21.0 4.7 %copy-start.10 = (bf16[6,48,128]{2,1,0:T(8,128)(2,1)}, bf16[6,48,128]{2,1,0:T(8,128)(2,1)S(1)}, u32[]{:S(2)}) copy-start(bf16[6,48,128]{2,1,0:T(8,128)(2,1)S(1)} %collective-permute-done.s0) | copy-start | bytes 221188
  25.5 0.6 copy-start.14
  25.7 0.6 copy-start.15
  49.6 11.9 %copy-start.7 = (bf16[6,48,128]{2,1,0:T(8,128)(2,1)S(1)}, bf16[6,48,128]{2,1,0:T(8,128)(2,1)}, u32[]{:S(2)}) copy-start(bf16[6,48,128]{2,1,0:T(8,128)(2,1)} %get-tuple-element.50) | copy-start | bytes 221188
  49.6 15.6 %copy-start.13 = (bf16[6,48,128]{2,1,0:T(8,128)(2,1)S(1)}, bf16[6,48,128]{2,1,0:T(8,128)(2,1)}, u32[]{:S(2)}) copy-start(bf16[6,48,128]{2,1,0:T(8,128)(2,1)} %get-tuple-element.47) | copy-start | bytes 221188
  49.6 16.9 %copy-start.11 = (bf16[6,48,128]{2,1,0:T(8,128)(2,1)S(1)}, bf16[6,48,128]{2,1,0:T(8,128)(2,1)}, u32[]{:S(2)}) copy-start(bf16[6,48,128]{2,1,0:T(8,128)(2,1)} %get-tuple-element.48) | copy-start | bytes 221188
  49.6 23.9 %all-to-all-start = ((f32[32,40,128]{2,1,0:T(8,128)}), f32[32,40,128]{2,1,0:T(8,128)S(1)}, u32[]{:S(2)}, u32[]{:S(2)}) async-start(f32[32,40,128]{2,1,0:T(8,128)} %bitcast.14), calls=%async_computation | async-start | bytes 1310720 | tf_op jit(solution)/shard_map/all_to_all | solution.py:558
  61.5 12.1 %collective-permute-start.6 = (bf16[6,48,128]{2,1,0:T(8,128)(2,1)S(1)}, bf16[6,48,128]{2,1,0:T(8,128)(2,1)S(1)}, u32[]{:S(2)}, u32[]{:S(2)}) collective-permute-start(bf16[6,48,128]{2,1,0:T(8,128)(2,1)S(1)} %copy-done.7), channel_id=1, source_target_pairs={{0,2},{1,3},{2,4},{3,5},{4,6},{5,7},{6,8},{7,9},{8,10},{9,11},{10,... | collective-permute-start | bytes 221192 | tf_op jit(solution)/shard_map/ppermute | solution.py:461
  65.2 8.4 %collective-permute-start.8 = (bf16[6,48,128]{2,1,0:T(8,128)(2,1)S(1)}, bf16[6,48,128]{2,1,0:T(8,128)(2,1)S(1)}, u32[]{:S(2)}, u32[]{:S(2)}) collective-permute-start(bf16[6,48,128]{2,1,0:T(8,128)(2,1)S(1)} %copy-done.13), channel_id=1, source_target_pairs={{1,0},{2,1},{3,2},{4,3},{5,4},{6,5},{7,6},{8,7},{9,8},{10,9},{11,1... | collective-permute-start | bytes 221192 | tf_op jit(solution)/shard_map/ppermute | solution.py:461
  66.5 7.2 %collective-permute-start.7 = (bf16[6,48,128]{2,1,0:T(8,128)(2,1)S(1)}, bf16[6,48,128]{2,1,0:T(8,128)(2,1)S(1)}, u32[]{:S(2)}, u32[]{:S(2)}) collective-permute-start(bf16[6,48,128]{2,1,0:T(8,128)(2,1)S(1)} %copy-done.11), channel_id=1, source_target_pairs={{0,1},{1,2},{2,3},{3,4},{4,5},{5,6},{6,7},{7,8},{8,9},{9,10},{10,1... | collective-permute-start | bytes 221192 | tf_op jit(solution)/shard_map/ppermute | solution.py:461
  73.6 0.8 copy-start
  73.6 0.8 copy-start.1
  73.6 0.7 copy-start.2
  74.4 16.4 %copy-start.6 = (bf16[6,48,128]{2,1,0:T(8,128)(2,1)S(1)}, bf16[6,48,128]{2,1,0:T(8,128)(2,1)}, u32[]{:S(2)}) copy-start(bf16[6,48,128]{2,1,0:T(8,128)(2,1)} %get-tuple-element.51) | copy-start | bytes 221188
  74.4 28.5 %all-to-all-start.1 = ((bf16[16,40,128]{2,1,0:T(8,128)(2,1)}), bf16[16,40,128]{2,1,0:T(8,128)(2,1)S(1)}, u32[]{:S(2)}, u32[]{:S(2)}) async-start(bf16[16,40,128]{2,1,0:T(8,128)(2,1)} %broadcast_in_dim.29), calls=%async_computation.1 | async-start | bytes 327680 | tf_op jit(solution)/shard_map/all_to_all | solution.py:471
  90.8 12.2 %collective-permute-start.11 = (bf16[6,48,128]{2,1,0:T(8,128)(2,1)S(1)}, bf16[6,48,128]{2,1,0:T(8,128)(2,1)S(1)}, u32[]{:S(2)}, u32[]{:S(2)}) collective-permute-start(bf16[6,48,128]{2,1,0:T(8,128)(2,1)S(1)} %copy-done.6), channel_id=1, source_target_pairs={{3,0},{4,1},{5,2},{6,3},{7,4},{8,5},{9,6},{10,7},{11,8},{12,9},{13... | collective-permute-start | bytes 221192 | tf_op jit(solution)/shard_map/ppermute | solution.py:461
  92.1 10.9 %collective-permute-start.10 = (bf16[6,48,128]{2,1,0:T(8,128)(2,1)S(1)}, bf16[6,48,128]{2,1,0:T(8,128)(2,1)S(1)}, u32[]{:S(2)}, u32[]{:S(2)}) collective-permute-start(bf16[6,48,128]{2,1,0:T(8,128)(2,1)S(1)} %copy-done.6), channel_id=1, source_target_pairs={{2,0},{3,1},{4,2},{5,3},{6,4},{7,5},{8,6},{9,7},{10,8},{11,9},{12,... | collective-permute-start | bytes 221192 | tf_op jit(solution)/shard_map/ppermute | solution.py:461
  93.4 9.6 %collective-permute-start.9 = (bf16[6,48,128]{2,1,0:T(8,128)(2,1)S(1)}, bf16[6,48,128]{2,1,0:T(8,128)(2,1)S(1)}, u32[]{:S(2)}, u32[]{:S(2)}) collective-permute-start(bf16[6,48,128]{2,1,0:T(8,128)(2,1)S(1)} %copy-done.7), channel_id=1, source_target_pairs={{0,3},{1,4},{2,5},{3,6},{4,7},{5,8},{6,9},{7,10},{8,11},{9,12},{10... | collective-permute-start | bytes 221192 | tf_op jit(solution)/shard_map/ppermute | solution.py:461
  102.9 0.8 copy-start.5
  103.0 0.8 copy-start.3
  103.0 0.8 copy-start.4
  103.8 20.6 %all-to-all-start.2 = ((bf16[32,40,128]{2,1,0:T(8,128)(2,1)}), bf16[32,40,128]{2,1,0:T(8,128)(2,1)S(1)}, u32[]{:S(2)}, u32[]{:S(2)}) async-start(bf16[32,40,128]{2,1,0:T(8,128)(2,1)} %broadcast_in_dim.30), calls=%async_computation.2 | async-start | bytes 655360 | tf_op jit(solution)/shard_map/all_to_all | solution.py:471

commit v7 on v6

--- a/solution.py
+++ b/solution.py
@@ -244,9 +244,11 @@
         return 0
 
     lax.fori_loop(0, TILE, centre, 0, unroll=4)
-    for copy in copies[2:]:
+    for copy in copies[2:8]:
         copy.wait()
     place_rims(ext, ext_flat, beside, where, rims)
+    for copy in copies[8:]:
+        copy.wait()
     ones = jnp.ones((8, CELLS_IN_CHUNK), bf16)
 
     def chunk(step, _):
@@ -399,9 +401,11 @@
         return 0
 
     lax.fori_loop(0, TILE, centre, 0, unroll=4)
-    for copy in copies[1:]:
+    for copy in copies[1:7]:
         copy.wait()
     place_rims(ext, ext_flat, beside, where, rims)
+    for copy in copies[7:]:
+        copy.wait()
 
     def chunk(step, _):
         first = pl.multiple_of(step * CHUNK, CHUNK)
@@ -556,9 +560,9 @@
     cells = TILE * TILE * lax.axis_size(DP) * lax.axis_size(SPACE)
     part = sums.reshape(lax.axis_size(PLANE), -1, LANES)
     part = jnp.sum(lax.all_to_all(part, PLANE, 0, 0, tiled=True), axis=0)
-    near = exchange(*rims, steps=(-2, -1, 1))
+    near = exchange(*rims, steps=(-2, -1, 1, 2))
     part, rims, near = lax.optimization_barrier((part, rims, near))
-    far = exchange(*rims, steps=(-3, 2, 3))
+    far = exchange(*rims, steps=(-3, 3))
     part = jnp.sum(spread(part.astype(bf16), "z").astype(f32), axis=0) * (1.0 / math.sqrt(cells))
     part, far = lax.optimization_barrier((part, far))
     strips = [{**near, **far}[step] for step in STEPS]

time: 126 us -> 130 us (1.032)
  waiting for transfers between devices: 13.9 us -> 18.9 us
    all_to_all x2, waiting for transfers between devices: 4.8 us -> 10.7 us  [spread(): return lax.all_to_all(copies, axes, 0, 0, tiled=True)]
    ppermute x12, starting transfers between devices: 33.3 us -> 29.6 us  [shifted(): lax.ppermute(value, SPACE, [(source, source + step) for source in range(f...]
    all_to_all x2, starting transfers between devices: 27.9 us -> 30.9 us  [spread(): return lax.all_to_all(copies, axes, 0, 0, tiled=True)]
    all_to_all x1, waiting for transfers between devices: 3.06 us -> 1.18 us  [local(): part = jnp.sum(lax.all_to_all(part, PLANE, 0, 0, tiled=True), axis=0)]
  transfers between devices with their start and end apart: 15 -> 15, of which waited for: 6 -> 7; matrix products, arithmetic and copies ran while one was open for 0% -> 0% of each run, Pallas kernels for 7% -> 6%
where the time goes in v7:
time: 130 us; the launch traced here: 129 us
  starting transfers between devices  72.4 us (56%)
  Pallas kernels  34.6 us (27%)
  waiting for transfers between devices  18.9 us (15%)
  local copies, waits for them, and re-layouts  2.13 us (2%)
    pallas_call x4, Pallas kernels, call(): pl.pallas_call(kernel, out_shape=outs, in_specs=[SMEM] * len(scalars) + (...  34.6 us
    all_to_all x2, starting transfers between devices, spread(): return lax.all_to_all(copies, axes, 0, 0, tiled=True)  30.9 us
    ppermute x12, starting transfers between devices, shifted(): lax.ppermute(value, SPACE, [(source, source + step) for source in range(f...  29.6 us
    all_to_all x1, starting transfers between devices, local(): part = jnp.sum(lax.all_to_all(part, PLANE, 0, 0, tiled=True), axis=0)  11.9 us
    all_to_all x2, waiting for transfers between devices, spread(): return lax.all_to_all(copies, axes, 0, 0, tiled=True)  10.7 us
    ppermute x12, waiting for transfers between devices, shifted(): lax.ppermute(value, SPACE, [(source, source + step) for source in range(f...  7.04 us
  transfers between devices with their start and end apart: 15, of which 7 were waited for; matrix products, arithmetic and copies ran while one was open for 0% of the time, Pallas kernels for 6%

profile of v7, /device:TPU:1, one launch (start us, length us, event | category | flops | bytes accessed | tf_op | source)
XLA Modules:
  0.0 129.1 jit_solution(95171523708390919)
XLA Ops:
  0.6 2.7 %shard_map.161 = (bf16[48,48,128]{2,1,0:T(8,128)(2,1)}, bf16[6,48,128]{2,1,0:T(8,128)(2,1)}, bf16[6,48,128]{2,1,0:T(8,128)(2,1)}, bf16[6,48,128]{2,1,0:T(8,128)(2,1)}, bf16[6,48,128]{2,1,0:T(8,128)(2,1)}) custom-call(s32[1,8]{1,0:T(1,128)} %beside.5, s32[1]{0:T(128)} %bitcast.where, s32[1,48,48]{2,1,0:T(8,128)} %land_mask.1, bf16[1,1,48,48,128]{4,3,2,1,0:T(8,128)(2,1)} %fields.1), custom_call_target="tpu_custom_call" | custom-call | flops 294912 | bytes 1483776 | tf_op jit(solution)/shard_map/pallas_call | solution.py:451
  3.4 3.9 %collective-permute-start.2 = (bf16[6,48,128]{2,1,0:T(8,128)(2,1)}, bf16[6,48,128]{2,1,0:T(8,128)(2,1)S(1)}, u32[]{:S(2)}, u32[]{:S(2)}) collective-permute-start(bf16[6,48,128]{2,1,0:T(8,128)(2,1)} %get-tuple-element.40), channel_id=1, source_target_pairs={{0,1},{1,2},{2,3},{3,4},{4,5},{5,6},{6,7},{7,8},{8,9},{9,10},{10,1... | collective-permute-start | bytes 221192 | tf_op jit(solution)/shard_map/ppermute | solution.py:465
  7.3 3.5 %collective-permute-start.1 = (bf16[6,48,128]{2,1,0:T(8,128)(2,1)}, bf16[6,48,128]{2,1,0:T(8,128)(2,1)S(1)}, u32[]{:S(2)}, u32[]{:S(2)}) collective-permute-start(bf16[6,48,128]{2,1,0:T(8,128)(2,1)} %get-tuple-element.39), channel_id=1, source_target_pairs={{0,2},{1,3},{2,4},{3,5},{4,6},{5,7},{6,8},{7,9},{8,10},{9,11},{10,... | collective-permute-start | bytes 221192 | tf_op jit(solution)/shard_map/ppermute | solution.py:465
  10.8 4.9 %collective-permute-start = (bf16[6,48,128]{2,1,0:T(8,128)(2,1)}, bf16[6,48,128]{2,1,0:T(8,128)(2,1)S(1)}, u32[]{:S(2)}, u32[]{:S(2)}) collective-permute-start(bf16[6,48,128]{2,1,0:T(8,128)(2,1)} %get-tuple-element.39), channel_id=1, source_target_pairs={{0,3},{1,4},{2,5},{3,6},{4,7},{5,8},{6,9},{7,10},{8,11},{9,12},{10... | collective-permute-start | bytes 221192 | tf_op jit(solution)/shard_map/ppermute | solution.py:465
  15.7 1.3 %collective-permute-start.3 = (bf16[6,48,128]{2,1,0:T(8,128)(2,1)}, bf16[6,48,128]{2,1,0:T(8,128)(2,1)S(1)}, u32[]{:S(2)}, u32[]{:S(2)}) collective-permute-start(bf16[6,48,128]{2,1,0:T(8,128)(2,1)} %get-tuple-element.41), channel_id=1, source_target_pairs={{1,0},{2,1},{3,2},{4,3},{5,4},{6,5},{7,6},{8,7},{9,8},{10,9},{11,1... | collective-permute-start | bytes 221192 | tf_op jit(solution)/shard_map/ppermute | solution.py:465
  17.0 1.3 %collective-permute-start.5 = (bf16[6,48,128]{2,1,0:T(8,128)(2,1)}, bf16[6,48,128]{2,1,0:T(8,128)(2,1)S(1)}, u32[]{:S(2)}, u32[]{:S(2)}) collective-permute-start(bf16[6,48,128]{2,1,0:T(8,128)(2,1)} %get-tuple-element.42), channel_id=1, source_target_pairs={{3,0},{4,1},{5,2},{6,3},{7,4},{8,5},{9,6},{10,7},{11,8},{12,9},{13... | collective-permute-start | bytes 221192 | tf_op jit(solution)/shard_map/ppermute | solution.py:465
  18.3 0.0 collective-permute-done.2.s2
  18.3 0.0 copy-start.8
  18.3 1.3 %collective-permute-start.4 = (bf16[6,48,128]{2,1,0:T(8,128)(2,1)}, bf16[6,48,128]{2,1,0:T(8,128)(2,1)S(1)}, u32[]{:S(2)}, u32[]{:S(2)}) collective-permute-start(bf16[6,48,128]{2,1,0:T(8,128)(2,1)} %get-tuple-element.42), channel_id=1, source_target_pairs={{2,0},{3,1},{4,2},{5,3},{6,4},{7,5},{8,6},{9,7},{10,8},{11,9},{12,... | collective-permute-start | bytes 221192 | tf_op jit(solution)/shard_map/ppermute | solution.py:465
  19.6 1.4 %collective-permute-done.3.s3 = bf16[6,48,128]{2,1,0:T(8,128)(2,1)S(1)} collective-permute-done((bf16[6,48,128]{2,1,0:T(8,128)(2,1)}, bf16[6,48,128]{2,1,0:T(8,128)(2,1)S(1)}, u32[]{:S(2)}, u32[]{:S(2)}) %collective-permute-start.3) | collective-permute-done | bytes 73760 | tf_op jit(solution)/shard_map/ppermute | solution.py:465
  21.0 0.0 collective-permute-done.1.s1
  21.0 0.0 collective-permute-done.s0
  21.0 0.0 copy-start.12
  21.1 4.5 %collective-permute-done.5.s5 = bf16[6,48,128]{2,1,0:T(8,128)(2,1)S(1)} collective-permute-done((bf16[6,48,128]{2,1,0:T(8,128)(2,1)}, bf16[6,48,128]{2,1,0:T(8,128)(2,1)S(1)}, u32[]{:S(2)}, u32[]{:S(2)}) %collective-permute-start.5) | collective-permute-done | bytes 73760 | tf_op jit(solution)/shard_map/ppermute | solution.py:465
  25.5 0.2 collective-permute-done.4.s4
  25.7 0.0 copy-done.8
  25.7 0.0 copy-done.13
  25.7 0.0 copy-done.10
  25.7 0.0 copy-done.12
  25.7 0.5 copy-done.14
  26.2 0.1 copy-done.15
  26.3 23.0 %shard_map.162 = (bf16[48,48,128]{2,1,0:T(8,128)(2,1)}, bf16[48,48,128]{2,1,0:T(8,128)(2,1)}, bf16[6,48,128]{2,1,0:T(8,128)(2,1)}, bf16[6,48,128]{2,1,0:T(8,128)...) custom-call(s32[1,8]{1,0:T(1,128)} %beside.5, s32[1]{0:T(128)} %bitcast.where, ...), custom_call_target="tpu_custom_call" | custom-call | flops 1811939328 | bytes 4632064 | tf_op jit(solution)/shard_map/pallas_call | solution.py:451
  49.4 0.0 copy-start.6
  49.4 0.0 copy-start.7
  49.4 0.0 copy-start.11
  49.4 0.0 copy-start.9
  49.4 11.9 %all-to-all-start = ((f32[32,40,128]{2,1,0:T(8,128)}), f32[32,40,128]{2,1,0:T(8,128)S(1)}, u32[]{:S(2)}, u32[]{:S(2)}) async-start(f32[32,40,128]{2,1,0:T(8,128)} %bitcast.14), calls=%async_computation | async-start | bytes 1310720 | tf_op jit(solution)/shard_map/all_to_all | solution.py:562
  61.3 0.0 copy-done.6
  61.3 1.3 %collective-permute-start.9 = (bf16[6,48,128]{2,1,0:T(8,128)(2,1)S(1)}, bf16[6,48,128]{2,1,0:T(8,128)(2,1)S(1)}, u32[]{:S(2)}, u32[]{:S(2)}) collective-permute-start(bf16[6,48,128]{2,1,0:T(8,128)(2,1)S(1)} %copy-done.6), channel_id=1, source_target_pairs={{2,0},{3,1},{4,2},{5,3},{6,4},{7,5},{8,6},{9,7},{10,8},{11,9},{12,... | collective-permute-start | bytes 221192 | tf_op jit(solution)/shard_map/ppermute | solution.py:465
  62.6 0.0 copy-done.7
  62.6 4.2 %collective-permute-start.6 = (bf16[6,48,128]{2,1,0:T(8,128)(2,1)S(1)}, bf16[6,48,128]{2,1,0:T(8,128)(2,1)S(1)}, u32[]{:S(2)}, u32[]{:S(2)}) collective-permute-start(bf16[6,48,128]{2,1,0:T(8,128)(2,1)S(1)} %copy-done.7), channel_id=1, source_target_pairs={{0,2},{1,3},{2,4},{3,5},{4,6},{5,7},{6,8},{7,9},{8,10},{9,11},{10,... | collective-permute-start | bytes 221192 | tf_op jit(solution)/shard_map/ppermute | solution.py:465
  66.9 0.0 copy-done.11
  66.9 1.3 %collective-permute-start.8 = (bf16[6,48,128]{2,1,0:T(8,128)(2,1)S(1)}, bf16[6,48,128]{2,1,0:T(8,128)(2,1)S(1)}, u32[]{:S(2)}, u32[]{:S(2)}) collective-permute-start(bf16[6,48,128]{2,1,0:T(8,128)(2,1)S(1)} %copy-done.11), channel_id=1, source_target_pairs={{1,0},{2,1},{3,2},{4,3},{5,4},{6,5},{7,6},{8,7},{9,8},{10,9},{11,1... | collective-permute-start | bytes 221192 | tf_op jit(solution)/shard_map/ppermute | solution.py:465
  68.2 0.0 copy-done.9
  68.2 4.0 %collective-permute-start.7 = (bf16[6,48,128]{2,1,0:T(8,128)(2,1)S(1)}, bf16[6,48,128]{2,1,0:T(8,128)(2,1)S(1)}, u32[]{:S(2)}, u32[]{:S(2)}) collective-permute-start(bf16[6,48,128]{2,1,0:T(8,128)(2,1)S(1)} %copy-done.9), channel_id=1, source_target_pairs={{0,1},{1,2},{2,3},{3,4},{4,5},{5,6},{6,7},{7,8},{8,9},{9,10},{10,1... | collective-permute-start | bytes 221192 | tf_op jit(solution)/shard_map/ppermute | solution.py:465
  72.2 1.2 all-to-all-done
  73.4 0.1 reduce_sum.18
  73.4 0.0 collective-permute-done.9.s4
  73.4 0.0 copy-start
  73.4 0.0 collective-permute-done.6.s1
  73.5 0.0 copy-start.1
  73.5 0.0 collective-permute-done.8.s3
  73.5 0.0 copy-start.2
  73.5 1.0 collective-permute-done.7.s2
  74.5 0.7 broadcast_in_dim.29
  75.2 0.0 copy-done
  75.2 0.0 copy-done.1
  75.2 0.0 copy-done.2
  75.2 0.0 copy-done.3
  75.2 18.9 %all-to-all-start.1 = ((bf16[16,40,128]{2,1,0:T(8,128)(2,1)}), bf16[16,40,128]{2,1,0:T(8,128)(2,1)S(1)}, u32[]{:S(2)}, u32[]{:S(2)}) async-start(bf16[16,40,128]{2,1,0:T(8,128)(2,1)} %broadcast_in_dim.29), calls=%async_computation.1 | async-start | bytes 327680 | tf_op jit(solution)/shard_map/all_to_all | solution.py:475
  94.1 1.3 %collective-permute-start.10 = (bf16[6,48,128]{2,1,0:T(8,128)(2,1)S(1)}, bf16[6,48,128]{2,1,0:T(8,128)(2,1)S(1)}, u32[]{:S(2)}, u32[]{:S(2)}) collective-permute-start(bf16[6,48,128]{2,1,0:T(8,128)(2,1)S(1)} %copy-done.7), channel_id=1, source_target_pairs={{0,3},{1,4},{2,5},{3,6},{4,7},{5,8},{6,9},{7,10},{8,11},{9,12},{10... | collective-permute-start | bytes 221192 | tf_op jit(solution)/shard_map/ppermute | solution.py:465
  95.4 1.3 %collective-permute-start.11 = (bf16[6,48,128]{2,1,0:T(8,128)(2,1)S(1)}, bf16[6,48,128]{2,1,0:T(8,128)(2,1)S(1)}, u32[]{:S(2)}, u32[]{:S(2)}) collective-permute-start(bf16[6,48,128]{2,1,0:T(8,128)(2,1)S(1)} %copy-done.6), channel_id=1, source_target_pairs={{3,0},{4,1},{5,2},{6,3},{7,4},{8,5},{9,6},{10,7},{11,8},{12,9},{13... | collective-permute-start | bytes 221192 | tf_op jit(solution)/shard_map/ppermute | solution.py:465
  96.7 9.6 %all-to-all-done.1 = bf16[16,40,128]{2,1,0:T(8,128)(2,1)S(1)} async-done(((bf16[16,40,128]{2,1,0:T(8,128)(2,1)}), bf16[16,40,128]{2,1,0:T(8,128)(2,1)S(1)}, u32[]{:S(2)}, u32[]{:S(2)}) %all-to-all-start.1) | async-done | bytes 163872 | tf_op jit(solution)/shard_map/all_to_all | solution.py:475
  106.3 0.0 collective-permute-done.10.s0
  106.3 0.0 copy-start.4
  106.3 0.0 collective-permute-done.11.s5
  106.4 0.0 copy-start.5
  106.4 0.8 broadcast_in_dim.30
  107.1 0.0 copy-done.4
  107.1 0.0 copy-done.5
  107.1 12.0 %all-to-all-start.2 = ((bf16[32,40,128]{2,1,0:T(8,128)(2,1)}), bf16[32,40,128]{2,1,0:T(8,128)(2,1)S(1)}, u32[]{:S(2)}, u32[]{:S(2)}) async-start(bf16[32,40,128]{2,1,0:T(8,128)(2,1)} %broadcast_in_dim.30), calls=%async_computation.2 | async-start | bytes 655360 | tf_op jit(solution)/shard_map/all_to_all | solution.py:475
  119.2 8.0 %shard_map.163 = bf16[48,48,128]{2,1,0:T(8,128)(2,1)} custom-call(s32[1,8]{1,0:T(1,128)} %beside.5, s32[1]{0:T(128)} %bitcast.where, bf16[48,48,128]{2,1,0:T(8,128)(2,1)} %get-tuple-element.53.conv_grad_hbm, bf16[6,48,128]{2,1,0:T(8,128)(2,1)} %copy-done.4, bf16[6,48,128]{2,1,0:T(8,128)(2,1)} %copy-done.1, bf16[6,48,128]{2,1,0:T(8,128)(2,1)} %copy-done.3, ...), custom_call_target="tpu_custom_call" | custom-call | flops 28901376 | bytes 2826752 | tf_op jit(solution)/shard_map/pallas_call | solution.py:451
  127.2 1.1 all-to-all-done.2
  128.3 0.8 shard_map.164
  (7 shorter events, 0.0 us)
Async XLA Ops:
  3.4 15.0 %collective-permute-start.2 = (bf16[6,48,128]{2,1,0:T(8,128)(2,1)}, bf16[6,48,128]{2,1,0:T(8,128)(2,1)S(1)}, u32[]{:S(2)}, u32[]{:S(2)}) collective-permute-start(bf16[6,48,128]{2,1,0:T(8,128)(2,1)} %get-tuple-element.40), channel_id=1, source_target_pairs={{0,1},{1,2},{2,3},{3,4},{4,5},{5,6},{6,7},{7,8},{8,9},{9,10},{10,1... | collective-permute-start | bytes 221192 | tf_op jit(solution)/shard_map/ppermute | solution.py:465
  7.3 13.7 %collective-permute-start.1 = (bf16[6,48,128]{2,1,0:T(8,128)(2,1)}, bf16[6,48,128]{2,1,0:T(8,128)(2,1)S(1)}, u32[]{:S(2)}, u32[]{:S(2)}) collective-permute-start(bf16[6,48,128]{2,1,0:T(8,128)(2,1)} %get-tuple-element.39), channel_id=1, source_target_pairs={{0,2},{1,3},{2,4},{3,5},{4,6},{5,7},{6,8},{7,9},{8,10},{9,11},{10,... | collective-permute-start | bytes 221192 | tf_op jit(solution)/shard_map/ppermute | solution.py:465
  10.8 10.2 %collective-permute-start = (bf16[6,48,128]{2,1,0:T(8,128)(2,1)}, bf16[6,48,128]{2,1,0:T(8,128)(2,1)S(1)}, u32[]{:S(2)}, u32[]{:S(2)}) collective-permute-start(bf16[6,48,128]{2,1,0:T(8,128)(2,1)} %get-tuple-element.39), channel_id=1, source_target_pairs={{0,3},{1,4},{2,5},{3,6},{4,7},{5,8},{6,9},{7,10},{8,11},{9,12},{10... | collective-permute-start | bytes 221192 | tf_op jit(solution)/shard_map/ppermute | solution.py:465
  15.7 5.3 %collective-permute-start.3 = (bf16[6,48,128]{2,1,0:T(8,128)(2,1)}, bf16[6,48,128]{2,1,0:T(8,128)(2,1)S(1)}, u32[]{:S(2)}, u32[]{:S(2)}) collective-permute-start(bf16[6,48,128]{2,1,0:T(8,128)(2,1)} %get-tuple-element.41), channel_id=1, source_target_pairs={{1,0},{2,1},{3,2},{4,3},{5,4},{6,5},{7,6},{8,7},{9,8},{10,9},{11,1... | collective-permute-start | bytes 221192 | tf_op jit(solution)/shard_map/ppermute | solution.py:465
  17.0 8.5 %collective-permute-start.5 = (bf16[6,48,128]{2,1,0:T(8,128)(2,1)}, bf16[6,48,128]{2,1,0:T(8,128)(2,1)S(1)}, u32[]{:S(2)}, u32[]{:S(2)}) collective-permute-start(bf16[6,48,128]{2,1,0:T(8,128)(2,1)} %get-tuple-element.42), channel_id=1, source_target_pairs={{3,0},{4,1},{5,2},{6,3},{7,4},{8,5},{9,6},{10,7},{11,8},{12,9},{13... | collective-permute-start | bytes 221192 | tf_op jit(solution)/shard_map/ppermute | solution.py:465
  18.3 7.4 %copy-start.8 = (bf16[6,48,128]{2,1,0:T(8,128)(2,1)}, bf16[6,48,128]{2,1,0:T(8,128)(2,1)S(1)}, u32[]{:S(2)}) copy-start(bf16[6,48,128]{2,1,0:T(8,128)(2,1)S(1)} %collective-permute-done.2.s2) | copy-start | bytes 221188
  18.3 7.3 %collective-permute-start.4 = (bf16[6,48,128]{2,1,0:T(8,128)(2,1)}, bf16[6,48,128]{2,1,0:T(8,128)(2,1)S(1)}, u32[]{:S(2)}, u32[]{:S(2)}) collective-permute-start(bf16[6,48,128]{2,1,0:T(8,128)(2,1)} %get-tuple-element.42), channel_id=1, source_target_pairs={{2,0},{3,1},{4,2},{5,3},{6,4},{7,5},{8,6},{9,7},{10,8},{11,9},{12,... | collective-permute-start | bytes 221192 | tf_op jit(solution)/shard_map/ppermute | solution.py:465
  21.0 4.7 %copy-start.13 = (bf16[6,48,128]{2,1,0:T(8,128)(2,1)}, bf16[6,48,128]{2,1,0:T(8,128)(2,1)S(1)}, u32[]{:S(2)}) copy-start(bf16[6,48,128]{2,1,0:T(8,128)(2,1)S(1)} %collective-permute-done.3.s3) | copy-start | bytes 221188
  21.0 4.7 %copy-start.10 = (bf16[6,48,128]{2,1,0:T(8,128)(2,1)}, bf16[6,48,128]{2,1,0:T(8,128)(2,1)S(1)}, u32[]{:S(2)}) copy-start(bf16[6,48,128]{2,1,0:T(8,128)(2,1)S(1)} %collective-permute-done.1.s1) | copy-start | bytes 221188
  21.0 4.7 %copy-start.12 = (bf16[6,48,128]{2,1,0:T(8,128)(2,1)}, bf16[6,48,128]{2,1,0:T(8,128)(2,1)S(1)}, u32[]{:S(2)}) copy-start(bf16[6,48,128]{2,1,0:T(8,128)(2,1)S(1)} %collective-permute-done.s0) | copy-start | bytes 221188
  25.5 0.6 copy-start.14
  25.7 0.6 copy-start.15
  49.4 11.9 %copy-start.6 = (bf16[6,48,128]{2,1,0:T(8,128)(2,1)S(1)}, bf16[6,48,128]{2,1,0:T(8,128)(2,1)}, u32[]{:S(2)}) copy-start(bf16[6,48,128]{2,1,0:T(8,128)(2,1)} %get-tuple-element.51) | copy-start | bytes 221188
  49.4 13.2 %copy-start.7 = (bf16[6,48,128]{2,1,0:T(8,128)(2,1)S(1)}, bf16[6,48,128]{2,1,0:T(8,128)(2,1)}, u32[]{:S(2)}) copy-start(bf16[6,48,128]{2,1,0:T(8,128)(2,1)} %get-tuple-element.50) | copy-start | bytes 221188
  49.4 17.5 %copy-start.11 = (bf16[6,48,128]{2,1,0:T(8,128)(2,1)S(1)}, bf16[6,48,128]{2,1,0:T(8,128)(2,1)}, u32[]{:S(2)}) copy-start(bf16[6,48,128]{2,1,0:T(8,128)(2,1)} %get-tuple-element.47) | copy-start | bytes 221188
  49.4 18.8 %copy-start.9 = (bf16[6,48,128]{2,1,0:T(8,128)(2,1)S(1)}, bf16[6,48,128]{2,1,0:T(8,128)(2,1)}, u32[]{:S(2)}) copy-start(bf16[6,48,128]{2,1,0:T(8,128)(2,1)} %get-tuple-element.48) | copy-start | bytes 221188
  49.4 24.0 %all-to-all-start = ((f32[32,40,128]{2,1,0:T(8,128)}), f32[32,40,128]{2,1,0:T(8,128)S(1)}, u32[]{:S(2)}, u32[]{:S(2)}) async-start(f32[32,40,128]{2,1,0:T(8,128)} %bitcast.14), calls=%async_computation | async-start | bytes 1310720 | tf_op jit(solution)/shard_map/all_to_all | solution.py:562
  61.3 12.1 %collective-permute-start.9 = (bf16[6,48,128]{2,1,0:T(8,128)(2,1)S(1)}, bf16[6,48,128]{2,1,0:T(8,128)(2,1)S(1)}, u32[]{:S(2)}, u32[]{:S(2)}) collective-permute-start(bf16[6,48,128]{2,1,0:T(8,128)(2,1)S(1)} %copy-done.6), channel_id=1, source_target_pairs={{2,0},{3,1},{4,2},{5,3},{6,4},{7,5},{8,6},{9,7},{10,8},{11,9},{12,... | collective-permute-start | bytes 221192 | tf_op jit(solution)/shard_map/ppermute | solution.py:465
  62.6 10.8 %collective-permute-start.6 = (bf16[6,48,128]{2,1,0:T(8,128)(2,1)S(1)}, bf16[6,48,128]{2,1,0:T(8,128)(2,1)S(1)}, u32[]{:S(2)}, u32[]{:S(2)}) collective-permute-start(bf16[6,48,128]{2,1,0:T(8,128)(2,1)S(1)} %copy-done.7), channel_id=1, source_target_pairs={{0,2},{1,3},{2,4},{3,5},{4,6},{5,7},{6,8},{7,9},{8,10},{9,11},{10,... | collective-permute-start | bytes 221192 | tf_op jit(solution)/shard_map/ppermute | solution.py:465
  66.9 6.6 %collective-permute-start.8 = (bf16[6,48,128]{2,1,0:T(8,128)(2,1)S(1)}, bf16[6,48,128]{2,1,0:T(8,128)(2,1)S(1)}, u32[]{:S(2)}, u32[]{:S(2)}) collective-permute-start(bf16[6,48,128]{2,1,0:T(8,128)(2,1)S(1)} %copy-done.11), channel_id=1, source_target_pairs={{1,0},{2,1},{3,2},{4,3},{5,4},{6,5},{7,6},{8,7},{9,8},{10,9},{11,1... | collective-permute-start | bytes 221192 | tf_op jit(solution)/shard_map/ppermute | solution.py:465
  68.2 6.3 %collective-permute-start.7 = (bf16[6,48,128]{2,1,0:T(8,128)(2,1)S(1)}, bf16[6,48,128]{2,1,0:T(8,128)(2,1)S(1)}, u32[]{:S(2)}, u32[]{:S(2)}) collective-permute-start(bf16[6,48,128]{2,1,0:T(8,128)(2,1)S(1)} %copy-done.9), channel_id=1, source_target_pairs={{0,1},{1,2},{2,3},{3,4},{4,5},{5,6},{6,7},{7,8},{8,9},{9,10},{10,1... | collective-permute-start | bytes 221192 | tf_op jit(solution)/shard_map/ppermute | solution.py:465
  73.4 1.8 %copy-start = (bf16[6,48,128]{2,1,0:T(8,128)(2,1)}, bf16[6,48,128]{2,1,0:T(8,128)(2,1)S(1)}, u32[]{:S(2)}) copy-start(bf16[6,48,128]{2,1,0:T(8,128)(2,1)S(1)} %collective-permute-done.9.s4) | copy-start | bytes 221188
  73.5 1.7 %copy-start.1 = (bf16[6,48,128]{2,1,0:T(8,128)(2,1)}, bf16[6,48,128]{2,1,0:T(8,128)(2,1)S(1)}, u32[]{:S(2)}) copy-start(bf16[6,48,128]{2,1,0:T(8,128)(2,1)S(1)} %collective-permute-done.6.s1) | copy-start | bytes 221188
  73.5 1.7 %copy-start.2 = (bf16[6,48,128]{2,1,0:T(8,128)(2,1)}, bf16[6,48,128]{2,1,0:T(8,128)(2,1)S(1)}, u32[]{:S(2)}) copy-start(bf16[6,48,128]{2,1,0:T(8,128)(2,1)S(1)} %collective-permute-done.8.s3) | copy-start | bytes 221188
  74.5 0.7 copy-start.3
  75.2 31.1 %all-to-all-start.1 = ((bf16[16,40,128]{2,1,0:T(8,128)(2,1)}), bf16[16,40,128]{2,1,0:T(8,128)(2,1)S(1)}, u32[]{:S(2)}, u32[]{:S(2)}) async-start(bf16[16,40,128]{2,1,0:T(8,128)(2,1)} %broadcast_in_dim.29), calls=%async_computation.1 | async-start | bytes 327680 | tf_op jit(solution)/shard_map/all_to_all | solution.py:475
  94.1 12.2 %collective-permute-start.10 = (bf16[6,48,128]{2,1,0:T(8,128)(2,1)S(1)}, bf16[6,48,128]{2,1,0:T(8,128)(2,1)S(1)}, u32[]{:S(2)}, u32[]{:S(2)}) collective-permute-start(bf16[6,48,128]{2,1,0:T(8,128)(2,1)S(1)} %copy-done.7), channel_id=1, source_target_pairs={{0,3},{1,4},{2,5},{3,6},{4,7},{5,8},{6,9},{7,10},{8,11},{9,12},{10... | collective-permute-start | bytes 221192 | tf_op jit(solution)/shard_map/ppermute | solution.py:465
  95.4 10.9 %collective-permute-start.11 = (bf16[6,48,128]{2,1,0:T(8,128)(2,1)S(1)}, bf16[6,48,128]{2,1,0:T(8,128)(2,1)S(1)}, u32[]{:S(2)}, u32[]{:S(2)}) collective-permute-start(bf16[6,48,128]{2,1,0:T(8,128)(2,1)S(1)} %copy-done.6), channel_id=1, source_target_pairs={{3,0},{4,1},{5,2},{6,3},{7,4},{8,5},{9,6},{10,7},{11,8},{12,9},{13... | collective-permute-start | bytes 221192 | tf_op jit(solution)/shard_map/ppermute | solution.py:465
  106.3 0.8 copy-start.4
  106.4 0.8 copy-start.5
  107.1 21.1 %all-to-all-start.2 = ((bf16[32,40,128]{2,1,0:T(8,128)(2,1)}), bf16[32,40,128]{2,1,0:T(8,128)(2,1)S(1)}, u32[]{:S(2)}, u32[]{:S(2)}) async-start(bf16[32,40,128]{2,1,0:T(8,128)(2,1)} %broadcast_in_dim.30), calls=%async_computation.2 | async-start | bytes 655360 | tf_op jit(solution)/shard_map/all_to_all | solution.py:475
